TPU v7x, 128 devices: a whole 4x4x4 slice. The times are simulated.
128 devices in a mesh: dp: 16 (over y_hi, z, core), ctx: 8 (over y_lo, x).
Axes of the slice: x: 4, y: 4 (y_hi: 2, y_lo: 2; y = y_hi * 2 + y_lo), z: 4, core: 2. Of those that a mesh axis runs over, the one named last changes fastest.
Arguments:
- token_ids: int32 [16, 1024], P('dp', 'ctx'), may hold values from 0 to 511
- embedding: bfloat16 [512, 4096], replicated, may hold values from -6 to 6
- short_filter: float32 [3, 3, 4096], replicated, may hold values from -3 to 3
- long_filter: bfloat16 [1024, 4096], P('dp', 'ctx'), may hold values from -1.3 to 1.3
- cotangent: bfloat16 [16, 1024, 4096], P('dp', 'ctx'), may hold values from -1.5 to 1.5
Outputs:
- mixed: bfloat16 [16, 1024, 4096], P('dp', 'ctx')
- grad_embedding: float32 [512, 4096], P('dp', 'ctx')
- grad_filter: float32 [1024, 4096], P('dp', 'ctx')
All inputs are finite; a program needn't handle non-finite values.
Results may differ from a plain program's by a relative error of at most 0.02.
Values may be sent and summed in bfloat16 or wider, within the bound.
A program may use at most 128 MiB of HBM per device.

v0:
```python
import math

import jax
import jax.numpy as jnp
from jax import lax
from jax.sharding import PartitionSpec as P


def from_behind(block, axis, distance):
    devices = range(lax.axis_size(axis))
    route = [(i - distance, i) for i in devices if i - distance in devices]
    return lax.ppermute(block, axis, route)


def split_length(total):
    first = math.isqrt(total)
    while total % first:
        first = first - 1
    return (first, total // first)


def square_table(count):
    index = jnp.arange(count, dtype=jnp.int32)
    angle = (index[:, None] * index[None, :] % count).astype(jnp.float32) * (2.0 * math.pi / count)
    return (jnp.cos(angle).astype(jnp.bfloat16), jnp.sin(angle).astype(jnp.bfloat16))


def make_tables(total):
    first, second = split_length(total)
    cos_p, sin_p = square_table(first)
    cos_q, sin_q = square_table(second)
    rows_idx = jnp.arange(first, dtype=jnp.int32)
    cols_idx = jnp.arange(second, dtype=jnp.int32)
    angle = (rows_idx[:, None] * cols_idx[None, :] % total).astype(jnp.float32) * (
        2.0 * math.pi / total
    )
    return (cos_p, sin_p, cos_q, sin_q, jnp.cos(angle)[:, :, None], jnp.sin(angle)[:, :, None])


def mix(table, field, form):
    return jnp.einsum(form, table, field, preferred_element_type=jnp.float32)


def forward_dft(signal, tables):
    cos_p, sin_p, cos_q, sin_q, tw_cos, tw_sin = tables
    first = cos_p.shape[0]
    second = cos_q.shape[0]
    width = signal.shape[1]
    flat = signal.reshape(first, second * width)
    a_re = jnp.dot(cos_p, flat, preferred_element_type=jnp.float32).reshape(first, second, width)
    a_im = -jnp.dot(sin_p, flat, preferred_element_type=jnp.float32).reshape(first, second, width)
    b_re = (a_re * tw_cos + a_im * tw_sin).astype(jnp.bfloat16)
    b_im = (a_im * tw_cos - a_re * tw_sin).astype(jnp.bfloat16)
    form = "kn,anc->akc"
    x_re = mix(cos_q, b_re, form) + mix(sin_q, b_im, form)
    x_im = mix(cos_q, b_im, form) - mix(sin_q, b_re, form)
    return (x_re, x_im)


def inverse_dft(x_re, x_im, tables):
    cos_p, sin_p, cos_q, sin_q, tw_cos, tw_sin = tables
    first, second, width = x_re.shape
    form = "nk,akc->anc"
    b_re = mix(cos_q, x_re, form) - mix(sin_q, x_im, form)
    b_im = mix(cos_q, x_im, form) + mix(sin_q, x_re, form)
    c_re = (b_re * tw_cos - b_im * tw_sin).astype(jnp.bfloat16).reshape(first, second * width)
    c_im = (b_im * tw_cos + b_re * tw_sin).astype(jnp.bfloat16).reshape(first, second * width)
    result = jnp.dot(cos_p, c_re, preferred_element_type=jnp.float32) - jnp.dot(
        sin_p, c_im, preferred_element_type=jnp.float32
    )
    return result.reshape(first * second, width) / (first * second)


def padded_dft(field, tables):
    grown = jnp.concatenate([field, jnp.zeros_like(field)], 0)
    return forward_dft(grown, tables)


def times_conj(a_re, a_im, b_re, b_im):
    return (
        (a_re * b_re + a_im * b_im).astype(jnp.bfloat16),
        (a_im * b_re - a_re * b_im).astype(jnp.bfloat16),
    )


def body(token_ids, embedding, short_filter, long_filter, cotangent):
    seq = token_ids.shape[1]
    vocab = embedding.shape[0]
    width = embedding.shape[1]
    ids_row = token_ids[0]
    vocab_index = jnp.arange(vocab, dtype=jnp.int32)
    onehot = (ids_row[:, None] == vocab_index[None, :]).astype(jnp.bfloat16)
    x_rows = jnp.dot(onehot, embedding, preferred_element_type=jnp.float32).astype(jnp.bfloat16)
    before = from_behind(x_rows[seq - 2 :], "ctx", 1)
    extended = jnp.concatenate([before, x_rows], 0).astype(jnp.float32)
    branches = [
        short_filter[r, 0] * extended[2:]
        + short_filter[r, 1] * extended[1:-1]
        + short_filter[r, 2] * extended[:-2]
        for r in range(3)
    ]
    u_q, u_k, u_v = branches
    z_rows = (u_k * u_v).astype(jnp.bfloat16)
    full_filter = lax.all_gather(long_filter, "dp", axis=0, tiled=True)
    length = full_filter.shape[0]
    tables = make_tables(2 * length)
    z_chan = lax.all_to_all(z_rows, "ctx", split_axis=1, concat_axis=0, tiled=True)
    h_re, h_im = padded_dft(full_filter, tables)
    z_re, z_im = padded_dft(z_chan, tables)
    prod_re = (z_re * h_re - z_im * h_im).astype(jnp.bfloat16)
    prod_im = (z_re * h_im + z_im * h_re).astype(jnp.bfloat16)
    conv_chan = inverse_dft(prod_re, prod_im, tables)[:length].astype(jnp.bfloat16)
    conv = lax.all_to_all(conv_chan, "ctx", split_axis=0, concat_axis=1, tiled=True).astype(
        jnp.float32
    )
    mixed = (u_q * conv).astype(jnp.bfloat16)
    grad_out = cotangent[0].astype(jnp.float32)
    g_conv = (grad_out * u_q).astype(jnp.bfloat16)
    g_q = grad_out * conv
    g_chan = lax.all_to_all(g_conv, "ctx", split_axis=1, concat_axis=0, tiled=True)
    g_re, g_im = padded_dft(g_chan, tables)
    zq_re, zq_im = times_conj(g_re, g_im, h_re, h_im)
    g_z_chan = inverse_dft(zq_re, zq_im, tables)[:length].astype(jnp.bfloat16)
    f_re, f_im = times_conj(g_re, g_im, z_re, z_im)
    filter_term = inverse_dft(f_re, f_im, tables)[:length]
    grad_filter = lax.psum_scatter(filter_term, "dp", scatter_dimension=0, tiled=True)
    g_z = lax.all_to_all(g_z_chan, "ctx", split_axis=0, concat_axis=1, tiled=True).astype(
        jnp.float32
    )
    g_k = g_z * u_v
    g_v = g_z * u_k
    tail_zeros = jnp.zeros((2, width), jnp.float32)
    g_x = jnp.zeros((seq, width), jnp.float32)
    lead_first = jnp.zeros((width,), jnp.float32)
    lead_second = jnp.zeros((width,), jnp.float32)
    for r, g_r in enumerate((g_q, g_k, g_v)):
        grown = jnp.concatenate([g_r, tail_zeros], 0)
        g_x = (
            g_x
            + short_filter[r, 0] * grown[:-2]
            + short_filter[r, 1] * grown[1:-1]
            + short_filter[r, 2] * grown[2:]
        )
        lead_first = lead_first + short_filter[r, 2] * g_r[0]
        lead_second = lead_second + short_filter[r, 1] * g_r[0] + short_filter[r, 2] * g_r[1]
    incoming = from_behind(
        jnp.stack([lead_first, lead_second]).astype(jnp.bfloat16), "ctx", -1
    ).astype(jnp.float32)
    g_x = g_x + jnp.concatenate([jnp.zeros((seq - 2, width), jnp.float32), incoming], 0)
    g_x = g_x.astype(jnp.bfloat16)
    table_term = jnp.einsum("sv,sd->vd", onehot, g_x, preferred_element_type=jnp.float32)
    row_share = lax.psum_scatter(
        table_term.astype(jnp.bfloat16), "dp", scatter_dimension=0, tiled=True
    )
    grad_embedding = lax.psum_scatter(row_share, "ctx", scatter_dimension=1, tiled=True).astype(
        jnp.float32
    )
    return (mixed[None], grad_embedding, grad_filter)


def solution(mesh):
    in_specs = (P("dp", "ctx"), P(), P(), P("dp", "ctx"), P("dp", "ctx", None))
    out_specs = (P("dp", "ctx", None), P("dp", "ctx"), P("dp", "ctx"))
    return jax.shard_map(body, mesh=mesh, in_specs=in_specs, out_specs=out_specs, check_vma=False)
```

profile of v0, /device:TPU:1, one launch (start us, length us, event | category | flops | bytes accessed | tf_op | source)
XLA Modules:
  0.0 438.4 jit_solution(6981092115847375486)
XLA Ops:
  7.9 3.0 convolution_convert_fusion.1
  10.9 4.1 collective-permute-start
  16.2 2.1 fusion.16
  19.4 5.5 %all-to-all-start.2 = ((bf16[128,8,512]{2,0,1:T(8,128)(2,1)}), bf16[128,8,512]{2,0,1:T(8,128)(2,1)S(1)}, u32[]{:S(2)}, u32[]{:S(2)}) async-start(bf16[128,8,512]{2,0,1:T(8,128)(2,1)} %bitcast.230), calls=%async_computation.2 | async-start | bytes 2097152 | tf_op jit(solution)/shard_map/all_to_all | solution.py:120
  26.5 14.2 %all-to-all-done.2 = bf16[128,8,512]{2,0,1:T(8,128)(2,1)S(1)} async-done(((bf16[128,8,512]{2,0,1:T(8,128)(2,1)}), bf16[128,8,512]{2,0,1:T(8,128)(2,1)S(1)}, u32[]{:S(2)}, u32[]{:S(2)}) %all-to-all-start.2) | async-done | bytes 1048608 | tf_op jit(solution)/shard_map/all_to_all | solution.py:120
  40.7 1.5 concatenate.30
  42.2 4.2 reshape.138
  46.4 4.5 %fusion.23 = f32[32,64,512]{2,0,1:T(8,128)} fusion(bf16[4,64,8,512]{3,2,1,0:T(8,128)(2,1)} %bitcast.209), kind=kOutput, calls=%fused_computation.63 | convolution fusion | flops 67124224 | bytes 6291456 | tf_op jit(solution)/shard_map/dot_general | solution.py:51
  50.9 2.8 fusion.25
  53.7 5.4 %all-gather.2.cloned.1.call-done = bf16[1024,512]{1,0:T(8,128)(2,1)} async-done(((bf16[64,512]{1,0:T(8,128)(2,1)}), bf16[1024,512]{1,0:T(8,128)(2,1)}) %all-gather.2.cloned.1.call-update) | async-done | bytes 1048592 | tf_op jit(solution)/shard_map/all_gather | solution.py:104
  59.1 2.7 concatenate.28
  61.8 4.2 reshape.135
  66.0 2.5 fusion.27
  69.5 4.9 %add_convert_fusion.7 = (bf16[32,64,512]{2,0,1:T(8,128)(2,1)S(1)}, bf16[32,64,512]{2,0,1:T(8,128)(2,1)S(1)}, bf16[32,64,512]{2,0,1:T(8,128)(2,1)S(1)}, bf16[32,64,512]{2,0,1:T(8,128)(2,1)S(1)}) fusion(f32[32,64,512]{2,0,1:T(8,128)S(1)} %fusion.27, f32[32,64]{0,1:T(8,128)S(1)} %copy.76, f32[32,64]{0,1:T(8,128)S(1)} %copy.74, f32[32,64,512]{2,0,1:T(8,128)} %fusion.25, ...), kind=kOutput, calls=%fused_computation.17 | convolution fusion | flops 85998592 | bytes 23085056 | tf_op jit(solution)/shard_map/dot_general | solution.py:50
  74.4 2.9 fusion.55
  77.3 2.9 fusion.53
  80.1 3.0 convolution_add_fusion.4
  83.1 2.9 convolution_subtract_fusion.4
  86.0 3.1 fusion.47
  89.1 2.9 fusion.49
  92.0 3.0 convolution_subtract_fusion.2
  94.9 2.9 convolution_add_fusion.2
  97.9 3.0 fusion.20
  103.4 1.7 subtract_convert_fusion.2
  110.4 19.8 %all_to_all.64 = bf16[8,128,512]{2,1,0:T(8,128)(2,1)S(1)} all-to-all(bf16[8,128,512]{2,1,0:T(8,128)(2,1)} %all_to_all.58), channel_id=1, replica_groups=mesh['dp'=16,'ctx'=8] {'ctx'}, dimensions={0} | all-to-all | bytes 2097152 | tf_op jit(solution)/shard_map/all_to_all | solution.py:127
  131.4 3.2 fusion.288
  134.9 17.5 %all_to_all.65 = bf16[128,8,512]{2,0,1:T(8,128)(2,1)S(1)} all-to-all(bf16[128,8,512]{2,0,1:T(8,128)(2,1)S(1)} %bitcast.232), channel_id=1, replica_groups=mesh['dp'=16,'ctx'=8] {'ctx'}, dimensions={1} | all-to-all | bytes 2097152 | tf_op jit(solution)/shard_map/all_to_all | solution.py:107
  152.3 1.5 concatenate.27
  153.8 2.9 reshape.134
  157.5 1.6 add_convert_fusion.8
  159.1 4.9 %fusion.61 = f32[32,512,64]{1,2,0:T(8,128)} fusion(bf16[32,64,512]{2,0,1:T(8,128)(2,1)S(1)} %get-tuple-element.15), kind=kOutput, calls=%fused_computation.111 | convolution fusion | flops 134279168 | bytes 6291456 | tf_op jit(solution)/shard_map/kn,anc->akc/dot_general | solution.py:41
  164.0 2.9 fusion.59
  166.9 5.1 %convolution_subtract_fusion.5 = f32[32,512,64]{1,2,0:T(8,128)} fusion(f32[32,512,64]{1,2,0:T(8,128)S(1)} %fusion.59, bf16[32,64,512]{2,0,1:T(8,128)(2,1)S(1)} %get-tuple-element.15), kind=kOutput, calls=%fused_computation.37 | convolution fusion | flops 135327744 | bytes 10485760 | tf_op jit(solution)/shard_map/kn,anc->akc/dot_general | solution.py:41
  172.0 12.5 %fusion.22 = (bf16[32,64,512]{2,1,0:T(8,128)(2,1)}, bf16[32,64,512]{2,1,0:T(8,128)(2,1)}, bf16[32,64,512]{2,1,0:T(8,128)(2,1)S(1)}, bf16[32,64,512]{2,1,0:T(8,128)(2,1)}) fusion(f32[32,512,64]{1,2,0:T(8,128)} %copy-done.6, f32[32,512,64]{1,2,0:T(8,128)} %convolution_subtract_fusion.5, f32[32,512,64]{1,2,0:T(8,128)S(1)} %copy-done.5, ...), kind=kOutput, calls=%fused_computation.62 | convolution fusion | flops 152104960 | bytes 35651584 | tf_op jit(solution)/shard_map/kn,anc->akc/dot_general | solution.py:41
  184.4 2.5 fusion.118
  192.6 2.8 convolution_add_fusion.3
  195.4 6.3 %subtract_convert_fusion = (bf16[32,512,64]{1,2,0:T(8,128)(2,1)}, bf16[32,512,64]{1,2,0:T(8,128)(2,1)}, bf16[32,512,64]{1,2,0:T(8,128)(2,1)S(1)}, bf16[32,512,64]{1,2,0:T(8,128)(2,1)S(1)}) fusion(f32[32,512,64]{1,2,0:T(8,128)S(1)} %convolution_subtract_fusion, f32[32,64]{1,0:T(8,128)S(1)} %get-tuple-element.48, f32[32,64]{1,0:T(8,128)S(1)} %copy-done.23, ...), kind=kOutput, calls=%fused_computation.3 | convolution fusion | flops 152104960 | bytes 27279360 | tf_op jit(solution)/shard_map/nk,akc->anc/dot_general | solution.py:41
  206.3 16.5 %all_to_all.66 = bf16[8,128,512]{2,1,0:T(8,128)(2,1)S(1)} all-to-all(bf16[8,128,512]{2,1,0:T(8,128)(2,1)S(1)} %all_to_all.52), channel_id=1, replica_groups=mesh['dp'=16,'ctx'=8] {'ctx'}, dimensions={0} | all-to-all | bytes 2097152 | tf_op jit(solution)/shard_map/all_to_all | solution.py:113
  229.0 3.2 collective-permute-done.1
  232.2 4.7 %convolution_convert_fusion = bf16[512,4096]{1,0:T(8,128)(2,1)} fusion(f32[128,4096]{1,0:T(8,128)S(1)} %get-tuple-element.33, f32[128,4096]{1,0:T(8,128)S(1)} %copy-done.19, f32[128,4096]{1,0:T(8,128)S(1)} %copy-done.20, bf16[2,4096]{1,0:T(2,128)(2,1)S(1)} %collective-permute-done.1, f32[4096]{0:T(1024)S(1)} %bitcast.248, f32[4096]{0:T(1024)S(1)} %bitcast.250, ...), kind=kOutput, calls=%fused_computation | convolution fusion | flops 549519360 | bytes 10650112 | tf_op jit(solution)/shard_map/sv,sd->vd/dot_general | solution.py:151
  237.0 1.5 copy-done.16
  241.3 2.8 fusion.140
  244.1 2.9 fusion.137
  247.0 72.3 %reduce-scatter.4.cloned.1.call-done = bf16[32,4096]{1,0:T(8,128)(2,1)} async-done(((bf16[512,4096]{1,0:T(8,128)(2,1)}), bf16[32,4096]{1,0:T(8,128)(2,1)}) %reduce-scatter.4.cloned.1.call-update) | async-done | bytes 262160 | tf_op jit(solution)/shard_map/reduce_scatter | solution.py:152
  319.4 2.4 fusion.35
  321.8 1.6 slice.146
  323.4 30.5 %reduce-scatter.6.cloned.1.call-done = bf16[32,512]{1,0:T(8,128)(2,1)} async-done(((bf16[32,4096]{1,0:T(8,128)(2,1)}), bf16[32,512]{1,0:T(8,128)(2,1)}) %reduce-scatter.6.cloned.1.call-update) | async-done | bytes 32784 | tf_op jit(solution)/shard_map/reduce_scatter | solution.py:155
  355.3 76.2 %reduce-scatter.8.cloned.1.call-done = f32[64,512]{1,0:T(8,128)} async-done(((f32[1024,512]{1,0:T(8,128)}), f32[64,512]{1,0:T(8,128)}) %reduce-scatter.8.cloned.1.call-update) | async-done | bytes 131088 | tf_op jit(solution)/shard_map/reduce_scatter | solution.py:126
  (123 shorter events, 36.0 us)
Async XLA Ops:
  7.2 51.9 %all-gather.2.cloned.1.call-start = ((), (), s32[]{:S(2)}) async-start(), calls=%async_computation.7 | async-start | bytes 1114112 | tf_op jit(solution)/shard_map/all_gather | solution.py:104
  7.9 7.1 %copy-start.21 = (f32[3,3,4096]{2,1,0:T(4,128)S(1)}, f32[3,3,4096]{2,1,0:T(4,128)}, u32[]{:S(2)}) copy-start(f32[3,3,4096]{2,1,0:T(4,128)} %param.7) | copy-start | bytes 442372
  10.9 5.3 %copy-start.17 = (bf16[1,128,4096]{2,1,0:T(8,128)(2,1)S(1)}, bf16[1,128,4096]{2,1,0:T(8,128)(2,1)}, u32[]{:S(2)}) copy-start(bf16[1,128,4096]{2,1,0:T(8,128)(2,1)} %param.9) | copy-start | bytes 3145732
  10.9 4.9 %collective-permute-start = (bf16[2,4096]{1,0:T(2,128)(2,1)S(1)}, bf16[2,4096]{1,0:T(2,128)(2,1)S(1)}, u32[]{:S(2)}, u32[]{:S(2)}) collective-permute-start(bf16[2,4096]{1,0:T(2,128)(2,1)S(1)} %slice.147), channel_id=1, source_target_pairs={{0,1},{1,2},{2,3},{3,4},{4,5},{5,6},{6,7},{8,9},{9,10},{10,11},{11... | collective-permute-start | bytes 49160 | tf_op jit(solution)/shard_map/ppermute | solution.py:12
  15.8 2.6 copy-start.24
  15.8 2.6 copy-start.26
  15.8 2.6 copy-start.28
  19.4 21.3 %all-to-all-start.2 = ((bf16[128,8,512]{2,0,1:T(8,128)(2,1)}), bf16[128,8,512]{2,0,1:T(8,128)(2,1)S(1)}, u32[]{:S(2)}, u32[]{:S(2)}) async-start(bf16[128,8,512]{2,0,1:T(8,128)(2,1)} %bitcast.230), calls=%async_computation.2 | async-start | bytes 2097152 | tf_op jit(solution)/shard_map/all_to_all | solution.py:120
  24.9 294.4 %reduce-scatter.4.cloned.1.call-start = ((), (), s32[]{:S(2)}) async-start(), calls=%async_computation.8 | async-start | bytes 4456448 | tf_op jit(solution)/shard_map/reduce_scatter | solution.py:152
  46.4 4.5 %copy-start.10 = (bf16[32,32768]{1,0:T(8,128)(2,1)S(1)}, bf16[32,32768]{1,0:T(8,128)(2,1)}, u32[]{:S(2)}) copy-start(bf16[32,32768]{1,0:T(8,128)(2,1)} %reshape.138) | copy-start | bytes 6291460
  66.0 2.5 copy-start.12
  66.0 3.5 copy-start.13
  83.1 14.8 %copy-start = (f32[32,512,64]{1,2,0:T(8,128)}, f32[32,512,64]{1,2,0:T(8,128)S(1)}, u32[]{:S(2)}) copy-start(f32[32,512,64]{1,2,0:T(8,128)S(1)} %convolution_add_fusion.4) | copy-start | bytes 12582916
  86.0 11.8 %copy-start.2 = (f32[32,512,64]{1,2,0:T(8,128)}, f32[32,512,64]{1,2,0:T(8,128)S(1)}, u32[]{:S(2)}) copy-start(f32[32,512,64]{1,2,0:T(8,128)S(1)} %convolution_subtract_fusion.4) | copy-start | bytes 12582916
  94.9 3.0 copy-start.4
  97.9 3.0 copy-start.6
  102.5 0.8 copy-start.22
  130.5 0.7 copy-start.30
  130.6 0.7 copy-start.31
  130.6 0.7 copy-start.32
  130.6 0.7 copy-start.33
  130.6 0.7 copy-start.34
  130.6 0.8 copy-start.35
  159.1 4.9 %copy-start.7 = (bf16[32,64,512]{2,0,1:T(8,128)(2,1)}, bf16[32,64,512]{2,0,1:T(8,128)(2,1)S(1)}, u32[]{:S(2)}) copy-start(bf16[32,64,512]{2,0,1:T(8,128)(2,1)S(1)} %get-tuple-element.16) | copy-start | bytes 6291460
  164.0 8.0 %copy-start.5 = (f32[32,512,64]{1,2,0:T(8,128)S(1)}, f32[32,512,64]{1,2,0:T(8,128)}, u32[]{:S(2)}) copy-start(f32[32,512,64]{1,2,0:T(8,128)} %copy-done.4) | copy-start | bytes 12582916
  166.9 5.1 %copy-start.1 = (f32[32,512,64]{1,2,0:T(8,128)S(1)}, f32[32,512,64]{1,2,0:T(8,128)}, u32[]{:S(2)}) copy-start(f32[32,512,64]{1,2,0:T(8,128)} %copy-done) | copy-start | bytes 12582916
  166.9 5.1 %copy-start.3 = (f32[32,512,64]{1,2,0:T(8,128)S(1)}, f32[32,512,64]{1,2,0:T(8,128)}, u32[]{:S(2)}) copy-start(f32[32,512,64]{1,2,0:T(8,128)} %copy-done.2) | copy-start | bytes 12582916
  184.4 2.5 copy-start.11
  187.0 1.6 copy-start.9
  189.4 1.6 copy-start.8
  192.6 2.8 copy-start.23
  223.1 1.6 copy-start.14
  223.1 1.9 copy-start.18
  224.9 2.0 copy-start.19
  224.9 2.6 copy-start.20
  224.9 7.3 %copy-start.25 = (f32[1,1,4096]{2,1,0:T(1,128)S(1)}, f32[1,1,4096]{2,1,0:T(1,128)}, u32[]{:S(2)}) copy-start(f32[1,1,4096]{2,1,0:T(1,128)} %copy-done.24) | copy-start | bytes 49156
  224.9 7.3 %copy-start.27 = (f32[1,1,4096]{2,1,0:T(1,128)S(1)}, f32[1,1,4096]{2,1,0:T(1,128)}, u32[]{:S(2)}) copy-start(f32[1,1,4096]{2,1,0:T(1,128)} %copy-done.26) | copy-start | bytes 49156
  224.9 7.3 %copy-start.29 = (f32[1,1,4096]{2,1,0:T(1,128)S(1)}, f32[1,1,4096]{2,1,0:T(1,128)}, u32[]{:S(2)}) copy-start(f32[1,1,4096]{2,1,0:T(1,128)} %copy-done.28) | copy-start | bytes 49156
  224.9 7.3 %copy-start.36 = (s32[1,128]{1,0:T(1,128)S(1)}, s32[1,128]{1,0:T(1,128)}, u32[]{:S(2)}) copy-start(s32[1,128]{1,0:T(1,128)} %param.5) | copy-start | bytes 1540
  227.7 4.5 %collective-permute-start.1 = (bf16[2,4096]{1,0:T(2,128)(2,1)S(1)}, bf16[2,4096]{1,0:T(2,128)(2,1)S(1)}, u32[]{:S(2)}, u32[]{:S(2)}) collective-permute-start(bf16[2,4096]{1,0:T(2,128)(2,1)S(1)} %pad_maximum_fusion), channel_id=1, source_target_pairs={{1,0},{2,1},{3,2},{4,3},{5,4},{6,5},{7,6},{9,8},{10,9},{11,10},{12... | collective-permute-start | bytes 49160 | tf_op jit(solution)/shard_map/ppermute | solution.py:12
  237.0 1.6 copy-start.16
  237.0 116.9 %reduce-scatter.6.cloned.1.call-start = ((), (), s32[]{:S(2)}) async-start(), calls=%async_computation.9 | async-start | bytes 294912 | tf_op jit(solution)/shard_map/reduce_scatter | solution.py:155
  238.6 1.6 copy-start.15
  319.3 112.1 %reduce-scatter.8.cloned.1.call-start = ((), (), s32[]{:S(2)}) async-start(), calls=%async_computation.10 | async-start | bytes 2228224 | tf_op jit(solution)/shard_map/reduce_scatter | solution.py:126
Sparse Core Ops, SparseCore 0:
  10.5 48.5 all-gather.1
  237.1 82.1 reduce-scatter.3
  321.8 32.0 reduce-scatter.5
  358.2 73.2 reduce-scatter.7
where the time goes:
time: 445 us; the launch traced here: 438 us
  waiting for transfers between devices  203 us (46%)
  matrix products  102 us (23%)
  blocking collectives  53.8 us (12%)
  local copies, waits for them, and re-layouts  38.5 us (9%)
  other arithmetic  15.8 us (4%)
  between operations  14.7 us (3%)
  starting transfers between devices  11.1 us (2%)
    reduce_scatter x1, waiting for transfers between devices, body(): lax.psum_scatter(filter_term, 'dp', scatter_dimension=0, tiled=True)  76.2 us
    reduce_scatter x1, waiting for transfers between devices, body(): lax.psum_scatter(table_term.astype(jnp.bfloat16), 'dp', scatter_dimension...  72.3 us
    dot_general x24, matrix products, mix(): return jnp.einsum(form, table, field, preferred_element_type=jnp.float32)  68.4 us
    reduce_scatter x1, waiting for transfers between devices, body(): lax.psum_scatter(row_share, 'ctx', scatter_dimension=1, tiled=True)  30.5 us
    all_to_all x1, blocking collectives, body(): lax.all_to_all(g_z_chan, 'ctx', split_axis=0, concat_axis=1, tiled=True)  19.8 us
    all_to_all x1, blocking collectives, body(): lax.all_to_all(z_rows, 'ctx', split_axis=1, concat_axis=0, tiled=True)  17.5 us
    all_to_all x1, blocking collectives, body(): lax.all_to_all(conv_chan, 'ctx', split_axis=0, concat_axis=1, tiled=True)  16.5 us
    unnamed x80, local copies, waits for them, and re-layouts  14.9 us
  transfers between devices with their start and end apart: 7, of which 7 were waited for; matrix products, arithmetic and copies ran while one was open for 8% of the time, Pallas kernels for 0%

commit v1 on v0

v1 whole, which is shorter than its diff:
```python
import math

import jax
import jax.numpy as jnp
import numpy as np
from jax import lax
from jax.sharding import PartitionSpec as P

BF = jnp.bfloat16
F32 = jnp.float32


def tables(length):
    sub = length // 4
    k = np.arange(sub)[None, :, None]
    t = 4 * np.arange(sub)[None, None, :] + np.arange(4)[:, None, None]
    angle = 2.0 * math.pi * (((4 * k + 1) * t) % (4 * length)) / (4 * length)
    fwd = np.concatenate([np.cos(angle), -np.sin(angle)], 1)
    inv = fwd.transpose(0, 2, 1) / length
    return jnp.asarray(fwd, BF), jnp.asarray(inv, BF)


def forward(field, table):
    half = table.shape[1] // 2
    p = jnp.einsum("jkn,jnc->jkc", table, field, preferred_element_type=F32)
    re, im = p[:, :half], p[:, half:]
    a_re, a_im, b_re, b_im = re[0] + re[2], im[0] + im[2], re[0] - re[2], im[0] - im[2]
    c_re, c_im, d_re, d_im = re[1] + re[3], im[1] + im[3], re[1] - re[3], im[1] - im[3]
    return (
        jnp.stack([a_re + c_re, b_re + d_im, a_re - c_re, b_re - d_im]),
        jnp.stack([a_im + c_im, b_im - d_re, a_im - c_im, b_im + d_re]),
    )


def inverse(re, im, table):
    a_re, a_im, b_re, b_im = re[0] + re[2], im[0] + im[2], re[0] - re[2], im[0] - im[2]
    c_re, c_im, d_re, d_im = re[1] + re[3], im[1] + im[3], re[1] - re[3], im[1] - im[3]
    w_re = jnp.stack([a_re + c_re, b_re - d_im, a_re - c_re, b_re + d_im])
    w_im = jnp.stack([a_im + c_im, b_im + d_re, a_im - c_im, b_im - d_re])
    w = jnp.concatenate([w_re, w_im], 1).astype(BF)
    return jnp.einsum("jnk,jkc->jnc", table, w, preferred_element_type=F32)


def split4(rows):
    return rows.reshape(rows.shape[0] // 4, 4, rows.shape[1]).transpose(1, 0, 2)


def join4(parts):
    return parts.transpose(1, 0, 2).reshape(parts.shape[0] * parts.shape[1], parts.shape[2])


def body(token_ids, embedding, short_filter, long_filter, cotangent):
    vocab, width = embedding.shape
    ctx, dp = lax.axis_size("ctx"), lax.axis_size("dp")
    part = width // ctx
    length = token_ids.shape[1] * ctx
    mine = lax.axis_index("ctx") * part
    fwd, inv = tables(length)
    ids = lax.all_gather(token_ids[0], "ctx", axis=0, tiled=True)
    ids = ids.reshape(length // 4, 4).T
    emb = lax.dynamic_slice(embedding, (0, mine), (vocab, part))
    taps = lax.dynamic_slice(short_filter, (0, 0, mine), (3, 3, part))
    onehot = (ids[:, :, None] == jnp.arange(vocab, dtype=jnp.int32)).astype(BF)
    x = jnp.einsum("jnv,vc->jnc", onehot, emb, preferred_element_type=F32)

    cot = lax.all_to_all(split4(cotangent[0]), "ctx", split_axis=2, concat_axis=1, tiled=True).astype(F32)
    full = split4(lax.all_gather(long_filter, "dp", axis=0, tiled=True))

    late = jnp.concatenate([jnp.zeros_like(x[:, :1]), x[:, :-1]], 1)
    once = jnp.stack([late[3], x[0], x[1], x[2]])
    twice = jnp.stack([late[2], late[3], x[0], x[1]])
    u_q, u_k, u_v = [taps[r, 0] * x + taps[r, 1] * once + taps[r, 2] * twice for r in range(3)]
    z = (u_k * u_v).astype(BF)
    z_re, z_im = forward(z, fwd)
    h_re, h_im = forward(full, fwd)
    conv = inverse(z_re * h_re - z_im * h_im, z_re * h_im + z_im * h_re, inv).astype(BF).astype(F32)
    mixed = (u_q * conv).astype(BF)
    mixed = join4(lax.all_to_all(mixed, "ctx", split_axis=1, concat_axis=2, tiled=True))

    g_conv = (cot * u_q).astype(BF)
    g_q = cot * conv
    g_re, g_im = forward(g_conv, fwd)
    g_z = inverse(g_re * h_re + g_im * h_im, g_im * h_re - g_re * h_im, inv).astype(BF).astype(F32)
    term = inverse(g_re * z_re + g_im * z_im, g_im * z_re - g_re * z_im, inv).astype(BF)
    term = term.reshape(4, dp, length // 4 // dp, part).transpose(1, 0, 2, 3)
    term = lax.all_to_all(term, "dp", split_axis=0, concat_axis=0, tiled=True)
    grad_filter = join4(jnp.sum(term.astype(F32), 0))

    g_x = jnp.zeros_like(x)
    for r, g_r in enumerate((g_q, g_z * u_v, g_z * u_k)):
        early = jnp.concatenate([g_r[:, 1:], jnp.zeros_like(g_r[:, :1])], 1)
        once = jnp.stack([g_r[1], g_r[2], g_r[3], early[0]])
        twice = jnp.stack([g_r[2], g_r[3], early[0], early[1]])
        g_x = g_x + taps[r, 0] * g_r + taps[r, 1] * once + taps[r, 2] * twice
    g_x = g_x.astype(BF)
    table = jnp.einsum("jnv,jnc->vc", onehot, g_x, preferred_element_type=F32).astype(BF)
    table = lax.all_to_all(table.reshape(dp, vocab // dp, part), "dp", split_axis=0, concat_axis=0, tiled=True)
    grad_embedding = jnp.sum(table.astype(F32), 0)
    return (mixed[None], grad_embedding, grad_filter)


def solution(mesh):
    in_specs = (P("dp", "ctx"), P(), P(), P("dp", "ctx"), P("dp", "ctx", None))
    out_specs = (P("dp", "ctx", None), P("dp", "ctx"), P("dp", "ctx"))
    return jax.shard_map(body, mesh=mesh, in_specs=in_specs, out_specs=out_specs, check_vma=False)
```

time: 445 us -> 183 us (0.41); the launches traced: 438 us -> 182 us
  waiting for transfers between devices: 203 us -> 26.8 us
  matrix products: 102 us -> 13.8 us
  blocking collectives: 53.8 us -> 21.5 us
  local copies, waits for them, and re-layouts: 38.5 us -> 54.2 us
  starting transfers between devices: 11.1 us -> 25.7 us
  other arithmetic: 15.8 us -> 24.7 us
    reduce_scatter x3 -> x0, waiting for transfers between devices: 179 us -> none  [the longest x1 76.2 us: body(): lax.psum_scatter(filter_term, 'dp', scatter_dimension=0, tiled=True)]
    dot_general x38 -> x8, matrix products: 102 us -> 13.8 us  [the longest x3 4.77 us: inverse(): return jnp.einsum('jnk,jkc->jnc', table, w, preferred_element_type=F32)]
    all_to_all x3 -> x0, blocking collectives: 53.8 us -> none  [the longest x1 19.8 us: body(): lax.all_to_all(g_z_chan, 'ctx', split_axis=0, concat_axis=1, tiled=True)]
    all_gather x0 -> x1, blocking collectives: none -> 21.5 us  [body(): ids = lax.all_gather(token_ids[0], 'ctx', axis=0, tiled=True)]
    all_to_all x1 -> x4, starting transfers between devices: 5.54 us -> 25.7 us  [the longest x1 11.8 us: body(): lax.all_to_all(table.reshape(dp, vocab // dp, part), 'dp', split_axis=0,...]
    all_to_all x1 -> x4, waiting for transfers between devices: 14.2 us -> 26.2 us  [the longest x1 12.5 us: body(): term = lax.all_to_all(term, 'dp', split_axis=0, concat_axis=0, tiled=True)]
    add x0 -> x9, other arithmetic: none -> 10.7 us  [the longest x1 3.28 us: body(): g_re * z_re + g_im * z_im]
    unnamed x80 -> x85, local copies, waits for them, and re-layouts: 14.9 us -> 22.9 us
  transfers between devices with their start and end apart: 7 -> 5, of which waited for: 7 -> 3; matrix products, arithmetic and copies ran while one was open for 8% -> 26% of each run, Pallas kernels for 0% -> 0%
where the time goes in v1:
time: 183 us; the launch traced here: 182 us
  local copies, waits for them, and re-layouts  54.2 us (30%)
  waiting for transfers between devices  26.8 us (15%)
  starting transfers between devices  25.7 us (14%)
  other arithmetic  24.7 us (13%)
  blocking collectives  21.5 us (12%)
  between operations  14.8 us (8%)
  matrix products  13.8 us (8%)
    unnamed x85, local copies, waits for them, and re-layouts  22.9 us
    all_gather x1, blocking collectives, body(): ids = lax.all_gather(token_ids[0], 'ctx', axis=0, tiled=True)  21.5 us
    all_to_all x1, waiting for transfers between devices, body(): term = lax.all_to_all(term, 'dp', split_axis=0, concat_axis=0, tiled=True)  12.5 us
    all_to_all x1, starting transfers between devices, body(): lax.all_to_all(table.reshape(dp, vocab // dp, part), 'dp', split_axis=0,...  11.8 us
    all_to_all x1, waiting for transfers between devices, body(): lax.all_to_all(mixed, 'ctx', split_axis=1, concat_axis=2, tiled=True)  10.2 us
    all_to_all x1, local copies, waits for them, and re-layouts, body(): lax.all_to_all(split4(cotangent[0]), 'ctx', split_axis=2, concat_axis=1,...  6.31 us
    all_to_all x1, starting transfers between devices, body(): lax.all_to_all(split4(cotangent[0]), 'ctx', split_axis=2, concat_axis=1,...  5.99 us
    another operation x8, other arithmetic  5.84 us
  transfers between devices with their start and end apart: 5, of which 3 were waited for; matrix products, arithmetic and copies ran while one was open for 26% of the time, Pallas kernels for 0%

profile of v1, /device:TPU:1, one launch (start us, length us, event | category | flops | bytes accessed | tf_op | source)
XLA Modules:
  0.0 181.6 jit_solution(2975689182260135745)
XLA Ops:
  7.2 1.5 reshape_squeeze.3
  8.6 4.8 %copy.75 = bf16[4,32,4096]{1,0,2:T(4,128)(2,1)} copy(bf16[4,32,4096]{2,0,1:T(4,128)(2,1)S(1)} %bitcast.74) | data formatting | bytes 2097152 | tf_op jit(solution)/shard_map/transpose | solution.py:45
  13.5 7.8 %reshape.46 = bf16[8,2,32768]{2,1,0:T(2,128)(2,1)} reshape(bf16[4096,4,32]{2,1,0:T(4,128)(2,1)} %bitcast.70) | data formatting | bytes 2097152
  21.3 6.0 %all-to-all-start.1 = ((bf16[8,2,32768]{2,1,0:T(2,128)(2,1)}), bf16[8,2,32768]{2,1,0:T(2,128)(2,1)}, u32[]{:S(2)}, u32[]{:S(2)}) async-start(bf16[8,2,32768]{2,1,0:T(2,128)(2,1)} %reshape.46), calls=%async_computation.1 | async-start | bytes 2097152 | tf_op jit(solution)/shard_map/all_to_all | solution.py:66
  28.0 21.5 %all-gather = s32[1,1024]{1,0:T(1,128)S(1)} all-gather(s32[1,128]{1,0:T(1,128)S(1)} %copy-done.38), channel_id=2, replica_groups=mesh['dp'=16,'ctx'=8] {'ctx'}, dimensions={1}, use_global_device_ids=true | all-gather | bytes 4608 | tf_op jit(solution)/shard_map/all_gather | solution.py:59
  50.9 1.8 fusion.60
  52.8 1.3 slice.424
  54.1 1.0 slice.425
  55.1 1.0 constant_dynamic-slice_fusion.4
  56.1 0.9 pad_slice_fusion.7
  57.1 7.2 %reshape.47 = bf16[4096,4,32]{2,1,0:T(4,128)(2,1)} reshape(bf16[8,2,32768]{2,1,0:T(2,128)(2,1)} %all-to-all-done.1) | data formatting | bytes 2097152
  64.3 6.3 %copy.76 = bf16[4,32,4096]{2,1,0:T(8,128)(2,1)} copy(bf16[4,32,4096]{1,0,2:T(4,128)(2,1)} %bitcast.71) | data formatting | bytes 2097152 | tf_op jit(solution)/shard_map/all_to_all | solution.py:66
  70.6 1.6 copy.89
  72.5 1.2 copy.77
  74.3 2.5 %fusion.57 = (bf16[4,256,512]{2,1,0:T(8,128)(2,1)S(1)}, f32[4,256,512]{2,1,0:T(8,128)}) fusion(f32[4,8,32,512]{3,2,1,0:T(8,128)S(1)} %copy.77, f32[2,256,512]{2,1,0:T(8,128)S(1)} %copy-done.32, f32[2,256,512]{2,1,0:T(8,128)S(1)} %pad_slice_fusion.6, f32[512]{0:T(512)S(1)} %bitcast.82, f32[3,256,512]{2,1,0:T(8,128)S(1)} %copy-done.28, ...), kind=kLoop, calls=%fused_computation.76 | loop fusion | flops 4718592 | bytes 11540480 | tf_op jit(solution)/shard_map/convert_element_type | solution.py:80
  76.7 0.7 fusion.110
  77.5 1.5 fusion.98
  79.0 1.8 fusion.100
  80.7 2.1 %reshape.27 = bf16[256,4,512]{2,1,0:T(4,128)(2,1)} reshape(bf16[1024,512]{1,0:T(8,128)(2,1)} %all-gather.3.cloned.1.call-done) | data formatting | bytes 2097152 | tf_op jit(solution)/shard_map/reshape | solution.py:45
  82.9 2.3 %fusion.73 = f32[4,512,512]{2,1,0:T(8,128)S(1)} fusion(bf16[4,512,256]{2,1,0:T(8,128)(2,1)} %constant.6.clone, bf16[256,4,512]{2,1,0:T(4,128)(2,1)} %reshape.27), kind=kOutput, calls=%fused_computation.107 | convolution fusion | flops 536870912 | bytes 6291456 | tf_op jit(solution)/shard_map/jkn,jnc->jkc/dot_general | solution.py:25
  87.5 1.0 multiply_subtract_fusion.1
  88.5 1.0 multiply_add_fusion.1
  90.9 0.8 copy-done.29
  92.7 2.0 %bitcast_multiply_fusion.1 = (f32[4,256,512]{2,1,0:T(8,128)S(1)}, f32[4,256,512]{2,1,0:T(8,128)S(1)}, f32[4,256,512]{2,1,0:T(8,128)S(1)}, f32[4,256,512]{2,1,0:T(8,128)S(1)}) fusion(f32[2,256,512]{2,1,0:T(8,128)S(1)} %copy-done.33, f32[2,256,512]{2,1,0:T(8,128)S(1)} %copy-done.31, f32[512]{0:T(512)S(1)} %bitcast.98, f32[3,256,512]{2,1,0:T(8,128)S(1)} %copy-done.29, ...), kind=kOutput, calls=%fused_computation.73 | convolution fusion | flops 562036736 | bytes 17838080 | tf_op jit(solution)/shard_map/jnk,jkc->jnc/dot_general | solution.py:41
  94.7 0.7 fusion.72
  96.5 1.0 multiply_subtract_fusion
  97.5 1.1 multiply_add_fusion.2
  98.7 1.1 multiply_subtract_fusion.2
  101.0 0.7 copy-done.36
  101.7 0.8 copy-done.27
  102.4 1.9 %bitcast_multiply_fusion.3 = (f32[4,256,512]{2,1,0:T(8,128)S(1)}, bf16[4,256,512]{2,1,0:T(8,128)(2,1)}) fusion(f32[4,8,32,512]{3,2,1,0:T(8,128)S(1)} %copy-done.27, f32[4,256,512]{2,1,0:T(8,128)S(1)} %copy-done.36, bf16[4,256,512]{2,1,0:T(8,128)(2,1)S(1)} %copy-done.39, bf16[1,256,512]{2,1,0:T(8,128)(2,1)S(1)} %get-tuple-element.16, ...), kind=kOutput, calls=%fused_computation.75 | convolution fusion | flops 556269568 | bytes 10485760 | tf_op jit(solution)/shard_map/jnk,jkc->jnc/dot_general | solution.py:41
  106.2 3.5 %fusion.71 = bf16[512,512]{1,0:T(8,128)(2,1)} fusion(s32[4,256]{1,0:T(4,128)S(1)} %copy.67, f32[1,256,512]{2,1,0:T(8,128)S(1)} %pad_slice_fusion.5, f32[3,256,512]{2,1,0:T(8,128)S(1)} %slice.450, f32[2,256,512]{2,1,0:T(8,128)S(1)} %pad_slice_fusion.4, f32[2,256,512]{2,1,0:T(8,128)S(1)} %slice.452, f32[1,256,512]{2,1,0:T(8,128)S(1)} %pad_slice_fusion.3, ...), kind=kOutput, calls=%fused_computation.105 | convolution fusion | flops 550240256 | bytes 19421184 | tf_op jit(solution)/shard_map/jnv,jnc->vc/dot_general | solution.py:96
  109.7 11.8 %all-to-all-start.2 = ((bf16[16,32,512]{2,1,0:T(8,128)(2,1)}), bf16[16,32,512]{2,1,0:T(8,128)(2,1)}, u32[]{:S(2)}, u32[]{:S(2)}) async-start(bf16[16,32,512]{2,1,0:T(8,128)(2,1)} %bitcast.80), calls=%async_computation.2 | async-start | bytes 1048576 | tf_op jit(solution)/shard_map/all_to_all | solution.py:97
  121.6 1.0 add_convert_fusion.1
  122.5 3.5 %copy.72 = bf16[4,256,512]{2,0,1:T(4,128)(2,1)} copy(bf16[4,256,512]{2,1,0:T(8,128)(2,1)} %get-tuple-element.60) | data formatting | bytes 2097152 | tf_op jit(solution)/shard_map/convert_element_type | solution.py:77
  126.1 3.3 %multiply_add_fusion = f32[4,256,512]{2,1,0:T(8,128)} fusion(f32[1,256,512]{2,1,0:T(8,128)S(1)} %copy-done.4, f32[1,256,512]{2,1,0:T(8,128)S(1)} %get-tuple-element.40, f32[1,256,512]{2,1,0:T(8,128)S(1)} %copy-done.12, f32[1,256,512]{2,1,0:T(8,128)S(1)} %copy-done.8, f32[1,256,512]{2,1,0:T(8,128)S(1)} %copy-done.10, f32[1,256,512]{2,1,0:T(8,128)S(1)} %copy-done.2, ...), kind=kLoop, calls=%fused_computation.81 | loop fusion | flops 7864320 | bytes 10485760 | tf_op jit(solution)/shard_map/add | solution.py:84
  129.4 3.5 %all-to-all-done.2 = bf16[16,32,512]{2,1,0:T(8,128)(2,1)} async-done(((bf16[16,32,512]{2,1,0:T(8,128)(2,1)}), bf16[16,32,512]{2,1,0:T(8,128)(2,1)}, u32[]{:S(2)}, u32[]{:S(2)}) %all-to-all-start.2) | async-done | bytes 524320 | tf_op jit(solution)/shard_map/all_to_all | solution.py:97
  132.9 3.6 %all-to-all-start = ((bf16[4,256,512]{2,0,1:T(4,128)(2,1)}), bf16[4,256,512]{2,0,1:T(4,128)(2,1)S(1)}, u32[]{:S(2)}, u32[]{:S(2)}) async-start(bf16[4,256,512]{2,0,1:T(4,128)(2,1)} %copy.72), calls=%async_computation | async-start | bytes 2097152 | tf_op jit(solution)/shard_map/all_to_all | solution.py:78
  136.5 1.9 %add_convert_fusion.3 = (bf16[1,256,512]{2,1,0:T(8,128)(2,1)S(1)}, bf16[1,256,512]{2,1,0:T(8,128)(2,1)S(1)}) fusion(f32[4,256,512]{2,1,0:T(8,128)} %multiply_add_fusion), kind=kLoop, calls=%fused_computation.123 | loop fusion | flops 786432 | bytes 2621440 | tf_op jit(solution)/shard_map/convert.11
  140.0 0.9 fusion.61
  140.9 1.1 copy.96
  142.0 10.2 %all-to-all-done = bf16[4,256,512]{2,0,1:T(4,128)(2,1)S(1)} async-done(((bf16[4,256,512]{2,0,1:T(4,128)(2,1)}), bf16[4,256,512]{2,0,1:T(4,128)(2,1)S(1)}, u32[]{:S(2)}, u32[]{:S(2)}) %all-to-all-start) | async-done | bytes 1048608 | tf_op jit(solution)/shard_map/all_to_all | solution.py:78
  152.2 4.3 %all-to-all-start.3 = ((bf16[16,4,16,512]{3,2,1,0:T(8,128)(2,1)}), bf16[16,4,16,512]{3,2,1,0:T(8,128)(2,1)S(1)}, u32[]{:S(2)}, u32[]{:S(2)}) async-start(bf16[16,4,16,512]{3,2,1,0:T(8,128)(2,1)} %bitcast.64), calls=%async_computation.3 | async-start | bytes 2097152 | tf_op jit(solution)/shard_map/all_to_all | solution.py:86
  156.5 1.7 convert_reduce_fusion.1
  159.4 0.8 copy.74
  160.2 1.1 broadcast_in_dim_reshape.3
  161.3 12.5 %all-to-all-done.3 = bf16[16,4,16,512]{3,2,1,0:T(8,128)(2,1)S(1)} async-done(((bf16[16,4,16,512]{3,2,1,0:T(8,128)(2,1)}), bf16[16,4,16,512]{3,2,1,0:T(8,128)(2,1)S(1)}, u32[]{:S(2)}, u32[]{:S(2)}) %all-to-all-start.3) | async-done | bytes 1048608 | tf_op jit(solution)/shard_map/all_to_all | solution.py:86
  174.1 0.7 reshape.30
  (118 shorter events, 14.5 us)
Async XLA Ops:
  21.3 6.7 %copy-start.38 = (s32[1,128]{1,0:T(1,128)S(1)}, s32[1,128]{1,0:T(1,128)}, u32[]{:S(2)}) copy-start(s32[1,128]{1,0:T(1,128)} %param.7) | copy-start | bytes 1540
  21.3 35.8 %all-to-all-start.1 = ((bf16[8,2,32768]{2,1,0:T(2,128)(2,1)}), bf16[8,2,32768]{2,1,0:T(2,128)(2,1)}, u32[]{:S(2)}, u32[]{:S(2)}) async-start(bf16[8,2,32768]{2,1,0:T(2,128)(2,1)} %reshape.46), calls=%async_computation.1 | async-start | bytes 2097152 | tf_op jit(solution)/shard_map/all_to_all | solution.py:66
  27.3 53.4 %all-gather.3.cloned.1.call-start = ((), (), s32[]{:S(2)}) async-start(), calls=%async_computation.4 | async-start | bytes 1114112 | tf_op jit(solution)/shard_map/all_gather | solution.py:67
  57.1 16.6 %copy-start.30 = (f32[2,256,512]{2,1,0:T(8,128)}, f32[2,256,512]{2,1,0:T(8,128)S(1)}, u32[]{:S(2)}) copy-start(f32[2,256,512]{2,1,0:T(8,128)S(1)} %pad_slice_fusion.6) | copy-start | bytes 3145732
  72.4 1.4 copy-start.28
  72.4 1.7 copy-start.32
  72.4 1.8 %copy-start.34 = (f32[1,256,512]{2,1,0:T(8,128)S(1)}, f32[1,256,512]{2,1,0:T(8,128)}, u32[]{:S(2)}) copy-start(f32[1,256,512]{2,1,0:T(8,128)} %pad_slice_fusion.7) | copy-start | bytes 1572868
  73.7 3.1 %copy-start.26 = (f32[4,8,32,512]{3,2,1,0:T(8,128)}, f32[4,8,32,512]{3,2,1,0:T(8,128)S(1)}, u32[]{:S(2)}) copy-start(f32[4,8,32,512]{3,2,1,0:T(8,128)S(1)} %copy.77) | copy-start | bytes 6291460
  74.3 2.5 %copy-start.24 = (bf16[4,512,256]{2,1,0:T(8,128)(2,1)S(1)}, bf16[4,512,256]{2,1,0:T(8,128)(2,1)}, u32[]{:S(2)}) copy-start(bf16[4,512,256]{2,1,0:T(8,128)(2,1)} %constant.6.clone) | copy-start | bytes 3145732
  85.7 1.0 copy-start.1
  85.7 1.2 copy-start.3
  85.7 1.3 copy-start.5
  85.7 1.5 copy-start.7
  85.7 1.6 copy-start.9
  85.7 1.8 copy-start.11
  90.2 1.4 copy-start.29
  90.2 1.7 copy-start.31
  90.2 2.0 %copy-start.33 = (f32[2,256,512]{2,1,0:T(8,128)S(1)}, f32[2,256,512]{2,1,0:T(8,128)}, u32[]{:S(2)}) copy-start(f32[2,256,512]{2,1,0:T(8,128)} %slice.425) | copy-start | bytes 3145732
  90.2 2.1 %copy-start.35 = (f32[1,256,512]{2,1,0:T(8,128)S(1)}, f32[1,256,512]{2,1,0:T(8,128)}, u32[]{:S(2)}) copy-start(f32[1,256,512]{2,1,0:T(8,128)} %pad_slice_fusion.7) | copy-start | bytes 1572868
  90.2 2.5 %copy-start.39 = (bf16[4,256,512]{2,1,0:T(8,128)(2,1)S(1)}, bf16[4,256,512]{2,1,0:T(8,128)(2,1)}, u32[]{:S(2)}) copy-start(bf16[4,256,512]{2,1,0:T(8,128)(2,1)} %constant.18.clone) | copy-start | bytes 3145732
  92.7 2.0 %copy-start.25 = (bf16[4,512,256]{2,1,0:T(8,128)(2,1)S(1)}, bf16[4,512,256]{2,1,0:T(8,128)(2,1)}, u32[]{:S(2)}) copy-start(bf16[4,512,256]{2,1,0:T(8,128)(2,1)} %constant.6.clone) | copy-start | bytes 3145732
  95.9 2.7 %copy-start.13 = (f32[1,256,512]{2,1,0:T(8,128)}, f32[1,256,512]{2,1,0:T(8,128)S(1)}, u32[]{:S(2)}) copy-start(f32[1,256,512]{2,1,0:T(8,128)S(1)} %get-tuple-element.19) | copy-start | bytes 1572868
  95.9 2.7 %copy-start.15 = (f32[1,256,512]{2,1,0:T(8,128)}, f32[1,256,512]{2,1,0:T(8,128)S(1)}, u32[]{:S(2)}) copy-start(f32[1,256,512]{2,1,0:T(8,128)S(1)} %get-tuple-element.20) | copy-start | bytes 1572868
  95.9 2.7 %copy-start.17 = (f32[1,256,512]{2,1,0:T(8,128)}, f32[1,256,512]{2,1,0:T(8,128)S(1)}, u32[]{:S(2)}) copy-start(f32[1,256,512]{2,1,0:T(8,128)S(1)} %get-tuple-element.21) | copy-start | bytes 1572868
  95.9 2.7 %copy-start.19 = (f32[1,256,512]{2,1,0:T(8,128)}, f32[1,256,512]{2,1,0:T(8,128)S(1)}, u32[]{:S(2)}) copy-start(f32[1,256,512]{2,1,0:T(8,128)S(1)} %get-tuple-element.22) | copy-start | bytes 1572868
  96.5 2.2 %copy-start.20 = (f32[1,256,512]{2,1,0:T(8,128)}, f32[1,256,512]{2,1,0:T(8,128)S(1)}, u32[]{:S(2)}) copy-start(f32[1,256,512]{2,1,0:T(8,128)S(1)} %get-tuple-element.23) | copy-start | bytes 1572868
  96.5 2.2 %copy-start.21 = (f32[1,256,512]{2,1,0:T(8,128)}, f32[1,256,512]{2,1,0:T(8,128)S(1)}, u32[]{:S(2)}) copy-start(f32[1,256,512]{2,1,0:T(8,128)S(1)} %get-tuple-element.24) | copy-start | bytes 1572868
  96.5 2.2 %copy-start.22 = (f32[1,256,512]{2,1,0:T(8,128)}, f32[1,256,512]{2,1,0:T(8,128)S(1)}, u32[]{:S(2)}) copy-start(f32[1,256,512]{2,1,0:T(8,128)S(1)} %get-tuple-element.25) | copy-start | bytes 1572868
  96.5 2.2 %copy-start.23 = (f32[1,256,512]{2,1,0:T(8,128)}, f32[1,256,512]{2,1,0:T(8,128)S(1)}, u32[]{:S(2)}) copy-start(f32[1,256,512]{2,1,0:T(8,128)S(1)} %get-tuple-element.26) | copy-start | bytes 1572868
  100.1 1.6 copy-start.36
  100.7 1.8 copy-start.27
  109.7 23.2 %all-to-all-start.2 = ((bf16[16,32,512]{2,1,0:T(8,128)(2,1)}), bf16[16,32,512]{2,1,0:T(8,128)(2,1)}, u32[]{:S(2)}, u32[]{:S(2)}) async-start(bf16[16,32,512]{2,1,0:T(8,128)(2,1)} %bitcast.80), calls=%async_computation.2 | async-start | bytes 1048576 | tf_op jit(solution)/shard_map/all_to_all | solution.py:97
  121.5 4.5 %copy-start.2 = (f32[1,256,512]{2,1,0:T(8,128)S(1)}, f32[1,256,512]{2,1,0:T(8,128)}, u32[]{:S(2)}) copy-start(f32[1,256,512]{2,1,0:T(8,128)} %get-tuple-element.41) | copy-start | bytes 1572868
  121.5 4.5 %copy-start.4 = (f32[1,256,512]{2,1,0:T(8,128)S(1)}, f32[1,256,512]{2,1,0:T(8,128)}, u32[]{:S(2)}) copy-start(f32[1,256,512]{2,1,0:T(8,128)} %get-tuple-element.42) | copy-start | bytes 1572868
  121.5 4.5 %copy-start.6 = (f32[1,256,512]{2,1,0:T(8,128)S(1)}, f32[1,256,512]{2,1,0:T(8,128)}, u32[]{:S(2)}) copy-start(f32[1,256,512]{2,1,0:T(8,128)} %get-tuple-element.43) | copy-start | bytes 1572868
  121.5 4.5 %copy-start.8 = (f32[1,256,512]{2,1,0:T(8,128)S(1)}, f32[1,256,512]{2,1,0:T(8,128)}, u32[]{:S(2)}) copy-start(f32[1,256,512]{2,1,0:T(8,128)} %get-tuple-element.44) | copy-start | bytes 1572868
  121.5 4.5 %copy-start.10 = (f32[1,256,512]{2,1,0:T(8,128)S(1)}, f32[1,256,512]{2,1,0:T(8,128)}, u32[]{:S(2)}) copy-start(f32[1,256,512]{2,1,0:T(8,128)} %get-tuple-element.45) | copy-start | bytes 1572868
  121.5 4.5 %copy-start.12 = (f32[1,256,512]{2,1,0:T(8,128)S(1)}, f32[1,256,512]{2,1,0:T(8,128)}, u32[]{:S(2)}) copy-start(f32[1,256,512]{2,1,0:T(8,128)} %get-tuple-element.46) | copy-start | bytes 1572868
  121.5 4.5 %copy-start.14 = (f32[1,256,512]{2,1,0:T(8,128)S(1)}, f32[1,256,512]{2,1,0:T(8,128)}, u32[]{:S(2)}) copy-start(f32[1,256,512]{2,1,0:T(8,128)} %copy-done.13) | copy-start | bytes 1572868
  121.5 4.5 %copy-start.16 = (f32[1,256,512]{2,1,0:T(8,128)S(1)}, f32[1,256,512]{2,1,0:T(8,128)}, u32[]{:S(2)}) copy-start(f32[1,256,512]{2,1,0:T(8,128)} %copy-done.15) | copy-start | bytes 1572868
  121.6 4.5 %copy-start.18 = (f32[1,256,512]{2,1,0:T(8,128)S(1)}, f32[1,256,512]{2,1,0:T(8,128)}, u32[]{:S(2)}) copy-start(f32[1,256,512]{2,1,0:T(8,128)} %copy-done.17) | copy-start | bytes 1572868
  132.9 19.3 %all-to-all-start = ((bf16[4,256,512]{2,0,1:T(4,128)(2,1)}), bf16[4,256,512]{2,0,1:T(4,128)(2,1)S(1)}, u32[]{:S(2)}, u32[]{:S(2)}) async-start(bf16[4,256,512]{2,0,1:T(4,128)(2,1)} %copy.72), calls=%async_computation | async-start | bytes 2097152 | tf_op jit(solution)/shard_map/all_to_all | solution.py:78
  136.4 2.2 %copy-start = (f32[4,256,512]{2,1,0:T(8,128)S(1)}, f32[4,256,512]{2,1,0:T(8,128)}, u32[]{:S(2)}) copy-start(f32[4,256,512]{2,1,0:T(8,128)} %multiply_add_fusion) | copy-start | bytes 6291460
  138.7 0.9 copy-start.37
  138.7 1.3 copy-start.40
  152.2 21.6 %all-to-all-start.3 = ((bf16[16,4,16,512]{3,2,1,0:T(8,128)(2,1)}), bf16[16,4,16,512]{3,2,1,0:T(8,128)(2,1)S(1)}, u32[]{:S(2)}, u32[]{:S(2)}) async-start(bf16[16,4,16,512]{3,2,1,0:T(8,128)(2,1)} %bitcast.64), calls=%async_computation.3 | async-start | bytes 2097152 | tf_op jit(solution)/shard_map/all_to_all | solution.py:86
Sparse Core Ops, SparseCore 0:
  30.6 48.2 all-gather.2

commit v2 on v1

v2 whole, which is shorter than its diff:
```python
import functools
import math

import jax
import jax.numpy as jnp
import numpy as np
from jax import lax
from jax.experimental import pallas as pl
from jax.experimental.pallas import tpu as pltpu
from jax.sharding import PartitionSpec as P

BF = jnp.bfloat16
F32 = jnp.float32
MESH = pl.DeviceIdType.MESH
LANES = 128
KC = 16


def tables(length, block):
    sub = length // 4
    k = np.arange(sub)[None, :, None]
    t = 4 * np.arange(sub)[None, None, :] + np.arange(4)[:, None, None]
    angle = 2.0 * math.pi * (((4 * k + 1) * t) % (4 * length)) / (4 * length)
    fwd = np.concatenate([np.cos(angle), -np.sin(angle)], 1)
    inv = fwd.transpose(0, 2, 1) / length
    out = np.arange(block)
    perm = np.zeros((2, block, block))
    perm[0, out, 4 * (out % (block // 4)) + out // (block // 4)] = 1.0
    perm[1] = perm[0].T
    return jnp.asarray(fwd, BF), jnp.asarray(inv, BF), jnp.asarray(perm, BF)


def radix4(re, im, sign):
    a_re, a_im, b_re, b_im = re[0] + re[2], im[0] + im[2], re[0] - re[2], im[0] - im[2]
    c_re, c_im, d_re, d_im = re[1] + re[3], im[1] + im[3], re[1] - re[3], im[1] - im[3]
    if sign > 0:
        d_re, d_im = -d_re, -d_im
    return (
        [a_re + c_re, b_re + d_im, a_re - c_re, b_re - d_im],
        [a_im + c_im, b_im - d_re, a_im - c_im, b_im + d_re],
    )


def loop(count, step):
    def run(i, carry):
        step(i)
        return carry

    lax.fori_loop(0, count, run, 0)


def dot(a, b):
    return jnp.dot(a, b, preferred_element_type=F32)


def kernel(
    dims,
    ids_ref, perm, emb_hbm, taps_hbm, lf_hbm, cot_hbm, fwd_hbm, inv_hbm,
    mixed_hbm, ge_ref, gf_ref,
    ids_in, emb, taps, lf_in, cot_in, fwd, inv,
    x, uq, uk, uv, field, hfield, spec_h, spec_z, pbuf, wbuf, wf, conv, gq, gx,
    mixed_out, gf_out, gf_in, ge_acc, ge_out, ge_in,
    local_sem, ids_send, ids_recv, lf_send, lf_recv, cot_send, cot_recv,
    mix_send, mix_recv, gf_send, gf_recv, ge_send, ge_recv,
):
    dp_n, ctx_n, vocab, part, block = dims
    cw = part // 2
    sub = ctx_n * block // 4
    bs = block // 4
    pair_n = 2 * ctx_n
    per = dp_n // ctx_n
    lr = block // per
    vr = vocab // dp_n
    dp = lax.axis_index("dp")
    p_me = lax.axis_index("ctx")
    g = lax.div(dp, 2)
    c_me = lax.rem(dp, 2)
    pair_me = c_me * ctx_n + p_me
    first = pl.multiple_of(p_me * part + c_me * cw, cw)
    halves = [pl.ds(h * LANES, LANES) for h in range(cw // LANES)]

    def chunk(i, size):
        return pl.ds(pl.multiple_of(i * size, size), size)

    loads = [
        pltpu.make_async_copy(emb_hbm.at[:, pl.ds(first, cw)], emb, local_sem.at[0]),
        pltpu.make_async_copy(taps_hbm.at[:, :, pl.ds(first, cw)], taps, local_sem.at[1]),
        pltpu.make_async_copy(fwd_hbm, fwd, local_sem.at[2]),
        pltpu.make_async_copy(inv_hbm, inv, local_sem.at[3]),
    ]
    for load in loads:
        load.start()

    barrier = pltpu.get_barrier_semaphore()

    def greet_pair(i):
        to = lax.rem(pair_me + 1 + i, pair_n)
        device = (2 * g + lax.div(to, ctx_n), lax.rem(to, ctx_n))
        pl.semaphore_signal(barrier, inc=1, device_id=device, device_id_type=MESH)

    def greet_dp(i):
        device = (lax.rem(dp + 1 + i, dp_n), p_me)
        pl.semaphore_signal(barrier, inc=1, device_id=device, device_id_type=MESH)

    loop(pair_n - 1, greet_pair)
    loop(dp_n - 1, greet_dp)
    pl.semaphore_wait(barrier, pair_n + dp_n - 2)

    def ids_copy(to):
        return pltpu.make_async_remote_copy(
            src_ref=ids_ref, dst_ref=ids_in.at[pair_me], send_sem=ids_send.at[to], recv_sem=ids_recv.at[pair_me],
            device_id=(2 * g + lax.div(to, ctx_n), lax.rem(to, ctx_n)), device_id_type=MESH,
        )

    def lf_copy(to):
        return pltpu.make_async_remote_copy(
            src_ref=lf_hbm.at[:, chunk(lax.rem(to, 2), cw)], dst_ref=lf_in.at[dp],
            send_sem=lf_send.at[to], recv_sem=lf_recv.at[dp], device_id=(to, p_me), device_id_type=MESH,
        )

    def cot_columns(to):
        return cot_hbm.at[0, :, chunk(2 * lax.rem(to, ctx_n) + lax.div(to, ctx_n), cw)]

    def cot_copy(to):
        return pltpu.make_async_remote_copy(
            src_ref=cot_columns(to), dst_ref=cot_in.at[pair_me], send_sem=cot_send.at[to], recv_sem=cot_recv.at[pair_me],
            device_id=(2 * g + lax.div(to, ctx_n), lax.rem(to, ctx_n)), device_id_type=MESH,
        )

    def mix_copy(to):
        return pltpu.make_async_remote_copy(
            src_ref=mixed_out.at[to], dst_ref=mixed_hbm.at[0, :, pl.ds(first, cw)],
            send_sem=mix_send.at[to], recv_sem=mix_recv.at[pair_me],
            device_id=(2 * g + lax.div(to, ctx_n), lax.rem(to, ctx_n)), device_id_type=MESH,
        )

    def gf_copy(to):
        return pltpu.make_async_remote_copy(
            src_ref=gf_out.at[to], dst_ref=gf_in.at[dp], send_sem=gf_send.at[to], recv_sem=gf_recv.at[dp],
            device_id=(to, p_me), device_id_type=MESH,
        )

    def ge_copy(to):
        return pltpu.make_async_remote_copy(
            src_ref=ge_out.at[chunk(to, vr)], dst_ref=ge_in.at[dp], send_sem=ge_send.at[to], recv_sem=ge_recv.at[dp],
            device_id=(to, p_me), device_id_type=MESH,
        )

    def others(count, me, step):
        loop(count - 1, lambda i: step(lax.rem(me + 1 + i, count)))

    def arrived(slot, sem):
        pltpu.make_async_copy(slot, slot, sem).wait()

    pltpu.make_async_copy(ids_ref, ids_in.at[pair_me], ids_recv.at[pair_me]).start()
    pltpu.make_async_copy(lf_hbm.at[:, chunk(c_me, cw)], lf_in.at[dp], lf_recv.at[dp]).start()
    pltpu.make_async_copy(cot_columns(pair_me), cot_in.at[pair_me], cot_recv.at[pair_me]).start()
    others(pair_n, pair_me, lambda to: ids_copy(to).start())
    others(dp_n, dp, lambda to: lf_copy(to).start())
    others(pair_n, pair_me, lambda to: cot_copy(to).start())

    loads[0].wait()
    loads[1].wait()
    vocab_lane = lax.broadcasted_iota(jnp.int32, (block, LANES), 1).astype(F32)

    def embed(i):
        s, p = lax.div(i, ctx_n), lax.rem(i, ctx_n)
        arrived(ids_in.at[i], ids_recv.at[i])
        row = ids_in[i, 0:1, :].astype(F32)
        column = jnp.transpose(jnp.broadcast_to(row, (block, block)))
        onehot = jnp.concatenate(
            [(column == vocab_lane + float(q * LANES)).astype(F32).astype(BF) for q in range(vocab // LANES)], 1
        )
        rows = dot(onehot, emb[...])
        for j in range(4):
            x[s, j, chunk(p, bs), :] = rows[j * bs : (j + 1) * bs]

    loop(pair_n, embed)

    row16 = lax.broadcasted_iota(jnp.int32, (bs, LANES), 0)
    for h in halves:
        f = [[taps[r, i : i + 1, h] for i in range(3)] for r in range(3)]

        def short(s, h=h, f=f):
            def step(p, carry):
                rows = chunk(p, bs)
                xs = [x[s, j, rows, h] for j in range(4)]
                turned = [pltpu.roll(xs[2], 1, 0), pltpu.roll(xs[3], 1, 0)]
                late = [jnp.where(row16 == 0, carry[q], turned[q]) for q in range(2)]
                line = late + xs
                us = [
                    [f[r][0] * line[j + 2] + f[r][1] * line[j + 1] + f[r][2] * line[j] for j in range(4)]
                    for r in range(3)
                ]
                for j in range(4):
                    uq[s, j, rows, h] = us[0][j]
                    uk[s, j, rows, h] = us[1][j]
                    uv[s, j, rows, h] = us[2][j]
                    field[s, j, rows, h] = (us[1][j] * us[2][j]).astype(BF)
                return tuple(turned)

            zero = jnp.zeros((bs, LANES), F32)
            lax.fori_loop(0, ctx_n, step, (zero, zero))

        loop(2, short)

    loads[2].wait()

    def gather_taps(i):
        for q in range(per):
            arrived(lf_in.at[i * per + q], lf_recv.at[i * per + q])
        rows = jnp.concatenate([lf_in[i * per + q] for q in range(per)], 0)
        rows = dot(perm[0], rows).astype(BF)
        for j in range(4):
            hfield[j, chunk(i, bs), :] = rows[j * bs : (j + 1) * bs]

    loop(ctx_n, gather_taps)

    def filter_dft(j):
        pbuf[0, j] = dot(fwd[j], hfield[j])

    loop(4, filter_dft)

    def butterfly(s, i, h):
        re = [pbuf[s, j, chunk(i, KC), h] for j in range(4)]
        im = [pbuf[s, j, pl.ds(pl.multiple_of(sub + i * KC, KC), KC), h] for j in range(4)]
        return radix4(re, im, -1)

    def filter_mix(i):
        for h in halves:
            re, im = butterfly(0, i, h)
            for m in range(4):
                spec_h[m, 0, chunk(i, KC), h] = re[m]
                spec_h[m, 1, chunk(i, KC), h] = im[m]

    loop(sub // KC, filter_mix)

    def field_dft(i):
        s, j = lax.div(i, 4), lax.rem(i, 4)
        pbuf[s, j] = dot(fwd[j], field[s, j])

    def put(ref, i, h, re, im):
        re, im = radix4(re, im, 1)
        for j in range(4):
            ref[j, chunk(i, KC), h] = re[j].astype(BF)
            ref[j, pl.ds(pl.multiple_of(sub + i * KC, KC), KC), h] = im[j].astype(BF)

    loop(8, field_dft)
    loads[3].wait()

    for s in range(2):

        def conv_mix(i, s=s):
            for h in halves:
                re, im = butterfly(s, i, h)
                out_re, out_im = [], []
                for m in range(4):
                    spec_z[s, m, 0, chunk(i, KC), h] = re[m]
                    spec_z[s, m, 1, chunk(i, KC), h] = im[m]
                    h_re, h_im = spec_h[m, 0, chunk(i, KC), h], spec_h[m, 1, chunk(i, KC), h]
                    out_re.append(re[m] * h_re - im[m] * h_im)
                    out_im.append(re[m] * h_im + im[m] * h_re)
                put(wbuf.at[s], i, h, out_re, out_im)

        loop(sub // KC, conv_mix)

        def conv_idft(j, s=s):
            conv[s, j] = dot(inv[j], wbuf[s, j]).astype(BF).astype(F32)

        loop(4, conv_idft)

        def mix(i, s=s):
            p = lax.rem(p_me + 1 + i, ctx_n)
            rows = chunk(p, bs)
            out = jnp.concatenate([(uq[s, j, rows, :] * conv[s, j, rows, :]).astype(BF) for j in range(4)], 0)
            to = s * ctx_n + p
            mixed_out[to] = dot(perm[1], out).astype(BF)

            @pl.when(to != pair_me)
            def _():
                mix_copy(to).start()

            @pl.when(to == pair_me)
            def _():
                pltpu.make_async_copy(
                    mixed_out.at[to], mixed_hbm.at[0, :, pl.ds(first, cw)], mix_recv.at[pair_me]
                ).start()

        loop(ctx_n, mix)

    def take(i):
        s, p = lax.div(i, ctx_n), lax.rem(i, ctx_n)
        arrived(cot_in.at[i], cot_recv.at[i])
        out = dot(perm[0], cot_in[i])
        rows = chunk(p, bs)
        for j in range(4):
            piece = out[j * bs : (j + 1) * bs]
            field[s, j, rows, :] = (piece * uq[s, j, rows, :]).astype(BF)
            gq[s, j, rows, :] = piece * conv[s, j, rows, :]

    loop(pair_n, take)
    loop(8, field_dft)

    def back_mix(i):
        for h in halves:
            sum_re, sum_im = None, None
            for s in range(2):
                re, im = butterfly(s, i, h)
                out_re, out_im, f_re, f_im = [], [], [], []
                for m in range(4):
                    h_re, h_im = spec_h[m, 0, chunk(i, KC), h], spec_h[m, 1, chunk(i, KC), h]
                    z_re, z_im = spec_z[s, m, 0, chunk(i, KC), h], spec_z[s, m, 1, chunk(i, KC), h]
                    out_re.append(re[m] * h_re + im[m] * h_im)
                    out_im.append(im[m] * h_re - re[m] * h_im)
                    f_re.append(re[m] * z_re + im[m] * z_im)
                    f_im.append(im[m] * z_re - re[m] * z_im)
                put(wbuf.at[s], i, h, out_re, out_im)
                if s == 0:
                    sum_re, sum_im = f_re, f_im
                else:
                    sum_re = [a + b for a, b in zip(sum_re, f_re)]
                    sum_im = [a + b for a, b in zip(sum_im, f_im)]
            put(wf, i, h, sum_re, sum_im)

    loop(sub // KC, back_mix)

    def filter_idft(j):
        hfield[j] = dot(inv[j], wf[j]).astype(BF)

    loop(4, filter_idft)

    def filter_rows(i):
        rows = jnp.concatenate([hfield[j, chunk(i, bs), :] for j in range(4)], 0)
        rows = dot(perm[1], rows).astype(BF)
        for q in range(per):
            gf_out[i * per + q] = rows[q * lr : (q + 1) * lr]

    loop(ctx_n, filter_rows)
    others(dp_n, dp, lambda to: gf_copy(to).start())
    pltpu.make_async_copy(gf_out.at[dp], gf_in.at[dp], gf_recv.at[dp]).start()

    def gz_idft(i):
        s, j = lax.div(i, 4), lax.rem(i, 4)
        conv[s, j] = dot(inv[j], wbuf[s, j])

    loop(8, gz_idft)

    for h in halves:
        f = [[taps[r, i : i + 1, h] for i in range(3)] for r in range(3)]

        def grad(s, h=h, f=f):
            def step(i, carry):
                p = ctx_n - 1 - i
                rows = chunk(p, bs)
                lines = [[], [], []]
                for j in range(4):
                    gz = conv[s, j, rows, h].astype(BF).astype(F32)
                    gs = [gq[s, j, rows, h], gz * uv[s, j, rows, h], gz * uk[s, j, rows, h]]
                    for tap in range(3):
                        lines[tap].append(f[0][tap] * gs[0] + f[1][tap] * gs[1] + f[2][tap] * gs[2])
                turned = [pltpu.roll(v, bs - 1, 0) for v in (lines[1][0], lines[2][0], lines[2][1])]
                early = [jnp.where(row16 == bs - 1, carry[q], turned[q]) for q in range(3)]
                once = lines[1][1:] + [early[0]]
                twice = lines[2][2:] + [early[1], early[2]]
                for j in range(4):
                    gx[s, p, j, :, h] = (lines[0][j] + once[j] + twice[j]).astype(BF)
                return tuple(turned)

            zero = jnp.zeros((bs, LANES), F32)
            lax.fori_loop(0, ctx_n, step, (zero, zero, zero))

        loop(2, grad)

    vocab_row = lax.broadcasted_iota(jnp.int32, (vocab, 2 * block), 0).astype(F32)
    ge_acc[...] = jnp.zeros_like(ge_acc)

    def scatter(i):
        s, p = lax.div(2 * i, ctx_n), lax.rem(2 * i, ctx_n)
        row = jnp.concatenate([ids_in[2 * i, 0:1, :], ids_in[2 * i + 1, 0:1, :]], 1).astype(F32)
        onehot = (vocab_row == row).astype(F32).astype(BF)
        rows = jnp.concatenate([gx[s, p + q, j] for q in range(2) for j in range(4)], 0)
        ge_acc[...] += dot(onehot, rows)

    loop(ctx_n, scatter)
    ge_out[...] = ge_acc[...].astype(BF)
    others(dp_n, dp, lambda to: ge_copy(to).start())
    pltpu.make_async_copy(ge_out.at[chunk(dp, vr)], ge_in.at[dp], ge_recv.at[dp]).start()

    loop(dp_n, lambda i: arrived(gf_in.at[i], gf_recv.at[i]))
    for q in range(2):
        total = gf_in[q].astype(F32)
        for i in range(1, dp_n // 2):
            total = total + gf_in[2 * i + q].astype(F32)
        gf_ref[:, q * cw : (q + 1) * cw] = total
    loop(dp_n, lambda i: arrived(ge_in.at[i], ge_recv.at[i]))
    for q in range(2):
        total = ge_in[q].astype(F32)
        for i in range(1, dp_n // 2):
            total = total + ge_in[2 * i + q].astype(F32)
        ge_ref[:, q * cw : (q + 1) * cw] = total

    def mixed_arrived(i):
        s, p = lax.div(i, ctx_n), lax.rem(i, ctx_n)
        arrived(mixed_hbm.at[0, :, chunk(2 * p + s, cw)], mix_recv.at[i])

    loop(pair_n, mixed_arrived)

    def pair_sent(to):
        ids_copy(to).wait_send()
        cot_copy(to).wait_send()
        mix_copy(to).wait_send()

    def dp_sent(to):
        lf_copy(to).wait_send()
        gf_copy(to).wait_send()
        ge_copy(to).wait_send()

    others(pair_n, pair_me, pair_sent)
    others(dp_n, dp, dp_sent)


def body(token_ids, embedding, short_filter, long_filter, cotangent):
    vocab, width = embedding.shape
    dp_n, ctx_n = lax.axis_size("dp"), lax.axis_size("ctx")
    part = width // ctx_n
    block = token_ids.shape[1]
    length = block * ctx_n
    cw, sub, bs, pair_n = part // 2, length // 4, block // 4, 2 * ctx_n
    lr, vr = length // dp_n, vocab // dp_n
    fwd, inv, perm = tables(length, block)
    ids = jnp.broadcast_to(token_ids.reshape(bs, 4).T.reshape(1, block), (8, block))
    hbm = pl.BlockSpec(memory_space=pl.ANY)
    vmem = pl.BlockSpec(memory_space=pltpu.VMEM)
    dma = pltpu.SemaphoreType.DMA
    return pl.pallas_call(
        functools.partial(kernel, (dp_n, ctx_n, vocab, part, block)),
        out_shape=[
            jax.ShapeDtypeStruct((1, block, width), BF),
            jax.ShapeDtypeStruct((vr, part), F32),
            jax.ShapeDtypeStruct((lr, part), F32),
        ],
        in_specs=[vmem, vmem, hbm, hbm, hbm, hbm, hbm, hbm],
        out_specs=[hbm, vmem, vmem],
        scratch_shapes=[
            pltpu.VMEM((pair_n, 8, block), jnp.int32),
            pltpu.VMEM((vocab, cw), BF),
            pltpu.VMEM((3, 3, cw), F32),
            pltpu.VMEM((dp_n, lr, cw), BF),
            pltpu.VMEM((pair_n, block, cw), BF),
            pltpu.VMEM(fwd.shape, BF),
            pltpu.VMEM(inv.shape, BF),
            pltpu.VMEM((2, 4, sub, cw), F32),
            pltpu.VMEM((2, 4, sub, cw), F32),
            pltpu.VMEM((2, 4, sub, cw), F32),
            pltpu.VMEM((2, 4, sub, cw), F32),
            pltpu.VMEM((2, 4, sub, cw), BF),
            pltpu.VMEM((4, sub, cw), BF),
            pltpu.VMEM((4, 2, sub, cw), F32),
            pltpu.VMEM((2, 4, 2, sub, cw), F32),
            pltpu.VMEM((2, 4, 2 * sub, cw), F32),
            pltpu.VMEM((2, 4, 2 * sub, cw), BF),
            pltpu.VMEM((4, 2 * sub, cw), BF),
            pltpu.VMEM((2, 4, sub, cw), F32),
            pltpu.VMEM((2, 4, sub, cw), F32),
            pltpu.VMEM((2, ctx_n, 4, bs, cw), BF),
            pltpu.VMEM((pair_n, block, cw), BF),
            pltpu.VMEM((dp_n, lr, cw), BF),
            pltpu.VMEM((dp_n, lr, cw), BF),
            pltpu.VMEM((vocab, cw), F32),
            pltpu.VMEM((vocab, cw), BF),
            pltpu.VMEM((dp_n, vr, cw), BF),
            dma((4,)),
            dma((pair_n,)), dma((pair_n,)),
            dma((dp_n,)), dma((dp_n,)),
            dma((pair_n,)), dma((pair_n,)),
            dma((pair_n,)), dma((pair_n,)),
            dma((dp_n,)), dma((dp_n,)),
            dma((dp_n,)), dma((dp_n,)),
        ],
        compiler_params=pltpu.CompilerParams(
            collective_id=0, has_side_effects=True, vmem_limit_bytes=56 * 1024 * 1024
        ),
        name="hyena",
    )(ids, perm, embedding, short_filter, long_filter, cotangent, fwd, inv)


def solution(mesh):
    in_specs = (P("dp", "ctx"), P(), P(), P("dp", "ctx"), P("dp", "ctx", None))
    out_specs = (P("dp", "ctx", None), P("dp", "ctx"), P("dp", "ctx"))
    return jax.shard_map(body, mesh=mesh, in_specs=in_specs, out_specs=out_specs, check_vma=False)
```

time: 183 us -> 69.2 us (0.38)
  Pallas kernels: 0 us -> 60.3 us
  local copies, waits for them, and re-layouts: 54.2 us -> 6.71 us
  waiting for transfers between devices: 26.8 us -> 0 us
  starting transfers between devices: 25.7 us -> 0 us
  other arithmetic: 24.7 us -> 1.32 us
  blocking collectives: 21.5 us -> 0 us
  between operations: 14.8 us -> 0.65 us
  matrix products: 13.8 us -> 0 us
    pallas_call x0 -> x1, Pallas kernels: none -> 60.3 us  [body(): pl.pallas_call(functools.partial(kernel, (dp_n, ctx_n, vocab, part, block...]
    all_to_all x4 -> x0, waiting for transfers between devices: 26.2 us -> none  [the longest x1 12.5 us: body(): term = lax.all_to_all(term, 'dp', split_axis=0, concat_axis=0, tiled=True)]
    all_to_all x4 -> x0, starting transfers between devices: 25.7 us -> none  [the longest x1 11.8 us: body(): lax.all_to_all(table.reshape(dp, vocab // dp, part), 'dp', split_axis=0,...]
    all_gather x1 -> x0, blocking collectives: 21.5 us -> none  [body(): ids = lax.all_gather(token_ids[0], 'ctx', axis=0, tiled=True)]
    unnamed x85 -> x4, local copies, waits for them, and re-layouts: 22.9 us -> 5.84 us
    dot_general x8 -> x0, matrix products: 13.8 us -> none  [the longest x3 4.77 us: inverse(): return jnp.einsum('jnk,jkc->jnc', table, w, preferred_element_type=F32)]
    add x9 -> x0, other arithmetic: 10.7 us -> none  [the longest x1 3.28 us: body(): g_re * z_re + g_im * z_im]
    all_to_all x3 -> x0, local copies, waits for them, and re-layouts: 7.41 us -> none  [the longest x1 6.31 us: body(): lax.all_to_all(split4(cotangent[0]), 'ctx', split_axis=2, concat_axis=1,...]
  transfers between devices with their start and end apart: 5 -> 0, of which waited for: 3 -> 0; matrix products, arithmetic and copies ran while one was open for 26% -> 0% of each run, Pallas kernels for 0% -> 0%
where the time goes in v2:
time: 69.2 us; the launch traced here: 69 us
  Pallas kernels  60.3 us (87%)
  local copies, waits for them, and re-layouts  6.71 us (10%)
  other arithmetic  1.32 us (2%)
    pallas_call x1, Pallas kernels, body(): pl.pallas_call(functools.partial(kernel, (dp_n, ctx_n, vocab, part, block...  60.3 us
    unnamed x4, local copies, waits for them, and re-layouts  5.84 us

profile of v2, /device:TPU:1, one launch (start us, length us, event | category | flops | bytes accessed | tf_op | source)
XLA Modules:
  0.0 69.0 jit_solution(8294381898250914077)
XLA Ops:
  0.6 0.5 broadcast.3
  1.1 1.3 %reduce.3 = s32[128]{0:T(128)S(1)} reduce(s32[1,128]{1,0:T(1,128)} %param.8, s32[]{:T(128)} %broadcast.3), dimensions={0}, to_apply=%param.8.reduce_sub_computation.3 | reduce | bytes 1028 | tf_op args[0]
  2.5 0.1 reshape.11
  2.6 0.1 copy.12
  2.6 0.1 broadcast_in_dim.7
  2.7 0.6 broadcast_in_dim.8.ids_ref
  3.3 60.3 %hyena.1 = (bf16[1,128,4096]{2,1,0:T(8,128)(2,1)}, f32[32,512]{1,0:T(8,128)}, f32[64,512]{1,0:T(8,128)}) custom-call(s32[8,128]{1,0:T(8,128)} %broadcast_in_dim.8.ids_ref, bf16[2,128,128]{2,1,0:T(8,128)(2,1)} %constant.8.clone.perm, bf16[512,4096]{1,0:T(8,128)(2,1)} %emb_hbm.1, f32[3,3,4096]{2,1,0:T(4,128)} %taps_hbm.1, bf16[64,512]{1,0:T(8,128)(2,1)} %lf_hbm.1, ...), custom_call_target="tpu_custom_call" | custom-call | tf_op jit(solution)/shard_map/hyena/pallas_call | solution.py:435
  63.6 2.3 %copy.16 = bf16[1,128,4096]{2,1,0:T(8,128)(2,1)} copy(bf16[1,128,4096]{2,1,0:T(8,128)(2,1)} %get-tuple-element.6) | data formatting | bytes 2097152
  65.9 1.5 %copy.17 = f32[32,512]{1,0:T(8,128)} copy(f32[32,512]{1,0:T(8,128)} %get-tuple-element.7) | data formatting | bytes 131072
  67.4 1.6 %copy.18 = f32[64,512]{1,0:T(8,128)} copy(f32[64,512]{1,0:T(8,128)} %get-tuple-element.8) | data formatting | bytes 262144

commit v3 on v2

--- a/solution.py
+++ b/solution.py
@@ -57,9 +57,9 @@
     dims,
     ids_ref, perm, emb_hbm, taps_hbm, lf_hbm, cot_hbm, fwd_hbm, inv_hbm,
     mixed_hbm, ge_ref, gf_ref,
-    ids_in, emb, taps, lf_in, cot_in, fwd, inv,
+    ids_mine, ids_in, emb, taps, lf_in, cot_in, fwd, inv,
     x, uq, uk, uv, field, hfield, spec_h, spec_z, pbuf, wbuf, wf, conv, gq, gx,
-    mixed_out, gf_out, gf_in, ge_acc, ge_out, ge_in,
+    onehot, lookups, mixed_out, gf_out, gf_in, ge_out, ge_in,
     local_sem, ids_send, ids_recv, lf_send, lf_recv, cot_send, cot_recv,
     mix_send, mix_recv, gf_send, gf_recv, ge_send, ge_recv,
 ):
@@ -91,6 +91,11 @@
     for load in loads:
         load.start()
 
+    ids = jnp.broadcast_to(ids_ref[...].astype(F32), (8, block))
+    high = jnp.where(ids >= 256.0, 1.0, 0.0)
+    low = ids - 256.0 * high
+    ids_mine[...] = dot(low.astype(BF), perm[1]) + 256.0 * dot(high.astype(BF), perm[1])
+
     barrier = pltpu.get_barrier_semaphore()
 
     def greet_pair(i):
@@ -108,7 +113,7 @@
 
     def ids_copy(to):
         return pltpu.make_async_remote_copy(
-            src_ref=ids_ref, dst_ref=ids_in.at[pair_me], send_sem=ids_send.at[to], recv_sem=ids_recv.at[pair_me],
+            src_ref=ids_mine, dst_ref=ids_in.at[pair_me], send_sem=ids_send.at[to], recv_sem=ids_recv.at[pair_me],
             device_id=(2 * g + lax.div(to, ctx_n), lax.rem(to, ctx_n)), device_id_type=MESH,
         )
 
@@ -152,7 +157,7 @@
     def arrived(slot, sem):
         pltpu.make_async_copy(slot, slot, sem).wait()
 
-    pltpu.make_async_copy(ids_ref, ids_in.at[pair_me], ids_recv.at[pair_me]).start()
+    pltpu.make_async_copy(ids_mine, ids_in.at[pair_me], ids_recv.at[pair_me]).start()
     pltpu.make_async_copy(lf_hbm.at[:, chunk(c_me, cw)], lf_in.at[dp], lf_recv.at[dp]).start()
     pltpu.make_async_copy(cot_columns(pair_me), cot_in.at[pair_me], cot_recv.at[pair_me]).start()
     others(pair_n, pair_me, lambda to: ids_copy(to).start())
@@ -163,63 +168,82 @@
     loads[1].wait()
     vocab_lane = lax.broadcasted_iota(jnp.int32, (block, LANES), 1).astype(F32)
 
-    def embed(i):
-        s, p = lax.div(i, ctx_n), lax.rem(i, ctx_n)
-        arrived(ids_in.at[i], ids_recv.at[i])
-        row = ids_in[i, 0:1, :].astype(F32)
-        column = jnp.transpose(jnp.broadcast_to(row, (block, block)))
-        onehot = jnp.concatenate(
-            [(column == vocab_lane + float(q * LANES)).astype(F32).astype(BF) for q in range(vocab // LANES)], 1
-        )
-        rows = dot(onehot, emb[...])
-        for j in range(4):
-            x[s, j, chunk(p, bs), :] = rows[j * bs : (j + 1) * bs]
-
-    loop(pair_n, embed)
+    def phase_lookup():
+        def lookup(i):
+            arrived(ids_in.at[i], ids_recv.at[i])
+            column = jnp.transpose(jnp.broadcast_to(ids_in[i, 0:1, :], (block, block)))
+            for q in range(vocab // LANES):
+                onehot[chunk(i, block), q * LANES : (q + 1) * LANES] = (
+                    (column == vocab_lane + float(q * LANES)).astype(F32).astype(BF)
+                )
+
+        loop(pair_n, lookup)
+
+    def phase_embed():
+        def embed(i):
+            rows = dot(onehot[chunk(i, 4 * block), :], emb[...])
+            for q in range(4):
+                s, p = lax.div(4 * i + q, ctx_n), lax.rem(4 * i + q, ctx_n)
+                for j in range(4):
+                    x[s, j, chunk(p, bs), :] = rows[q * block + j * bs : q * block + (j + 1) * bs]
+
+        loop(pair_n // 4, embed)
+
+    phase_lookup()
+    phase_embed()
 
     row16 = lax.broadcasted_iota(jnp.int32, (bs, LANES), 0)
-    for h in halves:
-        f = [[taps[r, i : i + 1, h] for i in range(3)] for r in range(3)]
-
-        def short(s, h=h, f=f):
-            def step(p, carry):
-                rows = chunk(p, bs)
-                xs = [x[s, j, rows, h] for j in range(4)]
-                turned = [pltpu.roll(xs[2], 1, 0), pltpu.roll(xs[3], 1, 0)]
-                late = [jnp.where(row16 == 0, carry[q], turned[q]) for q in range(2)]
-                line = late + xs
-                us = [
-                    [f[r][0] * line[j + 2] + f[r][1] * line[j + 1] + f[r][2] * line[j] for j in range(4)]
-                    for r in range(3)
-                ]
-                for j in range(4):
-                    uq[s, j, rows, h] = us[0][j]
-                    uk[s, j, rows, h] = us[1][j]
-                    uv[s, j, rows, h] = us[2][j]
-                    field[s, j, rows, h] = (us[1][j] * us[2][j]).astype(BF)
-                return tuple(turned)
-
-            zero = jnp.zeros((bs, LANES), F32)
-            lax.fori_loop(0, ctx_n, step, (zero, zero))
-
-        loop(2, short)
+    def phase_short():
+        for h in halves:
+            f = [[taps[r, i : i + 1, h] for i in range(3)] for r in range(3)]
+
+            def short(s, h=h, f=f):
+                def step(p, carry):
+                    rows = chunk(p, bs)
+                    xs = [x[s, j, rows, h] for j in range(4)]
+                    turned = [pltpu.roll(xs[2], 1, 0), pltpu.roll(xs[3], 1, 0)]
+                    late = [jnp.where(row16 == 0, carry[q], turned[q]) for q in range(2)]
+                    line = late + xs
+                    us = [
+                        [f[r][0] * line[j + 2] + f[r][1] * line[j + 1] + f[r][2] * line[j] for j in range(4)]
+                        for r in range(3)
+                    ]
+                    for j in range(4):
+                        uq[s, j, rows, h] = us[0][j]
+                        uk[s, j, rows, h] = us[1][j]
+                        uv[s, j, rows, h] = us[2][j]
+                        field[s, j, rows, h] = (us[1][j] * us[2][j]).astype(BF)
+                    return tuple(turned)
+
+                zero = jnp.zeros((bs, LANES), F32)
+                lax.fori_loop(0, ctx_n, step, (zero, zero))
+
+            loop(2, short)
+
+    phase_short()
 
     loads[2].wait()
 
-    def gather_taps(i):
-        for q in range(per):
-            arrived(lf_in.at[i * per + q], lf_recv.at[i * per + q])
-        rows = jnp.concatenate([lf_in[i * per + q] for q in range(per)], 0)
-        rows = dot(perm[0], rows).astype(BF)
-        for j in range(4):
-            hfield[j, chunk(i, bs), :] = rows[j * bs : (j + 1) * bs]
-
-    loop(ctx_n, gather_taps)
+    def phase_taps():
+        def gather_taps(i):
+            for q in range(per):
+                arrived(lf_in.at[i * per + q], lf_recv.at[i * per + q])
+            rows = jnp.concatenate([lf_in[i * per + q] for q in range(per)], 0)
+            rows = dot(perm[0], rows).astype(BF)
+            for j in range(4):
+                hfield[j, chunk(i, bs), :] = rows[j * bs : (j + 1) * bs]
+
+        loop(ctx_n, gather_taps)
+
+    phase_taps()
 
     def filter_dft(j):
         pbuf[0, j] = dot(fwd[j], hfield[j])
 
-    loop(4, filter_dft)
+    def phase_filter_dft():
+        loop(4, filter_dft)
+
+    phase_filter_dft()
 
     def butterfly(s, i, h):
         re = [pbuf[s, j, chunk(i, KC), h] for j in range(4)]
@@ -233,7 +257,10 @@
                 spec_h[m, 0, chunk(i, KC), h] = re[m]
                 spec_h[m, 1, chunk(i, KC), h] = im[m]
 
-    loop(sub // KC, filter_mix)
+    def phase_filter_mix():
+        loop(sub // KC, filter_mix)
+
+    phase_filter_mix()
 
     def field_dft(i):
         s, j = lax.div(i, 4), lax.rem(i, 4)
@@ -245,7 +272,10 @@
             ref[j, chunk(i, KC), h] = re[j].astype(BF)
             ref[j, pl.ds(pl.multiple_of(sub + i * KC, KC), KC), h] = im[j].astype(BF)
 
-    loop(8, field_dft)
+    def phase_field_dft():
+        loop(8, field_dft)
+
+    phase_field_dft()
     loads[3].wait()
 
     for s in range(2):
@@ -262,12 +292,18 @@
                     out_im.append(re[m] * h_im + im[m] * h_re)
                 put(wbuf.at[s], i, h, out_re, out_im)
 
-        loop(sub // KC, conv_mix)
+        def phase_conv_mix():
+            loop(sub // KC, conv_mix)
+
+        phase_conv_mix()
 
         def conv_idft(j, s=s):
             conv[s, j] = dot(inv[j], wbuf[s, j]).astype(BF).astype(F32)
 
-        loop(4, conv_idft)
+        def phase_conv_idft():
+            loop(4, conv_idft)
+
+        phase_conv_idft()
 
         def mix(i, s=s):
             p = lax.rem(p_me + 1 + i, ctx_n)
@@ -286,7 +322,18 @@
                     mixed_out.at[to], mixed_hbm.at[0, :, pl.ds(first, cw)], mix_recv.at[pair_me]
                 ).start()
 
-        loop(ctx_n, mix)
+        def phase_mix():
+            loop(ctx_n, mix)
+
+        phase_mix()
+
+    vocab_row = lax.broadcasted_iota(jnp.int32, (vocab, block), 0).astype(F32)
+
+    def phase_lookup_rows():
+        def lookup(i):
+            lookups[:, chunk(i, block)] = (vocab_row == ids_in[i, 0:1, :]).astype(F32).astype(BF)
+
+        loop(pair_n, lookup)
 
     def take(i):
         s, p = lax.div(i, ctx_n), lax.rem(i, ctx_n)
@@ -298,8 +345,12 @@
             field[s, j, rows, :] = (piece * uq[s, j, rows, :]).astype(BF)
             gq[s, j, rows, :] = piece * conv[s, j, rows, :]
 
-    loop(pair_n, take)
-    loop(8, field_dft)
+    def phase_take():
+        loop(pair_n, take)
+
+    phase_lookup_rows()
+    phase_take()
+    phase_field_dft()
 
     def back_mix(i):
         for h in halves:
@@ -322,12 +373,18 @@
                     sum_im = [a + b for a, b in zip(sum_im, f_im)]
             put(wf, i, h, sum_re, sum_im)
 
-    loop(sub // KC, back_mix)
+    def phase_back_mix():
+        loop(sub // KC, back_mix)
+
+    phase_back_mix()
 
     def filter_idft(j):
         hfield[j] = dot(inv[j], wf[j]).astype(BF)
 
-    loop(4, filter_idft)
+    def phase_filter_idft():
+        loop(4, filter_idft)
+
+    phase_filter_idft()
 
     def filter_rows(i):
         rows = jnp.concatenate([hfield[j, chunk(i, bs), :] for j in range(4)], 0)
@@ -335,7 +392,10 @@
         for q in range(per):
             gf_out[i * per + q] = rows[q * lr : (q + 1) * lr]
 
-    loop(ctx_n, filter_rows)
+    def phase_filter_rows():
+        loop(ctx_n, filter_rows)
+
+    phase_filter_rows()
     others(dp_n, dp, lambda to: gf_copy(to).start())
     pltpu.make_async_copy(gf_out.at[dp], gf_in.at[dp], gf_recv.at[dp]).start()
 
@@ -343,46 +403,44 @@
         s, j = lax.div(i, 4), lax.rem(i, 4)
         conv[s, j] = dot(inv[j], wbuf[s, j])
 
-    loop(8, gz_idft)
-
-    for h in halves:
-        f = [[taps[r, i : i + 1, h] for i in range(3)] for r in range(3)]
-
-        def grad(s, h=h, f=f):
-            def step(i, carry):
-                p = ctx_n - 1 - i
-                rows = chunk(p, bs)
-                lines = [[], [], []]
-                for j in range(4):
-                    gz = conv[s, j, rows, h].astype(BF).astype(F32)
-                    gs = [gq[s, j, rows, h], gz * uv[s, j, rows, h], gz * uk[s, j, rows, h]]
-                    for tap in range(3):
-                        lines[tap].append(f[0][tap] * gs[0] + f[1][tap] * gs[1] + f[2][tap] * gs[2])
-                turned = [pltpu.roll(v, bs - 1, 0) for v in (lines[1][0], lines[2][0], lines[2][1])]
-                early = [jnp.where(row16 == bs - 1, carry[q], turned[q]) for q in range(3)]
-                once = lines[1][1:] + [early[0]]
-                twice = lines[2][2:] + [early[1], early[2]]
-                for j in range(4):
-                    gx[s, p, j, :, h] = (lines[0][j] + once[j] + twice[j]).astype(BF)
-                return tuple(turned)
-
-            zero = jnp.zeros((bs, LANES), F32)
-            lax.fori_loop(0, ctx_n, step, (zero, zero, zero))
-
-        loop(2, grad)
-
-    vocab_row = lax.broadcasted_iota(jnp.int32, (vocab, 2 * block), 0).astype(F32)
-    ge_acc[...] = jnp.zeros_like(ge_acc)
-
-    def scatter(i):
-        s, p = lax.div(2 * i, ctx_n), lax.rem(2 * i, ctx_n)
-        row = jnp.concatenate([ids_in[2 * i, 0:1, :], ids_in[2 * i + 1, 0:1, :]], 1).astype(F32)
-        onehot = (vocab_row == row).astype(F32).astype(BF)
-        rows = jnp.concatenate([gx[s, p + q, j] for q in range(2) for j in range(4)], 0)
-        ge_acc[...] += dot(onehot, rows)
-
-    loop(ctx_n, scatter)
-    ge_out[...] = ge_acc[...].astype(BF)
+    def phase_gz_idft():
+        loop(8, gz_idft)
+
+    phase_gz_idft()
+
+    def phase_grad():
+        for h in halves:
+            f = [[taps[r, i : i + 1, h] for i in range(3)] for r in range(3)]
+
+            def grad(s, h=h, f=f):
+                def step(i, carry):
+                    p = ctx_n - 1 - i
+                    rows = chunk(p, bs)
+                    lines = [[], [], []]
+                    for j in range(4):
+                        gz = conv[s, j, rows, h].astype(BF).astype(F32)
+                        gs = [gq[s, j, rows, h], gz * uv[s, j, rows, h], gz * uk[s, j, rows, h]]
+                        for tap in range(3):
+                            lines[tap].append(f[0][tap] * gs[0] + f[1][tap] * gs[1] + f[2][tap] * gs[2])
+                    turned = [pltpu.roll(v, bs - 1, 0) for v in (lines[1][0], lines[2][0], lines[2][1])]
+                    early = [jnp.where(row16 == bs - 1, carry[q], turned[q]) for q in range(3)]
+                    once = lines[1][1:] + [early[0]]
+                    twice = lines[2][2:] + [early[1], early[2]]
+                    for j in range(4):
+                        gx[s, p, j, :, h] = (lines[0][j] + once[j] + twice[j]).astype(BF)
+                    return tuple(turned)
+
+                zero = jnp.zeros((bs, LANES), F32)
+                lax.fori_loop(0, ctx_n, step, (zero, zero, zero))
+
+            loop(2, grad)
+
+    phase_grad()
+
+    def phase_scatter():
+        ge_out[...] = dot(lookups[...], gx[...].reshape(pair_n * block, cw)).astype(BF)
+
+    phase_scatter()
     others(dp_n, dp, lambda to: ge_copy(to).start())
     pltpu.make_async_copy(ge_out.at[chunk(dp, vr)], ge_in.at[dp], ge_recv.at[dp]).start()
 
@@ -419,6 +477,17 @@
     others(dp_n, dp, dp_sent)
 
 
+def collect(mixed_raw, ge_raw, gf_raw, mixed, ge, gf, sem):
+    rows = mixed.shape[1] // 4
+    moves = [(mixed_raw.at[:, pl.ds(i * rows, rows)], mixed.at[:, pl.ds(i * rows, rows)]) for i in range(4)]
+    moves += [(ge_raw, ge), (gf_raw, gf)]
+    moves = [pltpu.make_async_copy(a, b, sem.at[i]) for i, (a, b) in enumerate(moves)]
+    for move in moves:
+        move.start()
+    for move in moves:
+        move.wait()
+
+
 def body(token_ids, embedding, short_filter, long_filter, cotangent):
     vocab, width = embedding.shape
     dp_n, ctx_n = lax.axis_size("dp"), lax.axis_size("ctx")
@@ -428,11 +497,10 @@
     cw, sub, bs, pair_n = part // 2, length // 4, block // 4, 2 * ctx_n
     lr, vr = length // dp_n, vocab // dp_n
     fwd, inv, perm = tables(length, block)
-    ids = jnp.broadcast_to(token_ids.reshape(bs, 4).T.reshape(1, block), (8, block))
     hbm = pl.BlockSpec(memory_space=pl.ANY)
     vmem = pl.BlockSpec(memory_space=pltpu.VMEM)
     dma = pltpu.SemaphoreType.DMA
-    return pl.pallas_call(
+    results = pl.pallas_call(
         functools.partial(kernel, (dp_n, ctx_n, vocab, part, block)),
         out_shape=[
             jax.ShapeDtypeStruct((1, block, width), BF),
@@ -442,7 +510,8 @@
         in_specs=[vmem, vmem, hbm, hbm, hbm, hbm, hbm, hbm],
         out_specs=[hbm, vmem, vmem],
         scratch_shapes=[
-            pltpu.VMEM((pair_n, 8, block), jnp.int32),
+            pltpu.VMEM((8, block), F32),
+            pltpu.VMEM((pair_n, 8, block), F32),
             pltpu.VMEM((vocab, cw), BF),
             pltpu.VMEM((3, 3, cw), F32),
             pltpu.VMEM((dp_n, lr, cw), BF),
@@ -463,10 +532,11 @@
             pltpu.VMEM((2, 4, sub, cw), F32),
             pltpu.VMEM((2, 4, sub, cw), F32),
             pltpu.VMEM((2, ctx_n, 4, bs, cw), BF),
+            pltpu.VMEM((pair_n * block, vocab), BF),
+            pltpu.VMEM((vocab, pair_n * block), BF),
             pltpu.VMEM((pair_n, block, cw), BF),
             pltpu.VMEM((dp_n, lr, cw), BF),
             pltpu.VMEM((dp_n, lr, cw), BF),
-            pltpu.VMEM((vocab, cw), F32),
             pltpu.VMEM((vocab, cw), BF),
             pltpu.VMEM((dp_n, vr, cw), BF),
             dma((4,)),
@@ -481,7 +551,16 @@
             collective_id=0, has_side_effects=True, vmem_limit_bytes=56 * 1024 * 1024
         ),
         name="hyena",
-    )(ids, perm, embedding, short_filter, long_filter, cotangent, fwd, inv)
+    )(token_ids, perm, embedding, short_filter, long_filter, cotangent, fwd, inv)
+    return pl.pallas_call(
+        collect,
+        out_shape=[jax.ShapeDtypeStruct(r.shape, r.dtype) for r in results],
+        in_specs=[hbm] * 3,
+        out_specs=[hbm] * 3,
+        scratch_shapes=[dma((6,))],
+        compiler_params=pltpu.CompilerParams(vmem_limit_bytes=56 * 1024 * 1024),
+        name="collect",
+    )(*results)
 
 
 def solution(mesh):

time: 69.2 us -> 101 us (1.46)
  Pallas kernels: 60.3 us -> 99.8 us
  local copies, waits for them, and re-layouts: 6.71 us -> 0 us
  other arithmetic: 1.32 us -> 0 us
    pallas_call x0 -> x1, Pallas kernels: none -> 38.9 us  [body(): pl.pallas_call(collect, out_shape=[jax.ShapeDtypeStruct(r.shape, r.dtype)...]
    unnamed x4 -> x0, local copies, waits for them, and re-layouts: 5.84 us -> none
    unnamed x1 -> x0, other arithmetic: 1.32 us -> none
where the time goes in v3:
time: 101 us; the launch traced here: 100 us
  Pallas kernels  99.8 us (99%)
    pallas_call x1, Pallas kernels, body(): pl.pallas_call(functools.partial(kernel, (dp_n, ctx_n, vocab, part, block...  60.9 us
    pallas_call x1, Pallas kernels, body(): pl.pallas_call(collect, out_shape=[jax.ShapeDtypeStruct(r.shape, r.dtype)...  38.9 us

profile of v3, /device:TPU:1, one launch (start us, length us, event | category | flops | bytes accessed | tf_op | source)
XLA Modules:
  0.0 100.4 jit_solution(17944775251333904593)
XLA Ops:
  0.6 60.9 %hyena.1 = (bf16[1,128,4096]{2,1,0:T(8,128)(2,1)}, f32[32,512]{1,0:T(8,128)}, f32[64,512]{1,0:T(8,128)}) custom-call(s32[1,128]{1,0:T(1,128)} %ids_ref.1, bf16[2,128,128]{2,1,0:T(8,128)(2,1)} %constant.8.clone.perm, bf16[512,4096]{1,0:T(8,128)(2,1)} %emb_hbm.1, f32[3,3,4096]{2,1,0:T(4,128)} %taps_hbm.1, bf16[64,512]{1,0:T(8,128)(2,1)} %lf_hbm.1, ...), custom_call_target="tpu_custom_call" | custom-call | tf_op jit(solution)/shard_map/hyena/pallas_call | solution.py:503
  61.5 38.9 %collect.1 = (bf16[1,128,4096]{2,1,0:T(8,128)(2,1)}, f32[32,512]{1,0:T(8,128)}, f32[64,512]{1,0:T(8,128)}) custom-call(bf16[1,128,4096]{2,1,0:T(8,128)(2,1)} %get-tuple-element.6.mixed_raw, f32[32,512]{1,0:T(8,128)} %get-tuple-element.7.ge_raw, f32[64,512]{1,0:T(8,128)} %get-tuple-element.8.gf_raw), custom_call_target="tpu_custom_call" | custom-call | tf_op jit(solution)/shard_map/collect/pallas_call | solution.py:555

commit v4 on v3

--- a/solution.py
+++ b/solution.py
@@ -477,15 +477,19 @@
     others(dp_n, dp, dp_sent)
 
 
-def collect(mixed_raw, ge_raw, gf_raw, mixed, ge, gf, sem):
+def collect(mixed_raw, ge_raw, gf_raw, mixed, ge, gf, mixed_vmem, ge_vmem, gf_vmem, in_sem, out_sem):
     rows = mixed.shape[1] // 4
-    moves = [(mixed_raw.at[:, pl.ds(i * rows, rows)], mixed.at[:, pl.ds(i * rows, rows)]) for i in range(4)]
-    moves += [(ge_raw, ge), (gf_raw, gf)]
-    moves = [pltpu.make_async_copy(a, b, sem.at[i]) for i, (a, b) in enumerate(moves)]
-    for move in moves:
-        move.start()
-    for move in moves:
-        move.wait()
+    moves = [[ref.at[:, pl.ds(i * rows, rows)] for ref in (mixed_raw, mixed_vmem, mixed)] for i in range(4)]
+    moves += [[ge_raw, ge_vmem, ge], [gf_raw, gf_vmem, gf]]
+    ins = [pltpu.make_async_copy(a, b, in_sem.at[i]) for i, (a, b, _) in enumerate(moves)]
+    outs = [pltpu.make_async_copy(b, c, out_sem.at[i]) for i, (_, b, c) in enumerate(moves)]
+    for load in ins:
+        load.start()
+    for load, store in zip(ins, outs):
+        load.wait()
+        store.start()
+    for store in outs:
+        store.wait()
 
 
 def body(token_ids, embedding, short_filter, long_filter, cotangent):
@@ -557,7 +561,7 @@
         out_shape=[jax.ShapeDtypeStruct(r.shape, r.dtype) for r in results],
         in_specs=[hbm] * 3,
         out_specs=[hbm] * 3,
-        scratch_shapes=[dma((6,))],
+        scratch_shapes=[pltpu.VMEM(r.shape, r.dtype) for r in results] + [dma((6,)), dma((6,))],
         compiler_params=pltpu.CompilerParams(vmem_limit_bytes=56 * 1024 * 1024),
         name="collect",
     )(*results)

time: 101 us -> 63.8 us (0.63)
  Pallas kernels: 99.8 us -> 63 us
    pallas_call x1, Pallas kernels: 38.9 us -> 2.08 us  [body(): pl.pallas_call(collect, out_shape=[jax.ShapeDtypeStruct(r.shape, r.dtype)...]
where the time goes in v4:
time: 63.8 us; the launch traced here: 63.6 us
  Pallas kernels  63 us (99%)
  between operations  0.64 us (1%)
    pallas_call x1, Pallas kernels, body(): pl.pallas_call(functools.partial(kernel, (dp_n, ctx_n, vocab, part, block...  60.9 us
    pallas_call x1, Pallas kernels, body(): pl.pallas_call(collect, out_shape=[jax.ShapeDtypeStruct(r.shape, r.dtype)...  2.08 us

profile of v4, /device:TPU:1, one launch (start us, length us, event | category | flops | bytes accessed | tf_op | source)
XLA Modules:
  0.0 63.6 jit_solution(17000229494032222831)
XLA Ops:
  0.6 60.9 %hyena.1 = (bf16[1,128,4096]{2,1,0:T(8,128)(2,1)}, f32[32,512]{1,0:T(8,128)}, f32[64,512]{1,0:T(8,128)}) custom-call(s32[1,128]{1,0:T(1,128)} %ids_ref.1, bf16[2,128,128]{2,1,0:T(8,128)(2,1)} %constant.8.clone.perm, bf16[512,4096]{1,0:T(8,128)(2,1)} %emb_hbm.1, f32[3,3,4096]{2,1,0:T(4,128)} %taps_hbm.1, bf16[64,512]{1,0:T(8,128)(2,1)} %lf_hbm.1, ...), custom_call_target="tpu_custom_call" | custom-call | tf_op jit(solution)/shard_map/hyena/pallas_call | solution.py:507
  61.5 2.1 %collect.1 = (bf16[1,128,4096]{2,1,0:T(8,128)(2,1)}, f32[32,512]{1,0:T(8,128)}, f32[64,512]{1,0:T(8,128)}) custom-call(bf16[1,128,4096]{2,1,0:T(8,128)(2,1)} %get-tuple-element.6.mixed_raw, f32[32,512]{1,0:T(8,128)} %get-tuple-element.7.ge_raw, f32[64,512]{1,0:T(8,128)} %get-tuple-element.8.gf_raw), custom_call_target="tpu_custom_call" | custom-call | tf_op jit(solution)/shard_map/collect/pallas_call | solution.py:559

commit v5 on v4

--- a/solution.py
+++ b/solution.py
@@ -41,12 +41,13 @@
     )
 
 
-def loop(count, step):
+def loop(count, step, unroll=1):
     def run(i, carry):
-        step(i)
+        for q in range(unroll):
+            step(i * unroll + q)
         return carry
 
-    lax.fori_loop(0, count, run, 0)
+    lax.fori_loop(0, count // unroll, run, 0)
 
 
 def dot(a, b):
@@ -59,9 +60,8 @@
     mixed_hbm, ge_ref, gf_ref,
     ids_mine, ids_in, emb, taps, lf_in, cot_in, fwd, inv,
     x, uq, uk, uv, field, hfield, spec_h, spec_z, pbuf, wbuf, wf, conv, gq, gx,
-    onehot, lookups, mixed_out, gf_out, gf_in, ge_out, ge_in,
-    local_sem, ids_send, ids_recv, lf_send, lf_recv, cot_send, cot_recv,
-    mix_send, mix_recv, gf_send, gf_recv, ge_send, ge_recv,
+    onehot, lookups, mixed_out, gf_out, gf_in, gf_mid, gf_end, ge_out, ge_in, ge_mid, ge_end,
+    local_sem, ids_send, ids_recv, cot_send, cot_recv, mix_send, mix_recv, quad_send, quad_recv, ring_send, ring_recv,
 ):
     dp_n, ctx_n, vocab, part, block = dims
     cw = part // 2
@@ -75,6 +75,9 @@
     p_me = lax.axis_index("ctx")
     g = lax.div(dp, 2)
     c_me = lax.rem(dp, 2)
+    ring_n = dp_n // 4
+    y_me, z_me = lax.div(g, ring_n), lax.rem(g, ring_n)
+    quad_me = 2 * y_me + c_me
     pair_me = c_me * ctx_n + p_me
     first = pl.multiple_of(p_me * part + c_me * cw, cw)
     halves = [pl.ds(h * LANES, LANES) for h in range(cw // LANES)]
@@ -103,13 +106,24 @@
         device = (2 * g + lax.div(to, ctx_n), lax.rem(to, ctx_n))
         pl.semaphore_signal(barrier, inc=1, device_id=device, device_id_type=MESH)
 
-    def greet_dp(i):
-        device = (lax.rem(dp + 1 + i, dp_n), p_me)
+    def quad_device(to):
+        return ((lax.div(to, 2) * ring_n + z_me) * 2 + lax.rem(to, 2), p_me)
+
+    def ring_device(to):
+        return ((y_me * ring_n + to) * 2 + c_me, p_me)
+
+    def greet_quad(i):
+        device = quad_device(lax.rem(quad_me + 1 + i, 4))
         pl.semaphore_signal(barrier, inc=1, device_id=device, device_id_type=MESH)
 
+    def greet_ring(i):
+        device = ring_device(lax.rem(z_me + 1 + i, ring_n))
+        pl.semaphore_signal(barrier, inc=1, device_id=device, device_id_type=MESH)
+
     loop(pair_n - 1, greet_pair)
-    loop(dp_n - 1, greet_dp)
-    pl.semaphore_wait(barrier, pair_n + dp_n - 2)
+    loop(3, greet_quad)
+    loop(ring_n - 1, greet_ring)
+    pl.semaphore_wait(barrier, pair_n - 1 + 3 + ring_n - 1)
 
     def ids_copy(to):
         return pltpu.make_async_remote_copy(
@@ -117,10 +131,20 @@
             device_id=(2 * g + lax.div(to, ctx_n), lax.rem(to, ctx_n)), device_id_type=MESH,
         )
 
-    def lf_copy(to):
+    def quad_copy(kind, to):
+        src = (lf_hbm.at[:, chunk(lax.rem(to, 2), cw)], gf_mid.at[to], ge_mid.at[to])[kind]
+        dst = (lf_in.at[y_me, z_me, c_me], gf_end.at[quad_me], ge_end.at[quad_me])[kind]
         return pltpu.make_async_remote_copy(
-            src_ref=lf_hbm.at[:, chunk(lax.rem(to, 2), cw)], dst_ref=lf_in.at[dp],
-            send_sem=lf_send.at[to], recv_sem=lf_recv.at[dp], device_id=(to, p_me), device_id_type=MESH,
+            src_ref=src, dst_ref=dst, send_sem=quad_send.at[kind, to], recv_sem=quad_recv.at[kind, quad_me],
+            device_id=quad_device(to), device_id_type=MESH,
+        )
+
+    def ring_copy(kind, to):
+        src = (lf_in.at[:, z_me], gf_out.at[:, to], ge_out.at[:, to])[kind]
+        dst = (lf_in.at[:, z_me], gf_in.at[z_me], ge_in.at[z_me])[kind]
+        return pltpu.make_async_remote_copy(
+            src_ref=src, dst_ref=dst, send_sem=ring_send.at[kind, to], recv_sem=ring_recv.at[kind, z_me],
+            device_id=ring_device(to), device_id_type=MESH,
         )
 
     def cot_columns(to):
@@ -139,18 +163,6 @@
             device_id=(2 * g + lax.div(to, ctx_n), lax.rem(to, ctx_n)), device_id_type=MESH,
         )
 
-    def gf_copy(to):
-        return pltpu.make_async_remote_copy(
-            src_ref=gf_out.at[to], dst_ref=gf_in.at[dp], send_sem=gf_send.at[to], recv_sem=gf_recv.at[dp],
-            device_id=(to, p_me), device_id_type=MESH,
-        )
-
-    def ge_copy(to):
-        return pltpu.make_async_remote_copy(
-            src_ref=ge_out.at[chunk(to, vr)], dst_ref=ge_in.at[dp], send_sem=ge_send.at[to], recv_sem=ge_recv.at[dp],
-            device_id=(to, p_me), device_id_type=MESH,
-        )
-
     def others(count, me, step):
         loop(count - 1, lambda i: step(lax.rem(me + 1 + i, count)))
 
@@ -158,10 +170,12 @@
         pltpu.make_async_copy(slot, slot, sem).wait()
 
     pltpu.make_async_copy(ids_mine, ids_in.at[pair_me], ids_recv.at[pair_me]).start()
-    pltpu.make_async_copy(lf_hbm.at[:, chunk(c_me, cw)], lf_in.at[dp], lf_recv.at[dp]).start()
+    pltpu.make_async_copy(lf_hbm.at[:, chunk(c_me, cw)], lf_in.at[y_me, z_me, c_me], quad_recv.at[0, quad_me]).start()
     pltpu.make_async_copy(cot_columns(pair_me), cot_in.at[pair_me], cot_recv.at[pair_me]).start()
     others(pair_n, pair_me, lambda to: ids_copy(to).start())
-    others(dp_n, dp, lambda to: lf_copy(to).start())
+    others(4, quad_me, lambda to: quad_copy(0, to).start())
+    loop(4, lambda i: arrived(lf_in.at[lax.div(i, 2), z_me, lax.rem(i, 2)], quad_recv.at[0, i]))
+    others(ring_n, z_me, lambda to: ring_copy(0, to).start())
     others(pair_n, pair_me, lambda to: cot_copy(to).start())
 
     loads[0].wait()
@@ -170,14 +184,17 @@
 
     def phase_lookup():
         def lookup(i):
-            arrived(ids_in.at[i], ids_recv.at[i])
-            column = jnp.transpose(jnp.broadcast_to(ids_in[i, 0:1, :], (block, block)))
-            for q in range(vocab // LANES):
-                onehot[chunk(i, block), q * LANES : (q + 1) * LANES] = (
-                    (column == vocab_lane + float(q * LANES)).astype(F32).astype(BF)
-                )
-
-        loop(pair_n, lookup)
+            for k in range(4):
+                arrived(ids_in.at[4 * i + k], ids_recv.at[4 * i + k])
+            rows = [jnp.broadcast_to(ids_in[4 * i + k, 0:1, :], (block, block)) for k in range(4)]
+            columns = [jnp.transpose(row) for row in rows]
+            for k in range(4):
+                for q in range(vocab // LANES):
+                    onehot[chunk(4 * i + k, block), q * LANES : (q + 1) * LANES] = (
+                        (columns[k] == vocab_lane + float(q * LANES)).astype(F32).astype(BF)
+                    )
+
+        loop(pair_n // 4, lookup)
 
     def phase_embed():
         def embed(i):
@@ -226,14 +243,17 @@
 
     def phase_taps():
         def gather_taps(i):
-            for q in range(per):
-                arrived(lf_in.at[i * per + q], lf_recv.at[i * per + q])
-            rows = jnp.concatenate([lf_in[i * per + q] for q in range(per)], 0)
-            rows = dot(perm[0], rows).astype(BF)
-            for j in range(4):
-                hfield[j, chunk(i, bs), :] = rows[j * bs : (j + 1) * bs]
-
-        loop(ctx_n, gather_taps)
+            outs = []
+            for k in range(2):
+                pieces = [(2 * i + k) * per + q for q in range(per)]
+                rows = [lf_in[lax.div(d, 2 * ring_n), lax.rem(lax.div(d, 2), ring_n), lax.rem(d, 2)] for d in pieces]
+                outs.append(dot(perm[0], jnp.concatenate(rows, 0)).astype(BF))
+            for k in range(2):
+                for j in range(4):
+                    hfield[j, chunk(2 * i + k, bs), :] = outs[k][j * bs : (j + 1) * bs]
+
+        others(ring_n, z_me, lambda i: arrived(lf_in.at[:, i], ring_recv.at[0, i]))
+        loop(ctx_n // 2, gather_taps)
 
     phase_taps()
 
@@ -241,7 +261,7 @@
         pbuf[0, j] = dot(fwd[j], hfield[j])
 
     def phase_filter_dft():
-        loop(4, filter_dft)
+        loop(4, filter_dft, 4)
 
     phase_filter_dft()
 
@@ -273,7 +293,7 @@
             ref[j, pl.ds(pl.multiple_of(sub + i * KC, KC), KC), h] = im[j].astype(BF)
 
     def phase_field_dft():
-        loop(8, field_dft)
+        loop(8, field_dft, 4)
 
     phase_field_dft()
     loads[3].wait()
@@ -301,29 +321,33 @@
             conv[s, j] = dot(inv[j], wbuf[s, j]).astype(BF).astype(F32)
 
         def phase_conv_idft():
-            loop(4, conv_idft)
+            loop(4, conv_idft, 4)
 
         phase_conv_idft()
 
         def mix(i, s=s):
-            p = lax.rem(p_me + 1 + i, ctx_n)
-            rows = chunk(p, bs)
-            out = jnp.concatenate([(uq[s, j, rows, :] * conv[s, j, rows, :]).astype(BF) for j in range(4)], 0)
-            to = s * ctx_n + p
-            mixed_out[to] = dot(perm[1], out).astype(BF)
-
-            @pl.when(to != pair_me)
-            def _():
-                mix_copy(to).start()
-
-            @pl.when(to == pair_me)
-            def _():
-                pltpu.make_async_copy(
-                    mixed_out.at[to], mixed_hbm.at[0, :, pl.ds(first, cw)], mix_recv.at[pair_me]
-                ).start()
+            outs = []
+            for k in range(2):
+                p = lax.rem(p_me + 1 + 2 * i + k, ctx_n)
+                rows = chunk(p, bs)
+                out = jnp.concatenate([(uq[s, j, rows, :] * conv[s, j, rows, :]).astype(BF) for j in range(4)], 0)
+                outs.append((s * ctx_n + p, dot(perm[1], out).astype(BF)))
+            for to, out in outs:
+                mixed_out[to] = out
+            for to, _ in outs:
+
+                @pl.when(to != pair_me)
+                def _():
+                    mix_copy(to).start()
+
+                @pl.when(to == pair_me)
+                def _():
+                    pltpu.make_async_copy(
+                        mixed_out.at[to], mixed_hbm.at[0, :, pl.ds(first, cw)], mix_recv.at[pair_me]
+                    ).start()
 
         def phase_mix():
-            loop(ctx_n, mix)
+            loop(ctx_n // 2, mix)
 
         phase_mix()
 
@@ -336,17 +360,19 @@
         loop(pair_n, lookup)
 
     def take(i):
-        s, p = lax.div(i, ctx_n), lax.rem(i, ctx_n)
-        arrived(cot_in.at[i], cot_recv.at[i])
-        out = dot(perm[0], cot_in[i])
-        rows = chunk(p, bs)
-        for j in range(4):
-            piece = out[j * bs : (j + 1) * bs]
-            field[s, j, rows, :] = (piece * uq[s, j, rows, :]).astype(BF)
-            gq[s, j, rows, :] = piece * conv[s, j, rows, :]
+        for k in range(4):
+            arrived(cot_in.at[4 * i + k], cot_recv.at[4 * i + k])
+        outs = [dot(perm[0], cot_in[4 * i + k]) for k in range(4)]
+        for k in range(4):
+            s, p = lax.div(4 * i + k, ctx_n), lax.rem(4 * i + k, ctx_n)
+            rows = chunk(p, bs)
+            for j in range(4):
+                piece = outs[k][j * bs : (j + 1) * bs]
+                field[s, j, rows, :] = (piece * uq[s, j, rows, :]).astype(BF)
+                gq[s, j, rows, :] = piece * conv[s, j, rows, :]
 
     def phase_take():
-        loop(pair_n, take)
+        loop(pair_n // 4, take)
 
     phase_lookup_rows()
     phase_take()
@@ -382,29 +408,47 @@
         hfield[j] = dot(inv[j], wf[j]).astype(BF)
 
     def phase_filter_idft():
-        loop(4, filter_idft)
+        loop(4, filter_idft, 4)
 
     phase_filter_idft()
 
     def filter_rows(i):
-        rows = jnp.concatenate([hfield[j, chunk(i, bs), :] for j in range(4)], 0)
-        rows = dot(perm[1], rows).astype(BF)
-        for q in range(per):
-            gf_out[i * per + q] = rows[q * lr : (q + 1) * lr]
+        outs = []
+        for k in range(2):
+            rows = jnp.concatenate([hfield[j, chunk(2 * i + k, bs), :] for j in range(4)], 0)
+            outs.append(dot(perm[1], rows).astype(BF))
+        for k in range(2):
+            for q in range(per):
+                d = (2 * i + k) * per + q
+                gf_out[lax.div(d, 2 * ring_n), lax.rem(lax.div(d, 2), ring_n), lax.rem(d, 2)] = outs[k][q * lr : (q + 1) * lr]
 
     def phase_filter_rows():
-        loop(ctx_n, filter_rows)
+        loop(ctx_n // 2, filter_rows)
 
     phase_filter_rows()
-    others(dp_n, dp, lambda to: gf_copy(to).start())
-    pltpu.make_async_copy(gf_out.at[dp], gf_in.at[dp], gf_recv.at[dp]).start()
+    others(ring_n, z_me, lambda to: ring_copy(1, to).start())
+
+    def ring_sum(kind, out, arrivals, mid, end):
+        others(ring_n, z_me, lambda i: arrived(arrivals.at[i], ring_recv.at[kind, i]))
+        for q in range(4):
+            total = out[q // 2, z_me, q % 2].astype(F32)
+            for i in range(1, ring_n):
+                total = total + arrivals[lax.rem(z_me + i, ring_n), q // 2, q % 2].astype(F32)
+            mid[q] = total.astype(BF)
+        end[quad_me] = mid[quad_me]
+        others(4, quad_me, lambda to: quad_copy(kind, to).start())
+
+    def quad_sum(kind, end, result):
+        others(4, quad_me, lambda i: arrived(end.at[i], quad_recv.at[kind, i]))
+        for c in range(2):
+            result[:, c * cw : (c + 1) * cw] = end[c].astype(F32) + end[2 + c].astype(F32)
 
     def gz_idft(i):
         s, j = lax.div(i, 4), lax.rem(i, 4)
         conv[s, j] = dot(inv[j], wbuf[s, j])
 
     def phase_gz_idft():
-        loop(8, gz_idft)
+        loop(8, gz_idft, 4)
 
     phase_gz_idft()
 
@@ -437,25 +481,17 @@
 
     phase_grad()
 
+    ring_sum(1, gf_out, gf_in, gf_mid, gf_end)
+
     def phase_scatter():
-        ge_out[...] = dot(lookups[...], gx[...].reshape(pair_n * block, cw)).astype(BF)
+        ge_out[...] = dot(lookups[...], gx[...].reshape(pair_n * block, cw)).astype(BF).reshape(ge_out.shape)
 
     phase_scatter()
-    others(dp_n, dp, lambda to: ge_copy(to).start())
-    pltpu.make_async_copy(ge_out.at[chunk(dp, vr)], ge_in.at[dp], ge_recv.at[dp]).start()
-
-    loop(dp_n, lambda i: arrived(gf_in.at[i], gf_recv.at[i]))
-    for q in range(2):
-        total = gf_in[q].astype(F32)
-        for i in range(1, dp_n // 2):
-            total = total + gf_in[2 * i + q].astype(F32)
-        gf_ref[:, q * cw : (q + 1) * cw] = total
-    loop(dp_n, lambda i: arrived(ge_in.at[i], ge_recv.at[i]))
-    for q in range(2):
-        total = ge_in[q].astype(F32)
-        for i in range(1, dp_n // 2):
-            total = total + ge_in[2 * i + q].astype(F32)
-        ge_ref[:, q * cw : (q + 1) * cw] = total
+    others(ring_n, z_me, lambda to: ring_copy(2, to).start())
+
+    quad_sum(1, gf_end, gf_ref)
+    ring_sum(2, ge_out, ge_in, ge_mid, ge_end)
+    quad_sum(2, ge_end, ge_ref)
 
     def mixed_arrived(i):
         s, p = lax.div(i, ctx_n), lax.rem(i, ctx_n)
@@ -468,13 +504,17 @@
         cot_copy(to).wait_send()
         mix_copy(to).wait_send()
 
-    def dp_sent(to):
-        lf_copy(to).wait_send()
-        gf_copy(to).wait_send()
-        ge_copy(to).wait_send()
+    def quad_sent(to):
+        for kind in range(3):
+            quad_copy(kind, to).wait_send()
+
+    def ring_sent(to):
+        for kind in range(3):
+            ring_copy(kind, to).wait_send()
 
     others(pair_n, pair_me, pair_sent)
-    others(dp_n, dp, dp_sent)
+    others(4, quad_me, quad_sent)
+    others(ring_n, z_me, ring_sent)
 
 
 def collect(mixed_raw, ge_raw, gf_raw, mixed, ge, gf, mixed_vmem, ge_vmem, gf_vmem, in_sem, out_sem):
@@ -499,7 +539,7 @@
     block = token_ids.shape[1]
     length = block * ctx_n
     cw, sub, bs, pair_n = part // 2, length // 4, block // 4, 2 * ctx_n
-    lr, vr = length // dp_n, vocab // dp_n
+    lr, vr, ring_n = length // dp_n, vocab // dp_n, dp_n // 4
     fwd, inv, perm = tables(length, block)
     hbm = pl.BlockSpec(memory_space=pl.ANY)
     vmem = pl.BlockSpec(memory_space=pltpu.VMEM)
@@ -518,7 +558,7 @@
             pltpu.VMEM((pair_n, 8, block), F32),
             pltpu.VMEM((vocab, cw), BF),
             pltpu.VMEM((3, 3, cw), F32),
-            pltpu.VMEM((dp_n, lr, cw), BF),
+            pltpu.VMEM((2, ring_n, 2, lr, cw), BF),
             pltpu.VMEM((pair_n, block, cw), BF),
             pltpu.VMEM(fwd.shape, BF),
             pltpu.VMEM(inv.shape, BF),
@@ -539,17 +579,20 @@
             pltpu.VMEM((pair_n * block, vocab), BF),
             pltpu.VMEM((vocab, pair_n * block), BF),
             pltpu.VMEM((pair_n, block, cw), BF),
-            pltpu.VMEM((dp_n, lr, cw), BF),
-            pltpu.VMEM((dp_n, lr, cw), BF),
-            pltpu.VMEM((vocab, cw), BF),
-            pltpu.VMEM((dp_n, vr, cw), BF),
+            pltpu.VMEM((2, ring_n, 2, lr, cw), BF),
+            pltpu.VMEM((ring_n, 2, 2, lr, cw), BF),
+            pltpu.VMEM((4, lr, cw), BF),
+            pltpu.VMEM((4, lr, cw), BF),
+            pltpu.VMEM((2, ring_n, 2, vr, cw), BF),
+            pltpu.VMEM((ring_n, 2, 2, vr, cw), BF),
+            pltpu.VMEM((4, vr, cw), BF),
+            pltpu.VMEM((4, vr, cw), BF),
             dma((4,)),
             dma((pair_n,)), dma((pair_n,)),
-            dma((dp_n,)), dma((dp_n,)),
             dma((pair_n,)), dma((pair_n,)),
             dma((pair_n,)), dma((pair_n,)),
-            dma((dp_n,)), dma((dp_n,)),
-            dma((dp_n,)), dma((dp_n,)),
+            dma((3, 4)), dma((3, 4)),
+            dma((3, ring_n)), dma((3, ring_n)),
         ],
         compiler_params=pltpu.CompilerParams(
             collective_id=0, has_side_effects=True, vmem_limit_bytes=56 * 1024 * 1024

time: 63.8 us -> 56.6 us (0.89)
  Pallas kernels: 63 us -> 55.8 us
    pallas_call x1, Pallas kernels: 60.9 us -> 53.7 us  [body(): pl.pallas_call(functools.partial(kernel, (dp_n, ctx_n, vocab, part, block...]
where the time goes in v5:
time: 56.6 us; the launch traced here: 56.4 us
  Pallas kernels  55.8 us (99%)
  between operations  0.64 us (1%)
    pallas_call x1, Pallas kernels, body(): pl.pallas_call(functools.partial(kernel, (dp_n, ctx_n, vocab, part, block...  53.7 us
    pallas_call x1, Pallas kernels, body(): pl.pallas_call(collect, out_shape=[jax.ShapeDtypeStruct(r.shape, r.dtype)...  2.08 us

profile of v5, /device:TPU:1, one launch (start us, length us, event | category | flops | bytes accessed | tf_op | source)
XLA Modules:
  0.0 56.4 jit_solution(10346651832358830934)
XLA Ops:
  0.6 53.7 %hyena.1 = (bf16[1,128,4096]{2,1,0:T(8,128)(2,1)}, f32[32,512]{1,0:T(8,128)}, f32[64,512]{1,0:T(8,128)}) custom-call(s32[1,128]{1,0:T(1,128)} %ids_ref.1, bf16[2,128,128]{2,1,0:T(8,128)(2,1)} %constant.8.clone.perm, bf16[512,4096]{1,0:T(8,128)(2,1)} %emb_hbm.1, f32[3,3,4096]{2,1,0:T(4,128)} %taps_hbm.1, bf16[64,512]{1,0:T(8,128)(2,1)} %lf_hbm.1, ...), custom_call_target="tpu_custom_call" | custom-call | tf_op jit(solution)/shard_map/hyena/pallas_call | solution.py:547
  54.3 2.1 %collect.1 = (bf16[1,128,4096]{2,1,0:T(8,128)(2,1)}, f32[32,512]{1,0:T(8,128)}, f32[64,512]{1,0:T(8,128)}) custom-call(bf16[1,128,4096]{2,1,0:T(8,128)(2,1)} %get-tuple-element.6.mixed_raw, f32[32,512]{1,0:T(8,128)} %get-tuple-element.7.ge_raw, f32[64,512]{1,0:T(8,128)} %get-tuple-element.8.gf_raw), custom_call_target="tpu_custom_call" | custom-call | tf_op jit(solution)/shard_map/collect/pallas_call | solution.py:602

commit v6 on v5

--- a/solution.py
+++ b/solution.py
@@ -16,18 +16,14 @@
 KC = 16
 
 
-def tables(length, block):
+def tables(length):
     sub = length // 4
     k = np.arange(sub)[None, :, None]
     t = 4 * np.arange(sub)[None, None, :] + np.arange(4)[:, None, None]
     angle = 2.0 * math.pi * (((4 * k + 1) * t) % (4 * length)) / (4 * length)
     fwd = np.concatenate([np.cos(angle), -np.sin(angle)], 1)
     inv = fwd.transpose(0, 2, 1) / length
-    out = np.arange(block)
-    perm = np.zeros((2, block, block))
-    perm[0, out, 4 * (out % (block // 4)) + out // (block // 4)] = 1.0
-    perm[1] = perm[0].T
-    return jnp.asarray(fwd, BF), jnp.asarray(inv, BF), jnp.asarray(perm, BF)
+    return jnp.asarray(fwd, BF), jnp.asarray(inv, BF)
 
 
 def radix4(re, im, sign):
@@ -56,12 +52,13 @@
 
 def kernel(
     dims,
-    ids_ref, perm, emb_hbm, taps_hbm, lf_hbm, cot_hbm, fwd_hbm, inv_hbm,
+    ids_hbm, emb_hbm, taps_hbm, lf_hbm, cot_hbm, fwd_hbm, inv_hbm,
     mixed_hbm, ge_ref, gf_ref,
-    ids_mine, ids_in, emb, taps, lf_in, cot_in, fwd, inv,
-    x, uq, uk, uv, field, hfield, spec_h, spec_z, pbuf, wbuf, wf, conv, gq, gx,
-    onehot, lookups, mixed_out, gf_out, gf_in, gf_mid, gf_end, ge_out, ge_in, ge_mid, ge_end,
+    ids_raw, ids_mine, ids_in, perm, emb, taps, lf_in, cot_in, fwd, inv,
+    x, uq, uk, uv, field, hfield, spec_h, spec_z, hbuf, pbuf, wbuf, wf, conv, gq, gx,
+    onehot, lookups, mixed_out, gf_out, gf_in, gf_mid, gf_end, ge_out, ge_in,
     local_sem, ids_send, ids_recv, cot_send, cot_recv, mix_send, mix_recv, quad_send, quad_recv, ring_send, ring_recv,
+    ge_send, ge_recv,
 ):
     dp_n, ctx_n, vocab, part, block = dims
     cw = part // 2
@@ -91,13 +88,10 @@
         pltpu.make_async_copy(fwd_hbm, fwd, local_sem.at[2]),
         pltpu.make_async_copy(inv_hbm, inv, local_sem.at[3]),
     ]
+    load_ids = pltpu.make_async_copy(ids_hbm, ids_raw, local_sem.at[4])
+    load_ids.start()
     for load in loads:
         load.start()
-
-    ids = jnp.broadcast_to(ids_ref[...].astype(F32), (8, block))
-    high = jnp.where(ids >= 256.0, 1.0, 0.0)
-    low = ids - 256.0 * high
-    ids_mine[...] = dot(low.astype(BF), perm[1]) + 256.0 * dot(high.astype(BF), perm[1])
 
     barrier = pltpu.get_barrier_semaphore()
 
@@ -112,18 +106,25 @@
     def ring_device(to):
         return ((y_me * ring_n + to) * 2 + c_me, p_me)
 
-    def greet_quad(i):
-        device = quad_device(lax.rem(quad_me + 1 + i, 4))
+    def greet_dp(i):
+        device = (lax.rem(dp + 1 + i, dp_n), p_me)
         pl.semaphore_signal(barrier, inc=1, device_id=device, device_id_type=MESH)
 
-    def greet_ring(i):
-        device = ring_device(lax.rem(z_me + 1 + i, ring_n))
-        pl.semaphore_signal(barrier, inc=1, device_id=device, device_id_type=MESH)
-
     loop(pair_n - 1, greet_pair)
-    loop(3, greet_quad)
-    loop(ring_n - 1, greet_ring)
-    pl.semaphore_wait(barrier, pair_n - 1 + 3 + ring_n - 1)
+    loop(dp_n - 1, greet_dp)
+    def natural(axis):
+        place = lax.broadcasted_iota(jnp.int32, (block, block), axis)
+        return 4 * lax.rem(place, bs) + lax.div(place, bs)
+
+    perm[0] = (natural(0) == lax.broadcasted_iota(jnp.int32, (block, block), 1)).astype(F32).astype(BF)
+    perm[1] = (natural(1) == lax.broadcasted_iota(jnp.int32, (block, block), 0)).astype(F32).astype(BF)
+
+    load_ids.wait()
+    ids = jnp.broadcast_to(ids_raw[...].astype(F32), (8, block))
+    high = jnp.where(ids >= 256.0, 1.0, 0.0)
+    low = ids - 256.0 * high
+    ids_mine[...] = dot(low.astype(BF), perm[1]) + 256.0 * dot(high.astype(BF), perm[1])
+    pl.semaphore_wait(barrier, pair_n - 1 + dp_n - 1)
 
     def ids_copy(to):
         return pltpu.make_async_remote_copy(
@@ -132,16 +133,16 @@
         )
 
     def quad_copy(kind, to):
-        src = (lf_hbm.at[:, chunk(lax.rem(to, 2), cw)], gf_mid.at[to], ge_mid.at[to])[kind]
-        dst = (lf_in.at[y_me, z_me, c_me], gf_end.at[quad_me], ge_end.at[quad_me])[kind]
+        src = (lf_hbm.at[:, chunk(lax.rem(to, 2), cw)], gf_mid.at[to])[kind]
+        dst = (lf_in.at[y_me, z_me, c_me], gf_end.at[quad_me])[kind]
         return pltpu.make_async_remote_copy(
             src_ref=src, dst_ref=dst, send_sem=quad_send.at[kind, to], recv_sem=quad_recv.at[kind, quad_me],
             device_id=quad_device(to), device_id_type=MESH,
         )
 
     def ring_copy(kind, to):
-        src = (lf_in.at[:, z_me], gf_out.at[:, to], ge_out.at[:, to])[kind]
-        dst = (lf_in.at[:, z_me], gf_in.at[z_me], ge_in.at[z_me])[kind]
+        src = (lf_in.at[:, z_me], gf_out.at[:, to])[kind]
+        dst = (lf_in.at[:, z_me], gf_in.at[z_me])[kind]
         return pltpu.make_async_remote_copy(
             src_ref=src, dst_ref=dst, send_sem=ring_send.at[kind, to], recv_sem=ring_recv.at[kind, z_me],
             device_id=ring_device(to), device_id_type=MESH,
@@ -163,6 +164,12 @@
             device_id=(2 * g + lax.div(to, ctx_n), lax.rem(to, ctx_n)), device_id_type=MESH,
         )
 
+    def ge_copy(to):
+        return pltpu.make_async_remote_copy(
+            src_ref=ge_out.at[to], dst_ref=ge_in.at[dp], send_sem=ge_send.at[to], recv_sem=ge_recv.at[dp],
+            device_id=(to, p_me), device_id_type=MESH,
+        )
+
     def others(count, me, step):
         loop(count - 1, lambda i: step(lax.rem(me + 1 + i, count)))
 
@@ -172,8 +179,8 @@
     pltpu.make_async_copy(ids_mine, ids_in.at[pair_me], ids_recv.at[pair_me]).start()
     pltpu.make_async_copy(lf_hbm.at[:, chunk(c_me, cw)], lf_in.at[y_me, z_me, c_me], quad_recv.at[0, quad_me]).start()
     pltpu.make_async_copy(cot_columns(pair_me), cot_in.at[pair_me], cot_recv.at[pair_me]).start()
+    others(4, quad_me, lambda to: quad_copy(0, to).start())
     others(pair_n, pair_me, lambda to: ids_copy(to).start())
-    others(4, quad_me, lambda to: quad_copy(0, to).start())
     loop(4, lambda i: arrived(lf_in.at[lax.div(i, 2), z_me, lax.rem(i, 2)], quad_recv.at[0, i]))
     others(ring_n, z_me, lambda to: ring_copy(0, to).start())
     others(pair_n, pair_me, lambda to: cot_copy(to).start())
@@ -241,6 +248,26 @@
 
     loads[2].wait()
 
+    def field_dft(i):
+        s, j = lax.div(i, 4), lax.rem(i, 4)
+        pbuf[s, j] = dot(fwd[j], field[s, j])
+
+    def phase_field_dft():
+        loop(8, field_dft, 4)
+
+    phase_field_dft()
+
+    vocab_row = lax.broadcasted_iota(jnp.int32, (vocab, block), 0).astype(F32)
+
+    def phase_lookup_rows():
+        def lookup(i):
+            lookups[:, chunk(i, block)] = (vocab_row == ids_in[i, 0:1, :]).astype(F32).astype(BF)
+
+        loop(pair_n, lookup)
+
+    phase_lookup_rows()
+
+
     def phase_taps():
         def gather_taps(i):
             outs = []
@@ -258,21 +285,21 @@
     phase_taps()
 
     def filter_dft(j):
-        pbuf[0, j] = dot(fwd[j], hfield[j])
+        hbuf[j] = dot(fwd[j], hfield[j])
 
     def phase_filter_dft():
         loop(4, filter_dft, 4)
 
     phase_filter_dft()
 
-    def butterfly(s, i, h):
-        re = [pbuf[s, j, chunk(i, KC), h] for j in range(4)]
-        im = [pbuf[s, j, pl.ds(pl.multiple_of(sub + i * KC, KC), KC), h] for j in range(4)]
+    def butterfly(ref, i, h):
+        re = [ref[j, chunk(i, KC), h] for j in range(4)]
+        im = [ref[j, pl.ds(pl.multiple_of(sub + i * KC, KC), KC), h] for j in range(4)]
         return radix4(re, im, -1)
 
     def filter_mix(i):
         for h in halves:
-            re, im = butterfly(0, i, h)
+            re, im = butterfly(hbuf, i, h)
             for m in range(4):
                 spec_h[m, 0, chunk(i, KC), h] = re[m]
                 spec_h[m, 1, chunk(i, KC), h] = im[m]
@@ -281,10 +308,6 @@
         loop(sub // KC, filter_mix)
 
     phase_filter_mix()
-
-    def field_dft(i):
-        s, j = lax.div(i, 4), lax.rem(i, 4)
-        pbuf[s, j] = dot(fwd[j], field[s, j])
 
     def put(ref, i, h, re, im):
         re, im = radix4(re, im, 1)
@@ -292,17 +315,14 @@
             ref[j, chunk(i, KC), h] = re[j].astype(BF)
             ref[j, pl.ds(pl.multiple_of(sub + i * KC, KC), KC), h] = im[j].astype(BF)
 
-    def phase_field_dft():
-        loop(8, field_dft, 4)
-
-    phase_field_dft()
+
     loads[3].wait()
 
     for s in range(2):
 
         def conv_mix(i, s=s):
             for h in halves:
-                re, im = butterfly(s, i, h)
+                re, im = butterfly(pbuf.at[s], i, h)
                 out_re, out_im = [], []
                 for m in range(4):
                     spec_z[s, m, 0, chunk(i, KC), h] = re[m]
@@ -350,14 +370,6 @@
             loop(ctx_n // 2, mix)
 
         phase_mix()
-
-    vocab_row = lax.broadcasted_iota(jnp.int32, (vocab, block), 0).astype(F32)
-
-    def phase_lookup_rows():
-        def lookup(i):
-            lookups[:, chunk(i, block)] = (vocab_row == ids_in[i, 0:1, :]).astype(F32).astype(BF)
-
-        loop(pair_n, lookup)
 
     def take(i):
         for k in range(4):
@@ -374,7 +386,6 @@
     def phase_take():
         loop(pair_n // 4, take)
 
-    phase_lookup_rows()
     phase_take()
     phase_field_dft()
 
@@ -382,7 +393,7 @@
         for h in halves:
             sum_re, sum_im = None, None
             for s in range(2):
-                re, im = butterfly(s, i, h)
+                re, im = butterfly(pbuf.at[s], i, h)
                 out_re, out_im, f_re, f_im = [], [], [], []
                 for m in range(4):
                     h_re, h_im = spec_h[m, 0, chunk(i, KC), h], spec_h[m, 1, chunk(i, KC), h]
@@ -481,17 +492,21 @@
 
     phase_grad()
 
-    ring_sum(1, gf_out, gf_in, gf_mid, gf_end)
-
     def phase_scatter():
         ge_out[...] = dot(lookups[...], gx[...].reshape(pair_n * block, cw)).astype(BF).reshape(ge_out.shape)
 
     phase_scatter()
-    others(ring_n, z_me, lambda to: ring_copy(2, to).start())
-
+    others(dp_n, dp, lambda to: ge_copy(to).start())
+
+    ring_sum(1, gf_out, gf_in, gf_mid, gf_end)
     quad_sum(1, gf_end, gf_ref)
-    ring_sum(2, ge_out, ge_in, ge_mid, ge_end)
-    quad_sum(2, ge_end, ge_ref)
+    others(dp_n, dp, lambda i: arrived(ge_in.at[i], ge_recv.at[i]))
+    ge_in[dp] = ge_out[dp]
+    for c in range(2):
+        total = ge_in[c].astype(F32)
+        for i in range(1, dp_n // 2):
+            total = total + ge_in[2 * i + c].astype(F32)
+        ge_ref[:, c * cw : (c + 1) * cw] = total
 
     def mixed_arrived(i):
         s, p = lax.div(i, ctx_n), lax.rem(i, ctx_n)
@@ -505,15 +520,16 @@
         mix_copy(to).wait_send()
 
     def quad_sent(to):
-        for kind in range(3):
+        for kind in range(2):
             quad_copy(kind, to).wait_send()
 
     def ring_sent(to):
-        for kind in range(3):
+        for kind in range(2):
             ring_copy(kind, to).wait_send()
 
     others(pair_n, pair_me, pair_sent)
     others(4, quad_me, quad_sent)
+    others(dp_n, dp, lambda to: ge_copy(to).wait_send())
     others(ring_n, z_me, ring_sent)
 
 
@@ -540,7 +556,7 @@
     length = block * ctx_n
     cw, sub, bs, pair_n = part // 2, length // 4, block // 4, 2 * ctx_n
     lr, vr, ring_n = length // dp_n, vocab // dp_n, dp_n // 4
-    fwd, inv, perm = tables(length, block)
+    fwd, inv = tables(length)
     hbm = pl.BlockSpec(memory_space=pl.ANY)
     vmem = pl.BlockSpec(memory_space=pltpu.VMEM)
     dma = pltpu.SemaphoreType.DMA
@@ -551,11 +567,13 @@
             jax.ShapeDtypeStruct((vr, part), F32),
             jax.ShapeDtypeStruct((lr, part), F32),
         ],
-        in_specs=[vmem, vmem, hbm, hbm, hbm, hbm, hbm, hbm],
+        in_specs=[hbm, hbm, hbm, hbm, hbm, hbm, hbm],
         out_specs=[hbm, vmem, vmem],
         scratch_shapes=[
+            pltpu.VMEM((1, block), jnp.int32),
             pltpu.VMEM((8, block), F32),
             pltpu.VMEM((pair_n, 8, block), F32),
+            pltpu.VMEM((2, block, block), BF),
             pltpu.VMEM((vocab, cw), BF),
             pltpu.VMEM((3, 3, cw), F32),
             pltpu.VMEM((2, ring_n, 2, lr, cw), BF),
@@ -570,6 +588,7 @@
             pltpu.VMEM((4, sub, cw), BF),
             pltpu.VMEM((4, 2, sub, cw), F32),
             pltpu.VMEM((2, 4, 2, sub, cw), F32),
+            pltpu.VMEM((4, 2 * sub, cw), F32),
             pltpu.VMEM((2, 4, 2 * sub, cw), F32),
             pltpu.VMEM((2, 4, 2 * sub, cw), BF),
             pltpu.VMEM((4, 2 * sub, cw), BF),
@@ -583,22 +602,21 @@
             pltpu.VMEM((ring_n, 2, 2, lr, cw), BF),
             pltpu.VMEM((4, lr, cw), BF),
             pltpu.VMEM((4, lr, cw), BF),
-            pltpu.VMEM((2, ring_n, 2, vr, cw), BF),
-            pltpu.VMEM((ring_n, 2, 2, vr, cw), BF),
-            pltpu.VMEM((4, vr, cw), BF),
-            pltpu.VMEM((4, vr, cw), BF),
-            dma((4,)),
+            pltpu.VMEM((dp_n, vr, cw), BF),
+            pltpu.VMEM((dp_n, vr, cw), BF),
+            dma((5,)),
             dma((pair_n,)), dma((pair_n,)),
             dma((pair_n,)), dma((pair_n,)),
             dma((pair_n,)), dma((pair_n,)),
-            dma((3, 4)), dma((3, 4)),
-            dma((3, ring_n)), dma((3, ring_n)),
+            dma((2, 4)), dma((2, 4)),
+            dma((2, ring_n)), dma((2, ring_n)),
+            dma((dp_n,)), dma((dp_n,)),
         ],
         compiler_params=pltpu.CompilerParams(
             collective_id=0, has_side_effects=True, vmem_limit_bytes=56 * 1024 * 1024
         ),
         name="hyena",
-    )(token_ids, perm, embedding, short_filter, long_filter, cotangent, fwd, inv)
+    )(token_ids, embedding, short_filter, long_filter, cotangent, fwd, inv)
     return pl.pallas_call(
         collect,
         out_shape=[jax.ShapeDtypeStruct(r.shape, r.dtype) for r in results],

time: 56.6 us -> 52.8 us (0.933)
  Pallas kernels: 55.8 us -> 52 us
    pallas_call x1, Pallas kernels: 53.7 us -> 49.9 us  [body(): pl.pallas_call(functools.partial(kernel, (dp_n, ctx_n, vocab, part, block...]
where the time goes in v6:
time: 52.8 us; the launch traced here: 52.6 us
  Pallas kernels  52 us (98%)
  between operations  0.64 us (1%)
    pallas_call x1, Pallas kernels, body(): pl.pallas_call(functools.partial(kernel, (dp_n, ctx_n, vocab, part, block...  49.9 us
    pallas_call x1, Pallas kernels, body(): pl.pallas_call(collect, out_shape=[jax.ShapeDtypeStruct(r.shape, r.dtype)...  2.08 us

profile of v6, /device:TPU:1, one launch (start us, length us, event | category | flops | bytes accessed | tf_op | source)
XLA Modules:
  0.0 52.6 jit_solution(13361940401567983723)
XLA Ops:
  0.6 49.9 %hyena.1 = (bf16[1,128,4096]{2,1,0:T(8,128)(2,1)}, f32[32,512]{1,0:T(8,128)}, f32[64,512]{1,0:T(8,128)}) custom-call(s32[1,128]{1,0:T(1,128)} %ids_hbm.1, bf16[512,4096]{1,0:T(8,128)(2,1)} %emb_hbm.1, f32[3,3,4096]{2,1,0:T(4,128)} %taps_hbm.1, bf16[64,512]{1,0:T(8,128)(2,1)} %lf_hbm.1, bf16[1,128,4096]{2,1,0:T(8,128)(2,1)} %cot_hbm.1, ...), custom_call_target="tpu_custom_call" | custom-call | tf_op jit(solution)/shard_map/hyena/pallas_call | solution.py:563
  50.5 2.1 %collect.1 = (bf16[1,128,4096]{2,1,0:T(8,128)(2,1)}, f32[32,512]{1,0:T(8,128)}, f32[64,512]{1,0:T(8,128)}) custom-call(bf16[1,128,4096]{2,1,0:T(8,128)(2,1)} %get-tuple-element.6.mixed_raw, f32[32,512]{1,0:T(8,128)} %get-tuple-element.7.ge_raw, f32[64,512]{1,0:T(8,128)} %get-tuple-element.8.gf_raw), custom_call_target="tpu_custom_call" | custom-call | tf_op jit(solution)/shard_map/collect/pallas_call | solution.py:620

commit v7 on v6

--- a/solution.py
+++ b/solution.py
@@ -56,9 +56,9 @@
     mixed_hbm, ge_ref, gf_ref,
     ids_raw, ids_mine, ids_in, perm, emb, taps, lf_in, cot_in, fwd, inv,
     x, uq, uk, uv, field, hfield, spec_h, spec_z, hbuf, pbuf, wbuf, wf, conv, gq, gx,
-    onehot, lookups, mixed_out, gf_out, gf_in, gf_mid, gf_end, ge_out, ge_in,
-    local_sem, ids_send, ids_recv, cot_send, cot_recv, mix_send, mix_recv, quad_send, quad_recv, ring_send, ring_recv,
-    ge_send, ge_recv,
+    onehot, lookups, mixed_out, gf_out, gf_in, ge_out, ge_in, lf_raw, cot_raw,
+    local_sem, ids_send, ids_recv, cot_send, cot_recv, mix_send, mix_recv, half_send, half_recv,
+    cross_send, cross_recv, relay_send, relay_recv, gf_send, gf_recv, ge_send, ge_recv,
 ):
     dp_n, ctx_n, vocab, part, block = dims
     cw = part // 2
@@ -74,7 +74,7 @@
     c_me = lax.rem(dp, 2)
     ring_n = dp_n // 4
     y_me, z_me = lax.div(g, ring_n), lax.rem(g, ring_n)
-    quad_me = 2 * y_me + c_me
+    half_n, half_me = 2 * ring_n, 2 * z_me + c_me
     pair_me = c_me * ctx_n + p_me
     first = pl.multiple_of(p_me * part + c_me * cw, cw)
     halves = [pl.ds(h * LANES, LANES) for h in range(cw // LANES)]
@@ -90,6 +90,10 @@
     ]
     load_ids = pltpu.make_async_copy(ids_hbm, ids_raw, local_sem.at[4])
     load_ids.start()
+    load_lf = pltpu.make_async_copy(lf_hbm, lf_raw, local_sem.at[5])
+    load_lf.start()
+    load_cot = pltpu.make_async_copy(cot_hbm.at[0], cot_raw, local_sem.at[6])
+    load_cot.start()
     for load in loads:
         load.start()
 
@@ -100,12 +104,6 @@
         device = (2 * g + lax.div(to, ctx_n), lax.rem(to, ctx_n))
         pl.semaphore_signal(barrier, inc=1, device_id=device, device_id_type=MESH)
 
-    def quad_device(to):
-        return ((lax.div(to, 2) * ring_n + z_me) * 2 + lax.rem(to, 2), p_me)
-
-    def ring_device(to):
-        return ((y_me * ring_n + to) * 2 + c_me, p_me)
-
     def greet_dp(i):
         device = (lax.rem(dp + 1 + i, dp_n), p_me)
         pl.semaphore_signal(barrier, inc=1, device_id=device, device_id_type=MESH)
@@ -114,7 +112,7 @@
     loop(dp_n - 1, greet_dp)
     def natural(axis):
         place = lax.broadcasted_iota(jnp.int32, (block, block), axis)
-        return 4 * lax.rem(place, bs) + lax.div(place, bs)
+        return 4 * (place & (bs - 1)) + (place >> (bs.bit_length() - 1))
 
     perm[0] = (natural(0) == lax.broadcasted_iota(jnp.int32, (block, block), 1)).astype(F32).astype(BF)
     perm[1] = (natural(1) == lax.broadcasted_iota(jnp.int32, (block, block), 0)).astype(F32).astype(BF)
@@ -132,24 +130,29 @@
             device_id=(2 * g + lax.div(to, ctx_n), lax.rem(to, ctx_n)), device_id_type=MESH,
         )
 
-    def quad_copy(kind, to):
-        src = (lf_hbm.at[:, chunk(lax.rem(to, 2), cw)], gf_mid.at[to])[kind]
-        dst = (lf_in.at[y_me, z_me, c_me], gf_end.at[quad_me])[kind]
-        return pltpu.make_async_remote_copy(
-            src_ref=src, dst_ref=dst, send_sem=quad_send.at[kind, to], recv_sem=quad_recv.at[kind, quad_me],
-            device_id=quad_device(to), device_id_type=MESH,
-        )
-
-    def ring_copy(kind, to):
-        src = (lf_in.at[:, z_me], gf_out.at[:, to])[kind]
-        dst = (lf_in.at[:, z_me], gf_in.at[z_me])[kind]
-        return pltpu.make_async_remote_copy(
-            src_ref=src, dst_ref=dst, send_sem=ring_send.at[kind, to], recv_sem=ring_recv.at[kind, z_me],
-            device_id=ring_device(to), device_id_type=MESH,
+    def half_copy(to):
+        return pltpu.make_async_remote_copy(
+            src_ref=lf_raw.at[:, chunk(lax.rem(to, 2), cw)], dst_ref=lf_in.at[y_me, z_me, c_me],
+            send_sem=half_send.at[to], recv_sem=half_recv.at[half_me],
+            device_id=(y_me * half_n + to, p_me), device_id_type=MESH,
+        )
+
+    def cross_copy(to):
+        return pltpu.make_async_remote_copy(
+            src_ref=lf_raw.at[:, to * cw : (to + 1) * cw], dst_ref=lf_in.at[y_me, z_me, c_me],
+            send_sem=cross_send.at[to], recv_sem=cross_recv.at[c_me],
+            device_id=((1 - y_me) * half_n + 2 * z_me + to, p_me), device_id_type=MESH,
+        )
+
+    def relay_copy(to):
+        return pltpu.make_async_remote_copy(
+            src_ref=lf_in.at[1 - y_me, z_me], dst_ref=lf_in.at[1 - y_me, z_me],
+            send_sem=relay_send.at[to], recv_sem=relay_recv.at[z_me],
+            device_id=(y_me * half_n + 2 * to + c_me, p_me), device_id_type=MESH,
         )
 
     def cot_columns(to):
-        return cot_hbm.at[0, :, chunk(2 * lax.rem(to, ctx_n) + lax.div(to, ctx_n), cw)]
+        return cot_raw.at[:, chunk(2 * lax.rem(to, ctx_n) + lax.div(to, ctx_n), cw)]
 
     def cot_copy(to):
         return pltpu.make_async_remote_copy(
@@ -164,6 +167,12 @@
             device_id=(2 * g + lax.div(to, ctx_n), lax.rem(to, ctx_n)), device_id_type=MESH,
         )
 
+    def gf_copy(to):
+        return pltpu.make_async_remote_copy(
+            src_ref=gf_out.at[to], dst_ref=gf_in.at[dp], send_sem=gf_send.at[to], recv_sem=gf_recv.at[dp],
+            device_id=(to, p_me), device_id_type=MESH,
+        )
+
     def ge_copy(to):
         return pltpu.make_async_remote_copy(
             src_ref=ge_out.at[to], dst_ref=ge_in.at[dp], send_sem=ge_send.at[to], recv_sem=ge_recv.at[dp],
@@ -176,13 +185,18 @@
     def arrived(slot, sem):
         pltpu.make_async_copy(slot, slot, sem).wait()
 
+    load_lf.wait()
+    for to in range(2):
+        cross_copy(to).start()
+    others(half_n, half_me, lambda to: half_copy(to).start())
+    others(pair_n, pair_me, lambda to: ids_copy(to).start())
     pltpu.make_async_copy(ids_mine, ids_in.at[pair_me], ids_recv.at[pair_me]).start()
-    pltpu.make_async_copy(lf_hbm.at[:, chunk(c_me, cw)], lf_in.at[y_me, z_me, c_me], quad_recv.at[0, quad_me]).start()
+    pltpu.make_async_copy(lf_raw.at[:, chunk(c_me, cw)], lf_in.at[y_me, z_me, c_me], half_recv.at[half_me]).start()
+    load_cot.wait()
     pltpu.make_async_copy(cot_columns(pair_me), cot_in.at[pair_me], cot_recv.at[pair_me]).start()
-    others(4, quad_me, lambda to: quad_copy(0, to).start())
-    others(pair_n, pair_me, lambda to: ids_copy(to).start())
-    loop(4, lambda i: arrived(lf_in.at[lax.div(i, 2), z_me, lax.rem(i, 2)], quad_recv.at[0, i]))
-    others(ring_n, z_me, lambda to: ring_copy(0, to).start())
+    for c in range(2):
+        arrived(lf_in.at[1 - y_me, z_me, c], cross_recv.at[c])
+    others(ring_n, z_me, lambda to: relay_copy(to).start())
     others(pair_n, pair_me, lambda to: cot_copy(to).start())
 
     loads[0].wait()
@@ -279,7 +293,8 @@
                 for j in range(4):
                     hfield[j, chunk(2 * i + k, bs), :] = outs[k][j * bs : (j + 1) * bs]
 
-        others(ring_n, z_me, lambda i: arrived(lf_in.at[:, i], ring_recv.at[0, i]))
+        loop(half_n, lambda i: arrived(lf_in.at[y_me, lax.div(i, 2), lax.rem(i, 2)], half_recv.at[i]))
+        others(ring_n, z_me, lambda i: arrived(lf_in.at[1 - y_me, i], relay_recv.at[i]))
         loop(ctx_n // 2, gather_taps)
 
     phase_taps()
@@ -431,28 +446,22 @@
         for k in range(2):
             for q in range(per):
                 d = (2 * i + k) * per + q
-                gf_out[lax.div(d, 2 * ring_n), lax.rem(lax.div(d, 2), ring_n), lax.rem(d, 2)] = outs[k][q * lr : (q + 1) * lr]
+                gf_out[d] = outs[k][q * lr : (q + 1) * lr]
 
     def phase_filter_rows():
         loop(ctx_n // 2, filter_rows)
 
     phase_filter_rows()
-    others(ring_n, z_me, lambda to: ring_copy(1, to).start())
-
-    def ring_sum(kind, out, arrivals, mid, end):
-        others(ring_n, z_me, lambda i: arrived(arrivals.at[i], ring_recv.at[kind, i]))
-        for q in range(4):
-            total = out[q // 2, z_me, q % 2].astype(F32)
-            for i in range(1, ring_n):
-                total = total + arrivals[lax.rem(z_me + i, ring_n), q // 2, q % 2].astype(F32)
-            mid[q] = total.astype(BF)
-        end[quad_me] = mid[quad_me]
-        others(4, quad_me, lambda to: quad_copy(kind, to).start())
-
-    def quad_sum(kind, end, result):
-        others(4, quad_me, lambda i: arrived(end.at[i], quad_recv.at[kind, i]))
+    others(dp_n, dp, lambda to: gf_copy(to).start())
+
+    def owner_sum(out, arrivals, sems, result):
+        others(dp_n, dp, lambda i: arrived(arrivals.at[i], sems.at[i]))
+        arrivals[dp] = out[dp]
         for c in range(2):
-            result[:, c * cw : (c + 1) * cw] = end[c].astype(F32) + end[2 + c].astype(F32)
+            total = arrivals[c].astype(F32)
+            for i in range(1, dp_n // 2):
+                total = total + arrivals[2 * i + c].astype(F32)
+            result[:, c * cw : (c + 1) * cw] = total
 
     def gz_idft(i):
         s, j = lax.div(i, 4), lax.rem(i, 4)
@@ -498,15 +507,8 @@
     phase_scatter()
     others(dp_n, dp, lambda to: ge_copy(to).start())
 
-    ring_sum(1, gf_out, gf_in, gf_mid, gf_end)
-    quad_sum(1, gf_end, gf_ref)
-    others(dp_n, dp, lambda i: arrived(ge_in.at[i], ge_recv.at[i]))
-    ge_in[dp] = ge_out[dp]
-    for c in range(2):
-        total = ge_in[c].astype(F32)
-        for i in range(1, dp_n // 2):
-            total = total + ge_in[2 * i + c].astype(F32)
-        ge_ref[:, c * cw : (c + 1) * cw] = total
+    owner_sum(gf_out, gf_in, gf_recv, gf_ref)
+    owner_sum(ge_out, ge_in, ge_recv, ge_ref)
 
     def mixed_arrived(i):
         s, p = lax.div(i, ctx_n), lax.rem(i, ctx_n)
@@ -519,18 +521,16 @@
         cot_copy(to).wait_send()
         mix_copy(to).wait_send()
 
-    def quad_sent(to):
-        for kind in range(2):
-            quad_copy(kind, to).wait_send()
-
-    def ring_sent(to):
-        for kind in range(2):
-            ring_copy(kind, to).wait_send()
+    def dp_sent(to):
+        gf_copy(to).wait_send()
+        ge_copy(to).wait_send()
 
     others(pair_n, pair_me, pair_sent)
-    others(4, quad_me, quad_sent)
-    others(dp_n, dp, lambda to: ge_copy(to).wait_send())
-    others(ring_n, z_me, ring_sent)
+    others(dp_n, dp, dp_sent)
+    others(half_n, half_me, lambda to: half_copy(to).wait_send())
+    others(ring_n, z_me, lambda to: relay_copy(to).wait_send())
+    for to in range(2):
+        cross_copy(to).wait_send()
 
 
 def collect(mixed_raw, ge_raw, gf_raw, mixed, ge, gf, mixed_vmem, ge_vmem, gf_vmem, in_sem, out_sem):
@@ -598,18 +598,20 @@
             pltpu.VMEM((pair_n * block, vocab), BF),
             pltpu.VMEM((vocab, pair_n * block), BF),
             pltpu.VMEM((pair_n, block, cw), BF),
-            pltpu.VMEM((2, ring_n, 2, lr, cw), BF),
-            pltpu.VMEM((ring_n, 2, 2, lr, cw), BF),
-            pltpu.VMEM((4, lr, cw), BF),
-            pltpu.VMEM((4, lr, cw), BF),
+            pltpu.VMEM((dp_n, lr, cw), BF),
+            pltpu.VMEM((dp_n, lr, cw), BF),
             pltpu.VMEM((dp_n, vr, cw), BF),
             pltpu.VMEM((dp_n, vr, cw), BF),
-            dma((5,)),
+            pltpu.VMEM((lr, part), BF),
+            pltpu.VMEM((block, width), BF),
+            dma((7,)),
             dma((pair_n,)), dma((pair_n,)),
             dma((pair_n,)), dma((pair_n,)),
             dma((pair_n,)), dma((pair_n,)),
-            dma((2, 4)), dma((2, 4)),
-            dma((2, ring_n)), dma((2, ring_n)),
+            dma((2 * ring_n,)), dma((2 * ring_n,)),
+            dma((2,)), dma((2,)),
+            dma((ring_n,)), dma((ring_n,)),
+            dma((dp_n,)), dma((dp_n,)),
             dma((dp_n,)), dma((dp_n,)),
         ],
         compiler_params=pltpu.CompilerParams(

time: 52.8 us -> 51.9 us (0.983)
  Pallas kernels: 52 us -> 50.9 us
    pallas_call x1, Pallas kernels: 49.9 us -> 48.8 us  [body(): pl.pallas_call(functools.partial(kernel, (dp_n, ctx_n, vocab, part, block...]
where the time goes in v7:
time: 51.9 us; the launch traced here: 51.5 us
  Pallas kernels  50.9 us (98%)
  between operations  0.64 us (1%)
    pallas_call x1, Pallas kernels, body(): pl.pallas_call(functools.partial(kernel, (dp_n, ctx_n, vocab, part, block...  48.8 us
    pallas_call x1, Pallas kernels, body(): pl.pallas_call(collect, out_shape=[jax.ShapeDtypeStruct(r.shape, r.dtype)...  2.08 us

profile of v7, /device:TPU:1, one launch (start us, length us, event | category | flops | bytes accessed | tf_op | source)
XLA Modules:
  0.0 51.5 jit_solution(14742664245039602444)
XLA Ops:
  0.6 48.8 %hyena.1 = (bf16[1,128,4096]{2,1,0:T(8,128)(2,1)}, f32[32,512]{1,0:T(8,128)}, f32[64,512]{1,0:T(8,128)}) custom-call(s32[1,128]{1,0:T(1,128)} %ids_hbm.1, bf16[512,4096]{1,0:T(8,128)(2,1)} %emb_hbm.1, f32[3,3,4096]{2,1,0:T(4,128)} %taps_hbm.1, bf16[64,512]{1,0:T(8,128)(2,1)} %lf_hbm.1, bf16[1,128,4096]{2,1,0:T(8,128)(2,1)} %cot_hbm.1, ...), custom_call_target="tpu_custom_call" | custom-call | tf_op jit(solution)/shard_map/hyena/pallas_call | solution.py:563
  49.5 2.1 %collect.1 = (bf16[1,128,4096]{2,1,0:T(8,128)(2,1)}, f32[32,512]{1,0:T(8,128)}, f32[64,512]{1,0:T(8,128)}) custom-call(bf16[1,128,4096]{2,1,0:T(8,128)(2,1)} %get-tuple-element.6.mixed_raw, f32[32,512]{1,0:T(8,128)} %get-tuple-element.7.ge_raw, f32[64,512]{1,0:T(8,128)} %get-tuple-element.8.gf_raw), custom_call_target="tpu_custom_call" | custom-call | tf_op jit(solution)/shard_map/collect/pallas_call | solution.py:622

commit v8 on v7

--- a/solution.py
+++ b/solution.py
@@ -79,6 +79,8 @@
     first = pl.multiple_of(p_me * part + c_me * cw, cw)
     halves = [pl.ds(h * LANES, LANES) for h in range(cw // LANES)]
 
+    unroll_n = 4 if ctx_n % 4 == 0 else 2
+
     def chunk(i, size):
         return pl.ds(pl.multiple_of(i * size, size), size)
 
@@ -219,7 +221,7 @@
 
     def phase_embed():
         def embed(i):
-            rows = dot(onehot[chunk(i, 4 * block), :], emb[...])
+            rows = dot(onehot[chunk(i, 4 * block), :], emb[...]).astype(BF)
             for q in range(4):
                 s, p = lax.div(4 * i + q, ctx_n), lax.rem(4 * i + q, ctx_n)
                 for j in range(4):
@@ -238,7 +240,7 @@
             def short(s, h=h, f=f):
                 def step(p, carry):
                     rows = chunk(p, bs)
-                    xs = [x[s, j, rows, h] for j in range(4)]
+                    xs = [x[s, j, rows, h].astype(F32) for j in range(4)]
                     turned = [pltpu.roll(xs[2], 1, 0), pltpu.roll(xs[3], 1, 0)]
                     late = [jnp.where(row16 == 0, carry[q], turned[q]) for q in range(2)]
                     line = late + xs
@@ -247,9 +249,9 @@
                         for r in range(3)
                     ]
                     for j in range(4):
-                        uq[s, j, rows, h] = us[0][j]
-                        uk[s, j, rows, h] = us[1][j]
-                        uv[s, j, rows, h] = us[2][j]
+                        uq[s, j, rows, h] = us[0][j].astype(BF)
+                        uk[s, j, rows, h] = us[1][j].astype(BF)
+                        uv[s, j, rows, h] = us[2][j].astype(BF)
                         field[s, j, rows, h] = (us[1][j] * us[2][j]).astype(BF)
                     return tuple(turned)
 
@@ -264,7 +266,7 @@
 
     def field_dft(i):
         s, j = lax.div(i, 4), lax.rem(i, 4)
-        pbuf[s, j] = dot(fwd[j], field[s, j])
+        pbuf[s, j] = dot(fwd[j], field[s, j]).astype(BF)
 
     def phase_field_dft():
         loop(8, field_dft, 4)
@@ -285,22 +287,22 @@
     def phase_taps():
         def gather_taps(i):
             outs = []
-            for k in range(2):
-                pieces = [(2 * i + k) * per + q for q in range(per)]
+            for k in range(unroll_n):
+                pieces = [(unroll_n * i + k) * per + q for q in range(per)]
                 rows = [lf_in[lax.div(d, 2 * ring_n), lax.rem(lax.div(d, 2), ring_n), lax.rem(d, 2)] for d in pieces]
                 outs.append(dot(perm[0], jnp.concatenate(rows, 0)).astype(BF))
-            for k in range(2):
+            for k in range(unroll_n):
                 for j in range(4):
-                    hfield[j, chunk(2 * i + k, bs), :] = outs[k][j * bs : (j + 1) * bs]
+                    hfield[j, chunk(unroll_n * i + k, bs), :] = outs[k][j * bs : (j + 1) * bs]
 
         loop(half_n, lambda i: arrived(lf_in.at[y_me, lax.div(i, 2), lax.rem(i, 2)], half_recv.at[i]))
         others(ring_n, z_me, lambda i: arrived(lf_in.at[1 - y_me, i], relay_recv.at[i]))
-        loop(ctx_n // 2, gather_taps)
+        loop(ctx_n // unroll_n, gather_taps)
 
     phase_taps()
 
     def filter_dft(j):
-        hbuf[j] = dot(fwd[j], hfield[j])
+        hbuf[j] = dot(fwd[j], hfield[j]).astype(BF)
 
     def phase_filter_dft():
         loop(4, filter_dft, 4)
@@ -308,16 +310,16 @@
     phase_filter_dft()
 
     def butterfly(ref, i, h):
-        re = [ref[j, chunk(i, KC), h] for j in range(4)]
-        im = [ref[j, pl.ds(pl.multiple_of(sub + i * KC, KC), KC), h] for j in range(4)]
+        re = [ref[j, chunk(i, KC), h].astype(F32) for j in range(4)]
+        im = [ref[j, pl.ds(pl.multiple_of(sub + i * KC, KC), KC), h].astype(F32) for j in range(4)]
         return radix4(re, im, -1)
 
     def filter_mix(i):
         for h in halves:
             re, im = butterfly(hbuf, i, h)
             for m in range(4):
-                spec_h[m, 0, chunk(i, KC), h] = re[m]
-                spec_h[m, 1, chunk(i, KC), h] = im[m]
+                spec_h[m, 0, chunk(i, KC), h] = re[m].astype(BF)
+                spec_h[m, 1, chunk(i, KC), h] = im[m].astype(BF)
 
     def phase_filter_mix():
         loop(sub // KC, filter_mix)
@@ -340,9 +342,9 @@
                 re, im = butterfly(pbuf.at[s], i, h)
                 out_re, out_im = [], []
                 for m in range(4):
-                    spec_z[s, m, 0, chunk(i, KC), h] = re[m]
-                    spec_z[s, m, 1, chunk(i, KC), h] = im[m]
-                    h_re, h_im = spec_h[m, 0, chunk(i, KC), h], spec_h[m, 1, chunk(i, KC), h]
+                    spec_z[s, m, 0, chunk(i, KC), h] = re[m].astype(BF)
+                    spec_z[s, m, 1, chunk(i, KC), h] = im[m].astype(BF)
+                    h_re, h_im = spec_h[m, 0, chunk(i, KC), h].astype(F32), spec_h[m, 1, chunk(i, KC), h].astype(F32)
                     out_re.append(re[m] * h_re - im[m] * h_im)
                     out_im.append(re[m] * h_im + im[m] * h_re)
                 put(wbuf.at[s], i, h, out_re, out_im)
@@ -353,7 +355,7 @@
         phase_conv_mix()
 
         def conv_idft(j, s=s):
-            conv[s, j] = dot(inv[j], wbuf[s, j]).astype(BF).astype(F32)
+            conv[s, j] = dot(inv[j], wbuf[s, j]).astype(BF)
 
         def phase_conv_idft():
             loop(4, conv_idft, 4)
@@ -362,29 +364,22 @@
 
         def mix(i, s=s):
             outs = []
-            for k in range(2):
-                p = lax.rem(p_me + 1 + 2 * i + k, ctx_n)
-                rows = chunk(p, bs)
-                out = jnp.concatenate([(uq[s, j, rows, :] * conv[s, j, rows, :]).astype(BF) for j in range(4)], 0)
-                outs.append((s * ctx_n + p, dot(perm[1], out).astype(BF)))
-            for to, out in outs:
-                mixed_out[to] = out
-            for to, _ in outs:
-
-                @pl.when(to != pair_me)
-                def _():
-                    mix_copy(to).start()
-
-                @pl.when(to == pair_me)
-                def _():
-                    pltpu.make_async_copy(
-                        mixed_out.at[to], mixed_hbm.at[0, :, pl.ds(first, cw)], mix_recv.at[pair_me]
-                    ).start()
+            for k in range(unroll_n):
+                rows = chunk(unroll_n * i + k, bs)
+                pieces = [
+                    (uq[s, j, rows, :].astype(F32) * conv[s, j, rows, :].astype(F32)).astype(BF) for j in range(4)
+                ]
+                outs.append(dot(perm[1], jnp.concatenate(pieces, 0)).astype(BF))
+            for k in range(unroll_n):
+                mixed_out[s * ctx_n + unroll_n * i + k] = outs[k]
 
         def phase_mix():
-            loop(ctx_n // 2, mix)
+            loop(ctx_n // unroll_n, mix)
 
         phase_mix()
+
+    others(pair_n, pair_me, lambda to: mix_copy(to).start())
+    pltpu.make_async_copy(mixed_out.at[pair_me], mixed_hbm.at[0, :, pl.ds(first, cw)], mix_recv.at[pair_me]).start()
 
     def take(i):
         for k in range(4):
@@ -395,8 +390,8 @@
             rows = chunk(p, bs)
             for j in range(4):
                 piece = outs[k][j * bs : (j + 1) * bs]
-                field[s, j, rows, :] = (piece * uq[s, j, rows, :]).astype(BF)
-                gq[s, j, rows, :] = piece * conv[s, j, rows, :]
+                field[s, j, rows, :] = (piece * uq[s, j, rows, :].astype(F32)).astype(BF)
+                gq[s, j, rows, :] = (piece * conv[s, j, rows, :].astype(F32)).astype(BF)
 
     def phase_take():
         loop(pair_n // 4, take)
@@ -411,8 +406,8 @@
                 re, im = butterfly(pbuf.at[s], i, h)
                 out_re, out_im, f_re, f_im = [], [], [], []
                 for m in range(4):
-                    h_re, h_im = spec_h[m, 0, chunk(i, KC), h], spec_h[m, 1, chunk(i, KC), h]
-                    z_re, z_im = spec_z[s, m, 0, chunk(i, KC), h], spec_z[s, m, 1, chunk(i, KC), h]
+                    h_re, h_im = spec_h[m, 0, chunk(i, KC), h].astype(F32), spec_h[m, 1, chunk(i, KC), h].astype(F32)
+                    z_re, z_im = spec_z[s, m, 0, chunk(i, KC), h].astype(F32), spec_z[s, m, 1, chunk(i, KC), h].astype(F32)
                     out_re.append(re[m] * h_re + im[m] * h_im)
                     out_im.append(im[m] * h_re - re[m] * h_im)
                     f_re.append(re[m] * z_re + im[m] * z_im)
@@ -440,16 +435,16 @@
 
     def filter_rows(i):
         outs = []
-        for k in range(2):
-            rows = jnp.concatenate([hfield[j, chunk(2 * i + k, bs), :] for j in range(4)], 0)
+        for k in range(unroll_n):
+            rows = jnp.concatenate([hfield[j, chunk(unroll_n * i + k, bs), :] for j in range(4)], 0)
             outs.append(dot(perm[1], rows).astype(BF))
-        for k in range(2):
+        for k in range(unroll_n):
             for q in range(per):
-                d = (2 * i + k) * per + q
+                d = (unroll_n * i + k) * per + q
                 gf_out[d] = outs[k][q * lr : (q + 1) * lr]
 
     def phase_filter_rows():
-        loop(ctx_n // 2, filter_rows)
+        loop(ctx_n // unroll_n, filter_rows)
 
     phase_filter_rows()
     others(dp_n, dp, lambda to: gf_copy(to).start())
@@ -465,7 +460,7 @@
 
     def gz_idft(i):
         s, j = lax.div(i, 4), lax.rem(i, 4)
-        conv[s, j] = dot(inv[j], wbuf[s, j])
+        conv[s, j] = dot(inv[j], wbuf[s, j]).astype(BF)
 
     def phase_gz_idft():
         loop(8, gz_idft, 4)
@@ -482,8 +477,12 @@
                     rows = chunk(p, bs)
                     lines = [[], [], []]
                     for j in range(4):
-                        gz = conv[s, j, rows, h].astype(BF).astype(F32)
-                        gs = [gq[s, j, rows, h], gz * uv[s, j, rows, h], gz * uk[s, j, rows, h]]
+                        gz = conv[s, j, rows, h].astype(F32)
+                        gs = [
+                        gq[s, j, rows, h].astype(F32),
+                        gz * uv[s, j, rows, h].astype(F32),
+                        gz * uk[s, j, rows, h].astype(F32),
+                    ]
                         for tap in range(3):
                             lines[tap].append(f[0][tap] * gs[0] + f[1][tap] * gs[1] + f[2][tap] * gs[2])
                     turned = [pltpu.roll(v, bs - 1, 0) for v in (lines[1][0], lines[2][0], lines[2][1])]
@@ -580,20 +579,20 @@
             pltpu.VMEM((pair_n, block, cw), BF),
             pltpu.VMEM(fwd.shape, BF),
             pltpu.VMEM(inv.shape, BF),
-            pltpu.VMEM((2, 4, sub, cw), F32),
-            pltpu.VMEM((2, 4, sub, cw), F32),
-            pltpu.VMEM((2, 4, sub, cw), F32),
-            pltpu.VMEM((2, 4, sub, cw), F32),
+            pltpu.VMEM((2, 4, sub, cw), BF),
+            pltpu.VMEM((2, 4, sub, cw), BF),
+            pltpu.VMEM((2, 4, sub, cw), BF),
+            pltpu.VMEM((2, 4, sub, cw), BF),
             pltpu.VMEM((2, 4, sub, cw), BF),
             pltpu.VMEM((4, sub, cw), BF),
-            pltpu.VMEM((4, 2, sub, cw), F32),
-            pltpu.VMEM((2, 4, 2, sub, cw), F32),
-            pltpu.VMEM((4, 2 * sub, cw), F32),
-            pltpu.VMEM((2, 4, 2 * sub, cw), F32),
+            pltpu.VMEM((4, 2, sub, cw), BF),
+            pltpu.VMEM((2, 4, 2, sub, cw), BF),
+            pltpu.VMEM((4, 2 * sub, cw), BF),
+            pltpu.VMEM((2, 4, 2 * sub, cw), BF),
             pltpu.VMEM((2, 4, 2 * sub, cw), BF),
             pltpu.VMEM((4, 2 * sub, cw), BF),
-            pltpu.VMEM((2, 4, sub, cw), F32),
-            pltpu.VMEM((2, 4, sub, cw), F32),
+            pltpu.VMEM((2, 4, sub, cw), BF),
+            pltpu.VMEM((2, 4, sub, cw), BF),
             pltpu.VMEM((2, ctx_n, 4, bs, cw), BF),
             pltpu.VMEM((pair_n * block, vocab), BF),
             pltpu.VMEM((vocab, pair_n * block), BF),

time: 51.9 us -> 52.1 us (level)
  no operation moved by 1% of the time
where the time goes in v8:
time: 52.1 us; the launch traced here: 52 us
  Pallas kernels  51.4 us (99%)
  between operations  0.64 us (1%)
    pallas_call x1, Pallas kernels, body(): pl.pallas_call(functools.partial(kernel, (dp_n, ctx_n, vocab, part, block...  49.3 us
    pallas_call x1, Pallas kernels, body(): pl.pallas_call(collect, out_shape=[jax.ShapeDtypeStruct(r.shape, r.dtype)...  2.08 us

profile of v8, /device:TPU:1, one launch (start us, length us, event | category | flops | bytes accessed | tf_op | source)
XLA Modules:
  0.0 52.0 jit_solution(5534793541720249094)
XLA Ops:
  0.6 49.3 %hyena.1 = (bf16[1,128,4096]{2,1,0:T(8,128)(2,1)}, f32[32,512]{1,0:T(8,128)}, f32[64,512]{1,0:T(8,128)}) custom-call(s32[1,128]{1,0:T(1,128)} %ids_hbm.1, bf16[512,4096]{1,0:T(8,128)(2,1)} %emb_hbm.1, f32[3,3,4096]{2,1,0:T(4,128)} %taps_hbm.1, bf16[64,512]{1,0:T(8,128)(2,1)} %lf_hbm.1, bf16[1,128,4096]{2,1,0:T(8,128)(2,1)} %cot_hbm.1, ...), custom_call_target="tpu_custom_call" | custom-call | tf_op jit(solution)/shard_map/hyena/pallas_call | solution.py:562
  49.9 2.1 %collect.1 = (bf16[1,128,4096]{2,1,0:T(8,128)(2,1)}, f32[32,512]{1,0:T(8,128)}, f32[64,512]{1,0:T(8,128)}) custom-call(bf16[1,128,4096]{2,1,0:T(8,128)(2,1)} %get-tuple-element.6.mixed_raw, f32[32,512]{1,0:T(8,128)} %get-tuple-element.7.ge_raw, f32[64,512]{1,0:T(8,128)} %get-tuple-element.8.gf_raw), custom_call_target="tpu_custom_call" | custom-call | tf_op jit(solution)/shard_map/collect/pallas_call | solution.py:621

commit v9 on v7

--- a/solution.py
+++ b/solution.py
@@ -79,6 +79,8 @@
     first = pl.multiple_of(p_me * part + c_me * cw, cw)
     halves = [pl.ds(h * LANES, LANES) for h in range(cw // LANES)]
 
+    unroll_n = 4 if ctx_n % 4 == 0 else 2
+
     def chunk(i, size):
         return pl.ds(pl.multiple_of(i * size, size), size)
 
@@ -126,28 +128,28 @@
 
     def ids_copy(to):
         return pltpu.make_async_remote_copy(
-            src_ref=ids_mine, dst_ref=ids_in.at[pair_me], send_sem=ids_send.at[to], recv_sem=ids_recv.at[pair_me],
+            src_ref=ids_mine, dst_ref=ids_in.at[pair_me], send_sem=ids_send, recv_sem=ids_recv,
             device_id=(2 * g + lax.div(to, ctx_n), lax.rem(to, ctx_n)), device_id_type=MESH,
         )
 
     def half_copy(to):
         return pltpu.make_async_remote_copy(
             src_ref=lf_raw.at[:, chunk(lax.rem(to, 2), cw)], dst_ref=lf_in.at[y_me, z_me, c_me],
-            send_sem=half_send.at[to], recv_sem=half_recv.at[half_me],
+            send_sem=half_send, recv_sem=half_recv,
             device_id=(y_me * half_n + to, p_me), device_id_type=MESH,
         )
 
     def cross_copy(to):
         return pltpu.make_async_remote_copy(
             src_ref=lf_raw.at[:, to * cw : (to + 1) * cw], dst_ref=lf_in.at[y_me, z_me, c_me],
-            send_sem=cross_send.at[to], recv_sem=cross_recv.at[c_me],
+            send_sem=cross_send, recv_sem=cross_recv,
             device_id=((1 - y_me) * half_n + 2 * z_me + to, p_me), device_id_type=MESH,
         )
 
     def relay_copy(to):
         return pltpu.make_async_remote_copy(
             src_ref=lf_in.at[1 - y_me, z_me], dst_ref=lf_in.at[1 - y_me, z_me],
-            send_sem=relay_send.at[to], recv_sem=relay_recv.at[z_me],
+            send_sem=relay_send, recv_sem=relay_recv,
             device_id=(y_me * half_n + 2 * to + c_me, p_me), device_id_type=MESH,
         )
 
@@ -156,26 +158,26 @@
 
     def cot_copy(to):
         return pltpu.make_async_remote_copy(
-            src_ref=cot_columns(to), dst_ref=cot_in.at[pair_me], send_sem=cot_send.at[to], recv_sem=cot_recv.at[pair_me],
+            src_ref=cot_columns(to), dst_ref=cot_in.at[pair_me], send_sem=cot_send, recv_sem=cot_recv,
             device_id=(2 * g + lax.div(to, ctx_n), lax.rem(to, ctx_n)), device_id_type=MESH,
         )
 
     def mix_copy(to):
         return pltpu.make_async_remote_copy(
             src_ref=mixed_out.at[to], dst_ref=mixed_hbm.at[0, :, pl.ds(first, cw)],
-            send_sem=mix_send.at[to], recv_sem=mix_recv.at[pair_me],
+            send_sem=mix_send, recv_sem=mix_recv,
             device_id=(2 * g + lax.div(to, ctx_n), lax.rem(to, ctx_n)), device_id_type=MESH,
         )
 
     def gf_copy(to):
         return pltpu.make_async_remote_copy(
-            src_ref=gf_out.at[to], dst_ref=gf_in.at[dp], send_sem=gf_send.at[to], recv_sem=gf_recv.at[dp],
+            src_ref=gf_out.at[to], dst_ref=gf_in.at[dp], send_sem=gf_send, recv_sem=gf_recv,
             device_id=(to, p_me), device_id_type=MESH,
         )
 
     def ge_copy(to):
         return pltpu.make_async_remote_copy(
-            src_ref=ge_out.at[to], dst_ref=ge_in.at[dp], send_sem=ge_send.at[to], recv_sem=ge_recv.at[dp],
+            src_ref=ge_out.at[to], dst_ref=ge_in.at[dp], send_sem=ge_send, recv_sem=ge_recv,
             device_id=(to, p_me), device_id_type=MESH,
         )
 
@@ -190,12 +192,11 @@
         cross_copy(to).start()
     others(half_n, half_me, lambda to: half_copy(to).start())
     others(pair_n, pair_me, lambda to: ids_copy(to).start())
-    pltpu.make_async_copy(ids_mine, ids_in.at[pair_me], ids_recv.at[pair_me]).start()
-    pltpu.make_async_copy(lf_raw.at[:, chunk(c_me, cw)], lf_in.at[y_me, z_me, c_me], half_recv.at[half_me]).start()
+    pltpu.make_async_copy(ids_mine, ids_in.at[pair_me], ids_recv).start()
+    pltpu.make_async_copy(lf_raw.at[:, chunk(c_me, cw)], lf_in.at[y_me, z_me, c_me], half_recv).start()
     load_cot.wait()
-    pltpu.make_async_copy(cot_columns(pair_me), cot_in.at[pair_me], cot_recv.at[pair_me]).start()
-    for c in range(2):
-        arrived(lf_in.at[1 - y_me, z_me, c], cross_recv.at[c])
+    pltpu.make_async_copy(cot_columns(pair_me), cot_in.at[pair_me], cot_recv).start()
+    arrived(lf_in.at[1 - y_me, z_me], cross_recv)
     others(ring_n, z_me, lambda to: relay_copy(to).start())
     others(pair_n, pair_me, lambda to: cot_copy(to).start())
 
@@ -205,8 +206,6 @@
 
     def phase_lookup():
         def lookup(i):
-            for k in range(4):
-                arrived(ids_in.at[4 * i + k], ids_recv.at[4 * i + k])
             rows = [jnp.broadcast_to(ids_in[4 * i + k, 0:1, :], (block, block)) for k in range(4)]
             columns = [jnp.transpose(row) for row in rows]
             for k in range(4):
@@ -215,6 +214,7 @@
                         (columns[k] == vocab_lane + float(q * LANES)).astype(F32).astype(BF)
                     )
 
+        arrived(ids_in, ids_recv)
         loop(pair_n // 4, lookup)
 
     def phase_embed():
@@ -285,17 +285,17 @@
     def phase_taps():
         def gather_taps(i):
             outs = []
-            for k in range(2):
-                pieces = [(2 * i + k) * per + q for q in range(per)]
+            for k in range(unroll_n):
+                pieces = [(unroll_n * i + k) * per + q for q in range(per)]
                 rows = [lf_in[lax.div(d, 2 * ring_n), lax.rem(lax.div(d, 2), ring_n), lax.rem(d, 2)] for d in pieces]
                 outs.append(dot(perm[0], jnp.concatenate(rows, 0)).astype(BF))
-            for k in range(2):
+            for k in range(unroll_n):
                 for j in range(4):
-                    hfield[j, chunk(2 * i + k, bs), :] = outs[k][j * bs : (j + 1) * bs]
-
-        loop(half_n, lambda i: arrived(lf_in.at[y_me, lax.div(i, 2), lax.rem(i, 2)], half_recv.at[i]))
-        others(ring_n, z_me, lambda i: arrived(lf_in.at[1 - y_me, i], relay_recv.at[i]))
-        loop(ctx_n // 2, gather_taps)
+                    hfield[j, chunk(unroll_n * i + k, bs), :] = outs[k][j * bs : (j + 1) * bs]
+
+        arrived(lf_in.at[y_me], half_recv)
+        arrived(lf_in.at[1 - y_me, pl.ds(0, ring_n - 1)], relay_recv)
+        loop(ctx_n // unroll_n, gather_taps)
 
     phase_taps()
 
@@ -362,33 +362,24 @@
 
         def mix(i, s=s):
             outs = []
-            for k in range(2):
-                p = lax.rem(p_me + 1 + 2 * i + k, ctx_n)
-                rows = chunk(p, bs)
-                out = jnp.concatenate([(uq[s, j, rows, :] * conv[s, j, rows, :]).astype(BF) for j in range(4)], 0)
-                outs.append((s * ctx_n + p, dot(perm[1], out).astype(BF)))
-            for to, out in outs:
-                mixed_out[to] = out
-            for to, _ in outs:
-
-                @pl.when(to != pair_me)
-                def _():
-                    mix_copy(to).start()
-
-                @pl.when(to == pair_me)
-                def _():
-                    pltpu.make_async_copy(
-                        mixed_out.at[to], mixed_hbm.at[0, :, pl.ds(first, cw)], mix_recv.at[pair_me]
-                    ).start()
+            for k in range(unroll_n):
+                rows = chunk(unroll_n * i + k, bs)
+                pieces = [
+                    (uq[s, j, rows, :] * conv[s, j, rows, :]).astype(BF) for j in range(4)
+                ]
+                outs.append(dot(perm[1], jnp.concatenate(pieces, 0)).astype(BF))
+            for k in range(unroll_n):
+                mixed_out[s * ctx_n + unroll_n * i + k] = outs[k]
 
         def phase_mix():
-            loop(ctx_n // 2, mix)
+            loop(ctx_n // unroll_n, mix)
 
         phase_mix()
 
+    others(pair_n, pair_me, lambda to: mix_copy(to).start())
+    pltpu.make_async_copy(mixed_out.at[pair_me], mixed_hbm.at[0, :, pl.ds(first, cw)], mix_recv).start()
+
     def take(i):
-        for k in range(4):
-            arrived(cot_in.at[4 * i + k], cot_recv.at[4 * i + k])
         outs = [dot(perm[0], cot_in[4 * i + k]) for k in range(4)]
         for k in range(4):
             s, p = lax.div(4 * i + k, ctx_n), lax.rem(4 * i + k, ctx_n)
@@ -399,6 +390,7 @@
                 gq[s, j, rows, :] = piece * conv[s, j, rows, :]
 
     def phase_take():
+        arrived(cot_in, cot_recv)
         loop(pair_n // 4, take)
 
     phase_take()
@@ -440,23 +432,23 @@
 
     def filter_rows(i):
         outs = []
-        for k in range(2):
-            rows = jnp.concatenate([hfield[j, chunk(2 * i + k, bs), :] for j in range(4)], 0)
+        for k in range(unroll_n):
+            rows = jnp.concatenate([hfield[j, chunk(unroll_n * i + k, bs), :] for j in range(4)], 0)
             outs.append(dot(perm[1], rows).astype(BF))
-        for k in range(2):
+        for k in range(unroll_n):
             for q in range(per):
-                d = (2 * i + k) * per + q
+                d = (unroll_n * i + k) * per + q
                 gf_out[d] = outs[k][q * lr : (q + 1) * lr]
 
     def phase_filter_rows():
-        loop(ctx_n // 2, filter_rows)
+        loop(ctx_n // unroll_n, filter_rows)
 
     phase_filter_rows()
     others(dp_n, dp, lambda to: gf_copy(to).start())
-
-    def owner_sum(out, arrivals, sems, result):
-        others(dp_n, dp, lambda i: arrived(arrivals.at[i], sems.at[i]))
-        arrivals[dp] = out[dp]
+    pltpu.make_async_copy(gf_out.at[dp], gf_in.at[dp], gf_recv).start()
+
+    def owner_sum(arrivals, sems, result):
+        arrived(arrivals, sems)
         for c in range(2):
             total = arrivals[c].astype(F32)
             for i in range(1, dp_n // 2):
@@ -483,7 +475,11 @@
                     lines = [[], [], []]
                     for j in range(4):
                         gz = conv[s, j, rows, h].astype(BF).astype(F32)
-                        gs = [gq[s, j, rows, h], gz * uv[s, j, rows, h], gz * uk[s, j, rows, h]]
+                        gs = [
+                        gq[s, j, rows, h],
+                        gz * uv[s, j, rows, h],
+                        gz * uk[s, j, rows, h],
+                    ]
                         for tap in range(3):
                             lines[tap].append(f[0][tap] * gs[0] + f[1][tap] * gs[1] + f[2][tap] * gs[2])
                     turned = [pltpu.roll(v, bs - 1, 0) for v in (lines[1][0], lines[2][0], lines[2][1])]
@@ -506,31 +502,23 @@
 
     phase_scatter()
     others(dp_n, dp, lambda to: ge_copy(to).start())
-
-    owner_sum(gf_out, gf_in, gf_recv, gf_ref)
-    owner_sum(ge_out, ge_in, ge_recv, ge_ref)
-
-    def mixed_arrived(i):
-        s, p = lax.div(i, ctx_n), lax.rem(i, ctx_n)
-        arrived(mixed_hbm.at[0, :, chunk(2 * p + s, cw)], mix_recv.at[i])
-
-    loop(pair_n, mixed_arrived)
-
-    def pair_sent(to):
-        ids_copy(to).wait_send()
-        cot_copy(to).wait_send()
-        mix_copy(to).wait_send()
-
-    def dp_sent(to):
-        gf_copy(to).wait_send()
-        ge_copy(to).wait_send()
-
-    others(pair_n, pair_me, pair_sent)
-    others(dp_n, dp, dp_sent)
-    others(half_n, half_me, lambda to: half_copy(to).wait_send())
-    others(ring_n, z_me, lambda to: relay_copy(to).wait_send())
-    for to in range(2):
-        cross_copy(to).wait_send()
+    pltpu.make_async_copy(ge_out.at[dp], ge_in.at[dp], ge_recv).start()
+
+    owner_sum(gf_in, gf_recv, gf_ref)
+    owner_sum(ge_in, ge_recv, ge_ref)
+
+    def sent(ref, sem):
+        pltpu.make_async_copy(ref, ref, sem).wait()
+
+    sent(ids_in.at[pl.ds(0, pair_n - 1)], ids_send)
+    sent(lf_in.at[:, 0, 0], cross_send)
+    sent(gf_in.at[pl.ds(0, half_n - 1)], half_send)
+    sent(lf_in.at[0, pl.ds(0, ring_n - 1)], relay_send)
+    sent(cot_in.at[pl.ds(0, pair_n - 1)], cot_send)
+    sent(gf_in.at[pl.ds(0, dp_n - 1)], gf_send)
+    sent(ge_in.at[pl.ds(0, dp_n - 1)], ge_send)
+    sent(mixed_out.at[pl.ds(0, pair_n - 1)], mix_send)
+    arrived(mixed_hbm.at[0], mix_recv)
 
 
 def collect(mixed_raw, ge_raw, gf_raw, mixed, ge, gf, mixed_vmem, ge_vmem, gf_vmem, in_sem, out_sem):
@@ -605,15 +593,7 @@
             pltpu.VMEM((lr, part), BF),
             pltpu.VMEM((block, width), BF),
             dma((7,)),
-            dma((pair_n,)), dma((pair_n,)),
-            dma((pair_n,)), dma((pair_n,)),
-            dma((pair_n,)), dma((pair_n,)),
-            dma((2 * ring_n,)), dma((2 * ring_n,)),
-            dma((2,)), dma((2,)),
-            dma((ring_n,)), dma((ring_n,)),
-            dma((dp_n,)), dma((dp_n,)),
-            dma((dp_n,)), dma((dp_n,)),
-        ],
+        ] + [dma] * 16,
         compiler_params=pltpu.CompilerParams(
             collective_id=0, has_side_effects=True, vmem_limit_bytes=56 * 1024 * 1024
         ),

time: 51.9 us -> 49.7 us (0.958)
  Pallas kernels: 50.9 us -> 48.9 us
    pallas_call x1, Pallas kernels: 48.8 us -> 46.8 us  [body(): pl.pallas_call(functools.partial(kernel, (dp_n, ctx_n, vocab, part, block...]
where the time goes in v9:
time: 49.7 us; the launch traced here: 49.5 us
  Pallas kernels  48.9 us (98%)
  between operations  0.64 us (1%)
    pallas_call x1, Pallas kernels, body(): pl.pallas_call(functools.partial(kernel, (dp_n, ctx_n, vocab, part, block...  46.8 us
    pallas_call x1, Pallas kernels, body(): pl.pallas_call(collect, out_shape=[jax.ShapeDtypeStruct(r.shape, r.dtype)...  2.08 us

profile of v9, /device:TPU:1, one launch (start us, length us, event | category | flops | bytes accessed | tf_op | source)
XLA Modules:
  0.0 49.5 jit_solution(9471224806790656043)
XLA Ops:
  0.6 46.8 %hyena.1 = (bf16[1,128,4096]{2,1,0:T(8,128)(2,1)}, f32[32,512]{1,0:T(8,128)}, f32[64,512]{1,0:T(8,128)}) custom-call(s32[1,128]{1,0:T(1,128)} %ids_hbm.1, bf16[512,4096]{1,0:T(8,128)(2,1)} %emb_hbm.1, f32[3,3,4096]{2,1,0:T(4,128)} %taps_hbm.1, bf16[64,512]{1,0:T(8,128)(2,1)} %lf_hbm.1, bf16[1,128,4096]{2,1,0:T(8,128)(2,1)} %cot_hbm.1, ...), custom_call_target="tpu_custom_call" | custom-call | tf_op jit(solution)/shard_map/hyena/pallas_call | solution.py:551
  47.5 2.1 %collect.1 = (bf16[1,128,4096]{2,1,0:T(8,128)(2,1)}, f32[32,512]{1,0:T(8,128)}, f32[64,512]{1,0:T(8,128)}) custom-call(bf16[1,128,4096]{2,1,0:T(8,128)(2,1)} %get-tuple-element.6.mixed_raw, f32[32,512]{1,0:T(8,128)} %get-tuple-element.7.ge_raw, f32[64,512]{1,0:T(8,128)} %get-tuple-element.8.gf_raw), custom_call_target="tpu_custom_call" | custom-call | tf_op jit(solution)/shard_map/collect/pallas_call | solution.py:602

commit v10 on v9

--- a/solution.py
+++ b/solution.py
@@ -196,9 +196,9 @@
     pltpu.make_async_copy(lf_raw.at[:, chunk(c_me, cw)], lf_in.at[y_me, z_me, c_me], half_recv).start()
     load_cot.wait()
     pltpu.make_async_copy(cot_columns(pair_me), cot_in.at[pair_me], cot_recv).start()
+    others(pair_n, pair_me, lambda to: cot_copy(to).start())
     arrived(lf_in.at[1 - y_me, z_me], cross_recv)
     others(ring_n, z_me, lambda to: relay_copy(to).start())
-    others(pair_n, pair_me, lambda to: cot_copy(to).start())
 
     loads[0].wait()
     loads[1].wait()

time: 49.7 us -> 50.9 us (1.024)
  Pallas kernels: 48.9 us -> 50.2 us
    pallas_call x1, Pallas kernels: 46.8 us -> 48.1 us  [body(): pl.pallas_call(functools.partial(kernel, (dp_n, ctx_n, vocab, part, block...]
where the time goes in v10:
time: 50.9 us; the launch traced here: 50.8 us
  Pallas kernels  50.2 us (99%)
  between operations  0.64 us (1%)
    pallas_call x1, Pallas kernels, body(): pl.pallas_call(functools.partial(kernel, (dp_n, ctx_n, vocab, part, block...  48.1 us
    pallas_call x1, Pallas kernels, body(): pl.pallas_call(collect, out_shape=[jax.ShapeDtypeStruct(r.shape, r.dtype)...  2.08 us

profile of v10, /device:TPU:1, one launch (start us, length us, event | category | flops | bytes accessed | tf_op | source)
XLA Modules:
  0.0 50.8 jit_solution(1472103613921908503)
XLA Ops:
  0.6 48.1 %hyena.1 = (bf16[1,128,4096]{2,1,0:T(8,128)(2,1)}, f32[32,512]{1,0:T(8,128)}, f32[64,512]{1,0:T(8,128)}) custom-call(s32[1,128]{1,0:T(1,128)} %ids_hbm.1, bf16[512,4096]{1,0:T(8,128)(2,1)} %emb_hbm.1, f32[3,3,4096]{2,1,0:T(4,128)} %taps_hbm.1, bf16[64,512]{1,0:T(8,128)(2,1)} %lf_hbm.1, bf16[1,128,4096]{2,1,0:T(8,128)(2,1)} %cot_hbm.1, ...), custom_call_target="tpu_custom_call" | custom-call | tf_op jit(solution)/shard_map/hyena/pallas_call | solution.py:551
  48.7 2.1 %collect.1 = (bf16[1,128,4096]{2,1,0:T(8,128)(2,1)}, f32[32,512]{1,0:T(8,128)}, f32[64,512]{1,0:T(8,128)}) custom-call(bf16[1,128,4096]{2,1,0:T(8,128)(2,1)} %get-tuple-element.6.mixed_raw, f32[32,512]{1,0:T(8,128)} %get-tuple-element.7.ge_raw, f32[64,512]{1,0:T(8,128)} %get-tuple-element.8.gf_raw), custom_call_target="tpu_custom_call" | custom-call | tf_op jit(solution)/shard_map/collect/pallas_call | solution.py:602
